TPU v7x, 32 devices: a whole 2x2x4 slice. The times are simulated.
32 devices in a mesh: groups: 2 (over x), wide: 16 (over z, y, core).
Axes of the slice: x: 2, y: 2, z: 4, core: 2. Of those that a mesh axis runs over, the one named last changes fastest.
Arguments:
- attention_out: bfloat16 [256, 8192], P(('groups', 'wide')), parts along dimension 0, may hold values from -6 to 6
- o_weight: bfloat16 [8192, 8192], P('wide'), may hold values from -0.0625 to 0.0625
- a_down: bfloat16 [128, 64, 8192], P(('groups', 'wide')), parts along dimension 0, may hold values from -0.0625 to 0.0625
- b_up: bfloat16 [128, 64, 8192], P(('groups', 'wide')), parts along dimension 0, may hold values from -0.75 to 0.75
- adapter_home: int32 [128], P('groups'), parts along dimension 0, may hold values from 0 to 63, as said below
- req_adapter: int32 [128], P('groups'), parts along dimension 0, may hold values from 0 to 63, as said below
- req_tokens: int32 [32, 4], P('groups'), parts along dimension 0, may hold values from 1 to 4, 8 in all within a row
Outputs:
- projected: bfloat16 [256, 8192], P(('groups', 'wide')), parts along dimension 0
There are 2 independent parts, one for each index of `groups`. A program takes and returns all parts, laid end to end along the dimension named above; an argument that names none is the same for every part. Nothing has to cross between parts.
Inputs may be any that keep to these rules, and one draw needn't show every extreme that they name: `adapter_home`: a permutation; store position p lies on the device of index p // 4 along wide. `req_adapter`: request q is held by the device of index q // 4; the adapters named by all requests include, for every keeping device, between 1 and 2 distinct adapters of its store, and exactly 2 for some device. `req_tokens`: each row sums to 8.
All inputs are finite; a program needn't handle non-finite values.
Results may differ from a plain program's by a relative error of at most 0.004.
Values may be sent and summed in bfloat16 or wider, within the bound.
No kernel may reach another device: no remote copies, remote signals or barrier semaphores. Data moves between devices by JAX's collectives and lax.ppermute only.
A program may use at most 128 MiB of HBM per device.

v0:
```python
import jax
import jax.numpy as jnp
from jax import lax
from jax.sharding import PartitionSpec as P


def match_table(lookup, queries):
    table_size = lookup.shape[0]
    matches = queries[:, None] == jnp.arange(table_size, dtype=jnp.int32)[None, :]
    return jnp.sum(jnp.where(matches, lookup[None, :], 0), axis=1)


def token_requests(req_tokens, tok_rows):
    request_ends = jnp.cumsum(req_tokens, axis=1)
    places = jnp.arange(tok_rows, dtype=jnp.int32)
    within = jnp.sum((places[None, :, None] >= request_ends[:, None, :]).astype(jnp.int32), axis=2)
    owners = jnp.arange(req_tokens.shape[0], dtype=jnp.int32)[:, None]
    return (within + owners * req_tokens.shape[1]).reshape(-1)


def slice_inputs(features_here, a_fetched, token_slot):
    a_rows = jnp.take(a_fetched, token_slot, axis=0)
    return jnp.einsum("tc,trc->tr", features_here, a_rows, preferred_element_type=jnp.float32)


def low_rank(partial_inputs, b_fetched, token_slot):
    summed = lax.psum(partial_inputs, "wide")
    coefficients = summed.astype(jnp.bfloat16)
    b_rows = jnp.take(b_fetched, token_slot, axis=0)
    return jnp.einsum("tr,trc->tc", coefficients, b_rows, preferred_element_type=jnp.float32)


def shards(attention_out, o_weight, a_down, b_up, adapter_home, req_adapter, req_tokens):
    devices = lax.axis_size("wide")
    this_device = lax.axis_index("wide")
    tok_rows, model_width = attention_out.shape
    columns = model_width // devices
    req_position = match_table(adapter_home, req_adapter)
    token_position = match_table(req_position, token_requests(req_tokens, tok_rows))
    a_fetched, b_fetched = (
        lax.all_to_all(a_down, "wide", split_axis=2, concat_axis=0, tiled=True),
        lax.all_to_all(b_up, "wide", split_axis=2, concat_axis=0, tiled=True),
    )
    column_start = this_device * columns
    features_here = lax.all_to_all(attention_out, "wide", split_axis=1, concat_axis=0, tiled=True)
    delta = low_rank(
        slice_inputs(features_here, a_fetched, token_position), b_fetched, token_position
    )
    partial_value = jnp.dot(features_here, o_weight, preferred_element_type=jnp.float32)
    own_block = lax.dynamic_slice_in_dim(partial_value, column_start, columns, 1)
    summed_rows = lax.psum_scatter(
        lax.dynamic_update_slice_in_dim(partial_value, own_block + delta, column_start, 1),
        "wide",
        scatter_dimension=0,
        tiled=True,
    )
    return summed_rows.astype(jnp.bfloat16)


def solution(mesh):
    in_specs = (
        P(("groups", "wide"), None),
        P("wide", None),
        P(("groups", "wide"), None, None),
        P(("groups", "wide"), None, None),
        P("groups"),
        P("groups"),
        P("groups", None),
    )
    out_specs = P(("groups", "wide"), None)
    return jax.shard_map(shards, mesh=mesh, in_specs=in_specs, out_specs=out_specs, check_vma=False)
```

profile of v0, /device:TPU:0, one launch (start us, length us, event | category | flops | bytes accessed | tf_op | source)
XLA Modules:
  0.0 397.8 jit_solution(15870992804380581199)
XLA Ops:
  6.5 7.4 %all-to-all-start = ((bf16[8,16,512]{2,0,1:T(8,128)(2,1)}), bf16[8,16,512]{2,0,1:T(8,128)(2,1)S(1)}, u32[]{:S(2)}, u32[]{:S(2)}) async-start(bf16[8,16,512]{2,0,1:T(8,128)(2,1)} %bitcast.39), calls=%async_computation | async-start | bytes 262144 | tf_op jit(solution)/shard_map/all_to_all | solution.py:45
  13.9 12.7 %copy.21 = bf16[4,64,8192]{1,0,2:T(4,128)(2,1)} copy(bf16[4,64,8192]{2,1,0:T(8,128)(2,1)} %param.11) | data formatting | bytes 8388608 | tf_op args[2]
  26.6 14.0 %reshape.59 = bf16[16,2,65536]{2,1,0:T(2,128)(2,1)} reshape(bf16[8192,4,64]{2,1,0:T(4,128)(2,1)} %bitcast.36) | data formatting | bytes 8388608
  40.6 0.0 all-to-all-done
  40.6 6.1 %all-to-all-start.1 = ((bf16[16,2,65536]{2,1,0:T(2,128)(2,1)}), bf16[16,2,65536]{2,1,0:T(2,128)(2,1)}, u32[]{:S(2)}, u32[]{:S(2)}) async-start(bf16[16,2,65536]{2,1,0:T(2,128)(2,1)} %reshape.59), calls=%async_computation.1 | async-start | bytes 8388608 | tf_op jit(solution)/shard_map/all_to_all | solution.py:41
  46.6 12.7 %copy.24 = bf16[4,64,8192]{1,0,2:T(4,128)(2,1)} copy(bf16[4,64,8192]{2,1,0:T(8,128)(2,1)} %param.12) | data formatting | bytes 8388608 | tf_op args[3]
  59.3 14.0 %reshape.57 = bf16[16,2,65536]{2,1,0:T(2,128)(2,1)} reshape(bf16[8192,4,64]{2,1,0:T(4,128)(2,1)} %bitcast.37) | data formatting | bytes 8388608
  73.3 51.0 %all-to-all-done.1 = bf16[16,2,65536]{2,1,0:T(2,128)(2,1)} async-done(((bf16[16,2,65536]{2,1,0:T(2,128)(2,1)}), bf16[16,2,65536]{2,1,0:T(2,128)(2,1)}, u32[]{:S(2)}, u32[]{:S(2)}) %all-to-all-start.1) | async-done | bytes 4194336 | tf_op jit(solution)/shard_map/all_to_all | solution.py:41
  124.3 19.7 %all-to-all-start.2 = ((bf16[16,2,65536]{2,1,0:T(2,128)(2,1)}), bf16[16,2,65536]{2,1,0:T(2,128)(2,1)}, u32[]{:S(2)}, u32[]{:S(2)}) async-start(bf16[16,2,65536]{2,1,0:T(2,128)(2,1)} %reshape.57), calls=%async_computation.2 | async-start | bytes 8388608 | tf_op jit(solution)/shard_map/all_to_all | solution.py:42
  144.0 0.0 reduce-scatter.2.cloned.1.call-start
  144.1 0.0 copy-done
  144.1 0.1 copy.20
  144.2 0.1 add.35
  144.3 0.0 copy-done.1
  144.3 0.0 copy-done.2
  144.3 0.2 select_reduce_fusion.1
  144.5 0.1 select_reduce_fusion
  144.6 6.6 %fusion.10 = f32[128,8192]{1,0:T(8,128)} fusion(bf16[512,8192]{1,0:T(8,128)(2,1)} %param.10, bf16[8,16,512]{2,0,1:T(8,128)(2,1)S(1)} %all-to-all-done), kind=kOutput, calls=%fused_computation.13 | convolution fusion | flops 1073741824 | bytes 12713984 | tf_op jit(solution)/shard_map/dot_general | solution.py:49
  151.3 13.6 %reshape.60 = bf16[8192,4,64]{2,1,0:T(4,128)(2,1)} reshape(bf16[16,2,65536]{2,1,0:T(2,128)(2,1)} %all-to-all-done.1) | data formatting | bytes 8388608
  164.9 12.7 %copy.32 = bf16[4,64,16,512]{3,1,0,2:T(8,128)(2,1)} copy(bf16[4,64,16,512]{1,0,3,2:T(4,128)(2,1)} %bitcast.34) | data formatting | bytes 8388608 | tf_op jit(solution)/shard_map/all_to_all | solution.py:41
  177.6 8.7 %gather_fusion = bf16[128,64,512]{2,1,0:T(8,128)(2,1)} fusion(bf16[64,64,512]{2,1,0:T(8,128)(2,1)} %bitcast.33, s32[1024]{0:T(1024)S(1)} %pad_clamp_fusion), kind=kCustom, calls=%fused_computation.clone | custom fusion | bytes 16777728 | tf_op jit(solution)/shard_map/jit(_take)/gather | solution.py:22
  186.3 5.7 %fusion.2 = f32[128,1,64]{2,1,0:T(1,128)S(1)} fusion(bf16[128,64,512]{2,1,0:T(8,128)(2,1)} %gather_fusion, pred[128]{0:T(512)(128)(4,1)S(1)} %compare_and_fusion, bf16[128,512,1]{1,0,2:T(8,128)(2,1)S(1)} %bitcast.38), kind=kOutput, calls=%fused_computation.4 | convolution fusion | flops 12582912 | bytes 8552576 | tf_op jit(solution)/shard_map/tc,trc->tr/dot_general | solution.py:23
  192.1 83.5 %psum.7 = bf16[128,64]{1,0:T(8,128)(2,1)S(1)} all-reduce(f32[128,64]{1,0:T(8,128)S(1)} %bitcast.40), channel_id=1, replica_groups=mesh['groups'=2,'wide'=16] {'wide'}, use_global_device_ids=true, to_apply=%region_4.6 | all-reduce | flops 8192 | bytes 49152 | tf_op jit(solution)/shard_map/psum | solution.py:27
  275.5 0.0 all-to-all-done.2
  275.5 13.6 %reshape.58 = bf16[8192,4,64]{2,1,0:T(4,128)(2,1)} reshape(bf16[16,2,65536]{2,1,0:T(2,128)(2,1)} %all-to-all-done.2) | data formatting | bytes 8388608
  289.2 12.7 %copy.34 = bf16[4,64,16,512]{3,1,0,2:T(8,128)(2,1)} copy(bf16[4,64,16,512]{1,0,3,2:T(4,128)(2,1)} %bitcast.35) | data formatting | bytes 8388608 | tf_op jit(solution)/shard_map/all_to_all | solution.py:42
  301.9 8.7 %gather_fusion.1 = bf16[128,64,512]{2,1,0:T(8,128)(2,1)} fusion(bf16[64,64,512]{2,1,0:T(8,128)(2,1)} %bitcast.32, s32[1024]{0:T(1024)S(1)} %pad_clamp_fusion), kind=kCustom, calls=%fused_computation.1.clone | custom fusion | bytes 16777728 | tf_op jit(solution)/shard_map/jit(_take)/gather | solution.py:29
  310.6 4.8 %fusion = f32[128,1,512]{2,1,0:T(1,128)S(1)} fusion(bf16[128,64,512]{2,1,0:T(8,128)(2,1)} %gather_fusion.1, pred[128]{0:T(512)(128)(4,1)S(1)} %compare_and_fusion, bf16[128,64,1]{1,0,2:T(8,128)(2,1)S(1)} %bitcast.41), kind=kOutput, calls=%fused_computation.2 | convolution fusion | flops 12582912 | bytes 8667264 | tf_op jit(solution)/shard_map/tr,trc->tc/dot_general | solution.py:30
  315.4 1.7 fusion.8
  317.1 0.0 reduce-scatter.2.cloned.1.call-update
  317.1 72.2 %reduce-scatter.2.cloned.1.call-done = f32[8,8192]{1,0:T(8,128)} async-done(((f32[128,8192]{1,0:T(8,128)}), f32[8,8192]{1,0:T(8,128)}) %reduce-scatter.2.cloned.1.call-update) | async-done | bytes 262160 | tf_op jit(solution)/shard_map/reduce_scatter | solution.py:51
  389.3 1.6 convert_element_type.11
  (10 shorter events, 0.1 us)
Async XLA Ops:
  6.5 34.0 %all-to-all-start = ((bf16[8,16,512]{2,0,1:T(8,128)(2,1)}), bf16[8,16,512]{2,0,1:T(8,128)(2,1)S(1)}, u32[]{:S(2)}, u32[]{:S(2)}) async-start(bf16[8,16,512]{2,0,1:T(8,128)(2,1)} %bitcast.39), calls=%async_computation | async-start | bytes 262144 | tf_op jit(solution)/shard_map/all_to_all | solution.py:45
  40.6 83.7 %all-to-all-start.1 = ((bf16[16,2,65536]{2,1,0:T(2,128)(2,1)}), bf16[16,2,65536]{2,1,0:T(2,128)(2,1)}, u32[]{:S(2)}, u32[]{:S(2)}) async-start(bf16[16,2,65536]{2,1,0:T(2,128)(2,1)} %reshape.59), calls=%async_computation.1 | async-start | bytes 8388608 | tf_op jit(solution)/shard_map/all_to_all | solution.py:41
  59.3 84.8 %copy-start = (s32[16,4]{0,1:T(4,128)S(1)}, s32[16,4]{0,1:T(4,128)}, u32[]{:S(2)}) copy-start(s32[16,4]{0,1:T(4,128)} %param.15) | copy-start | bytes 772
  59.3 85.0 %copy-start.1 = (s32[64]{0:T(128)S(1)}, s32[64]{0:T(128)}, u32[]{:S(2)}) copy-start(s32[64]{0:T(128)} %param.13) | copy-start | bytes 772
  59.3 85.0 %copy-start.2 = (s32[64]{0:T(128)S(1)}, s32[64]{0:T(128)}, u32[]{:S(2)}) copy-start(s32[64]{0:T(128)} %param.14) | copy-start | bytes 772
  124.3 151.2 %all-to-all-start.2 = ((bf16[16,2,65536]{2,1,0:T(2,128)(2,1)}), bf16[16,2,65536]{2,1,0:T(2,128)(2,1)}, u32[]{:S(2)}, u32[]{:S(2)}) async-start(bf16[16,2,65536]{2,1,0:T(2,128)(2,1)} %reshape.57), calls=%async_computation.2 | async-start | bytes 8388608 | tf_op jit(solution)/shard_map/all_to_all | solution.py:42
  144.0 245.3 %reduce-scatter.2.cloned.1.call-start = ((), (), s32[]{:S(2)}) async-start(), calls=%async_computation.4 | async-start | bytes 4456448 | tf_op jit(solution)/shard_map/reduce_scatter | solution.py:51
Sparse Core Ops, SparseCore 0:
  317.3 71.9 reduce-scatter.1
where the time goes:
time: 401 us; the launch traced here: 398 us
  local copies, waits for them, and re-layouts  124 us (31%)
  waiting for transfers between devices  123 us (31%)
  blocking collectives  83.5 us (21%)
  starting transfers between devices  33.2 us (8%)
  matrix products  17.1 us (4%)
  between operations  13.5 us (3%)
    psum x1, blocking collectives, low_rank(): summed = lax.psum(partial_inputs, 'wide')  83.5 us
    unnamed x12, local copies, waits for them, and re-layouts  80.6 us
    reduce_scatter x1, waiting for transfers between devices, shards(): lax.psum_scatter(lax.dynamic_update_slice_in_dim(partial_value, own_block...  72.2 us
    all_to_all x1, waiting for transfers between devices, shards(): lax.all_to_all(a_down, 'wide', split_axis=2, concat_axis=0, tiled=True)  51 us
    all_to_all x1, starting transfers between devices, shards(): lax.all_to_all(b_up, 'wide', split_axis=2, concat_axis=0, tiled=True)  19.7 us
    all_to_all x1, local copies, waits for them, and re-layouts, shards(): lax.all_to_all(a_down, 'wide', split_axis=2, concat_axis=0, tiled=True)  12.7 us
    all_to_all x1, local copies, waits for them, and re-layouts, shards(): lax.all_to_all(b_up, 'wide', split_axis=2, concat_axis=0, tiled=True)  12.7 us
    gather x1, local copies, waits for them, and re-layouts, slice_inputs(): a_rows = jnp.take(a_fetched, token_slot, axis=0)  8.73 us
  transfers between devices with their start and end apart: 4, of which 2 were waited for; matrix products, arithmetic and copies ran while one was open for 25% of the time, Pallas kernels for 0%

commit v1 on v0

v1 whole, which is shorter than its diff:
```python
import functools

import jax
import jax.numpy as jnp
from jax import lax
from jax.experimental import pallas as pl
from jax.experimental.pallas import tpu as pltpu
from jax.sharding import Mesh, PartitionSpec as P

BF16 = jnp.bfloat16
F32 = jnp.float32
VMEM = pltpu.VMEM
SWAP = ((0, 1), (1, 0))


def other(x, axis):
    return lax.ppermute(x, axis, SWAP)


def along(x, shift):
    size = lax.axis_size("z")
    return lax.ppermute(x, "z", [(i, (i + shift) % size) for i in range(size)])


def match_table(lookup, queries):
    matches = queries[:, None] == jnp.arange(lookup.shape[0], dtype=jnp.int32)[None, :]
    return jnp.sum(jnp.where(matches, lookup[None, :], 0), axis=1)


def token_requests(req_tokens, tok_rows):
    request_ends = jnp.cumsum(req_tokens, axis=1)
    places = jnp.arange(tok_rows, dtype=jnp.int32)
    within = jnp.sum((places[None, :, None] >= request_ends[:, None, :]).astype(jnp.int32), axis=2)
    owners = jnp.arange(req_tokens.shape[0], dtype=jnp.int32)[:, None]
    return (within + owners * req_tokens.shape[1]).reshape(-1)


def partial_kernel(me_ref, slot_ref, x_ref, w_ref, a_ref, b_ref, keep_ref, send_ref, *, rank):
    rows, width = x_ref.shape
    depth = w_ref.shape[0]
    store = a_ref.shape[0]
    half = rows // 2
    inputs = lax.dot_general(x_ref[...], a_ref[...], (((1,), (1,)), ((), ())), preferred_element_type=F32)
    columns = lax.broadcasted_iota(jnp.int32, (rows, store), 1) // rank
    inputs = jnp.where(columns == slot_ref[...], inputs, 0.0).astype(BF16)
    start = pl.multiple_of(me_ref[0] * depth, depth)
    features = x_ref[:, pl.ds(start, depth)]
    step = 512

    def body(i, carry):
        at = pl.ds(pl.multiple_of(i * step, step), step)
        total = jnp.dot(features, w_ref[:, at], preferred_element_type=F32)
        total += jnp.dot(inputs, b_ref[:, at], preferred_element_type=F32)
        keep_ref[:, at] = total[:half]
        send_ref[:, at] = total[half:].astype(BF16)
        return carry

    lax.fori_loop(0, width // step, body, 0)


def partial_rows(me, slots, x, w, a, b, rank):
    rows, width = x.shape
    whole = pl.BlockSpec(memory_space=VMEM)
    held = [pltpu.with_memory_space_constraint(v, VMEM) for v in (w, a, b)]
    return pl.pallas_call(
        functools.partial(partial_kernel, rank=rank),
        out_shape=(VMEM((rows // 2, width), F32), VMEM((rows // 2, width), BF16)),
        in_specs=[pl.BlockSpec(memory_space=pltpu.SMEM)] + [whole] * 5,
        out_specs=(whole, whole),
        compiler_params=pltpu.CompilerParams(vmem_limit_bytes=8 << 20),
        name="partial_rows",
    )(me, slots, x, *held)


def shards(attention_out, o_weight, a_down, b_up, adapter_home, req_adapter, req_tokens):
    tok_rows, width = attention_out.shape
    store, rank, _ = a_down.shape
    planes = lax.axis_size("z")
    z, y, core = lax.axis_index("z"), lax.axis_index("y"), lax.axis_index("core")
    me = (z * 2 + y) * 2 + core

    zs = [attention_out] + [along(attention_out, s) for s in range(1, planes)]
    ys = [other(v, "y") for v in zs]
    mine = jnp.concatenate(zs + ys, 0)
    gathered = jnp.concatenate([mine, other(mine, "core")], 0)

    req_position = match_table(adapter_home, req_adapter)
    token_position = match_table(req_position, token_requests(req_tokens, tok_rows))
    slots = (token_position - me * store).reshape(planes, 2, 2, tok_rows)
    slots = jnp.where(core == 1, slots[:, :, ::-1], slots)
    slots = jnp.where(y == 1, slots[:, ::-1], slots)
    slots = lax.dynamic_slice_in_dim(jnp.concatenate([slots[::-1]] * 2, 0), planes - 1 - z, planes, 0)
    slots = jnp.transpose(slots, (2, 1, 0, 3)).reshape(-1, 1)

    keep, send = partial_rows(
        me.reshape(1).astype(jnp.int32), slots, gathered, o_weight,
        a_down.reshape(-1, width), b_up.reshape(-1, width), rank,
    )
    keep = keep.reshape(2, planes, tok_rows, width)
    got = other(send, "core").reshape(2, planes, tok_rows, width)
    summed = keep + got.astype(F32)
    out = summed[0, 0] + other(summed[1, 0].astype(BF16), "y").astype(F32)
    for s in range(1, planes):
        part = summed[0, s] + other(summed[1, s].astype(BF16), "y").astype(F32)
        out = out + along(part.astype(BF16), -s).astype(F32)
    return out.astype(BF16)


def solution(mesh):
    groups, wide = mesh.shape["groups"], mesh.shape["wide"]
    wide_axes = ("z", "y", "core")
    grid = Mesh(mesh.devices.reshape(groups, wide // 4, 2, 2), ("groups",) + wide_axes)
    every = ("groups",) + wide_axes
    in_specs = (
        P(every, None),
        P(wide_axes, None),
        P(every, None, None),
        P(every, None, None),
        P("groups"),
        P("groups"),
        P("groups", None),
    )
    return jax.shard_map(shards, mesh=grid, in_specs=in_specs, out_specs=P(every, None), check_vma=False)
```

time: 401 us -> 70.4 us (0.18)
  local copies, waits for them, and re-layouts: 124 us -> 14.5 us
  waiting for transfers between devices: 123 us -> 27.3 us
  blocking collectives: 83.5 us -> 0 us
  matrix products: 17.1 us -> 0 us
  between operations: 13.5 us -> 0.17 us
  starting transfers between devices: 33.2 us -> 20 us
  Pallas kernels: 0 us -> 5.97 us
    psum x1 -> x0, blocking collectives: 83.5 us -> none  [low_rank(): summed = lax.psum(partial_inputs, 'wide')]
    reduce_scatter x1 -> x0, waiting for transfers between devices: 72.2 us -> none  [shards(): lax.psum_scatter(lax.dynamic_update_slice_in_dim(partial_value, own_block...]
    unnamed x12 -> x17, local copies, waits for them, and re-layouts: 80.6 us -> 13.4 us
    all_to_all x3 -> x0, waiting for transfers between devices: 51 us -> none  [the longest x1 51 us: shards(): lax.all_to_all(a_down, 'wide', split_axis=2, concat_axis=0, tiled=True)]
    all_to_all x3 -> x0, starting transfers between devices: 33.1 us -> none  [the longest x1 19.7 us: shards(): lax.all_to_all(b_up, 'wide', split_axis=2, concat_axis=0, tiled=True)]
    ppermute x0 -> x16, waiting for transfers between devices: none -> 27.3 us  [the longest x10 14.6 us: other(): return lax.ppermute(x, axis, SWAP)]
    all_to_all x2 -> x0, local copies, waits for them, and re-layouts: 25.4 us -> none  [the longest x1 12.7 us: shards(): lax.all_to_all(a_down, 'wide', split_axis=2, concat_axis=0, tiled=True)]
    ppermute x0 -> x16, starting transfers between devices: none -> 20 us  [the longest x6 11.5 us: along(): return lax.ppermute(x, 'z', [(i, (i + shift) % size) for i in range(size)])]
  transfers between devices with their start and end apart: 4 -> 16, of which waited for: 2 -> 10; matrix products, arithmetic and copies ran while one was open for 25% -> 10% of each run, Pallas kernels for 0% -> 0%
where the time goes in v1:
time: 70.4 us; the launch traced here: 70.2 us
  waiting for transfers between devices  27.3 us (39%)
  starting transfers between devices  20 us (28%)
  local copies, waits for them, and re-layouts  14.5 us (21%)
  Pallas kernels  5.97 us (8%)
  other arithmetic  2.14 us (3%)
    ppermute x10, waiting for transfers between devices, other(): return lax.ppermute(x, axis, SWAP)  14.6 us
    unnamed x17, local copies, waits for them, and re-layouts  13.4 us
    ppermute x6, waiting for transfers between devices, along(): return lax.ppermute(x, 'z', [(i, (i + shift) % size) for i in range(size)])  12.8 us
    ppermute x6, starting transfers between devices, along(): return lax.ppermute(x, 'z', [(i, (i + shift) % size) for i in range(size)])  11.5 us
    ppermute x10, starting transfers between devices, other(): return lax.ppermute(x, axis, SWAP)  8.5 us
    pallas_call x1, Pallas kernels, partial_rows(): pl.pallas_call(functools.partial(partial_kernel, rank=rank), out_shape=(V...  5.97 us
  transfers between devices with their start and end apart: 16, of which 10 were waited for; matrix products, arithmetic and copies ran while one was open for 10% of the time, Pallas kernels for 0%

profile of v1, /device:TPU:0, one launch (start us, length us, event | category | flops | bytes accessed | tf_op | source)
XLA Modules:
  0.0 70.2 jit_solution(13784929031562622667)
XLA Ops:
  0.0 3.0 %collective-permute-start = (bf16[8,8192]{1,0:T(8,128)(2,1)}, bf16[8,8192]{1,0:T(8,128)(2,1)S(1)}, u32[]{:S(2)}, u32[]{:S(2)}) collective-permute-start(bf16[8,8192]{1,0:T(8,128)(2,1)} %param.7), channel_id=1, source_target_pairs={{0,4},{4,8},{8,12},{12,0},{1,5},{5,9},{9,13},{13,1},{2,6},{6,10},{... | collective-permute-start | bytes 393224 | tf_op jit(solution)/shard_map/ppermute | solution.py:22
  3.0 2.6 %collective-permute-start.1 = (bf16[8,8192]{1,0:T(8,128)(2,1)}, bf16[8,8192]{1,0:T(8,128)(2,1)S(1)}, u32[]{:S(2)}, u32[]{:S(2)}) collective-permute-start(bf16[8,8192]{1,0:T(8,128)(2,1)} %param.7), channel_id=1, source_target_pairs={{0,8},{4,12},{8,0},{12,4},{1,9},{5,13},{9,1},{13,5},{2,10},{6,14},... | collective-permute-start | bytes 393224 | tf_op jit(solution)/shard_map/ppermute | solution.py:22
  5.6 1.3 %collective-permute-start.2 = (bf16[8,8192]{1,0:T(8,128)(2,1)}, bf16[8,8192]{1,0:T(8,128)(2,1)S(1)}, u32[]{:S(2)}, u32[]{:S(2)}) collective-permute-start(bf16[8,8192]{1,0:T(8,128)(2,1)} %param.7), channel_id=1, source_target_pairs={{0,12},{4,0},{8,4},{12,8},{1,13},{5,1},{9,5},{13,9},{2,14},{6,2},{... | collective-permute-start | bytes 393224 | tf_op jit(solution)/shard_map/ppermute | solution.py:22
  7.0 1.5 %collective-permute-start.3 = (bf16[8,8192]{1,0:T(8,128)(2,1)}, bf16[8,8192]{1,0:T(8,128)(2,1)S(1)}, u32[]{:S(2)}, u32[]{:S(2)}) collective-permute-start(bf16[8,8192]{1,0:T(8,128)(2,1)} %param.7), channel_id=1, source_target_pairs={{0,2},{2,0},{1,3},{3,1},{4,6},{6,4},{5,7},{7,5},{8,10},{10,8},{9,1... | collective-permute-start | bytes 393224 | tf_op jit(solution)/shard_map/ppermute | solution.py:17
  8.5 1.6 %constant_dynamic-update-slice_fusion.7 = (bf16[64,8192]{1,0:T(8,128)(2,1)}, bf16[128,8192]{1,0:T(8,128)(2,1)S(1)}) fusion(bf16[8,8192]{1,0:T(8,128)(2,1)} %param.7), kind=kLoop, calls=%fused_computation.27 | loop fusion | bytes 393216
  10.1 0.7 %reduce_window_sum.11 = s32[16,4]{0,1:T(4,128)S(1)} reduce-window(s32[16,4]{0,1:T(4,128)} %param.13, s32[]{:T(128)} %constant.24.clone.1), window={size=1x4 pad=0_0x3_0}, to_apply=%region_0.1 | reduce-window | flops 192 | bytes 516 | tf_op jit(solution)/shard_map/jit(cumsum)/reduce_window_sum | solution.py:31
  11.5 3.0 %collective-permute-done.1 = bf16[8,8192]{1,0:T(8,128)(2,1)S(1)} collective-permute-done((bf16[8,8192]{1,0:T(8,128)(2,1)}, bf16[8,8192]{1,0:T(8,128)(2,1)S(1)}, u32[]{:S(2)}, u32[]{:S(2)}) %collective-permute-start.1) | collective-permute-done | bytes 131104 | tf_op jit(solution)/shard_map/ppermute | solution.py:22
  14.5 1.5 %collective-permute-start.5 = (bf16[8,8192]{1,0:T(8,128)(2,1)S(1)}, bf16[8,8192]{1,0:T(8,128)(2,1)S(1)}, u32[]{:S(2)}, u32[]{:S(2)}) collective-permute-start(bf16[8,8192]{1,0:T(8,128)(2,1)S(1)} %collective-permute-done.1), channel_id=1, source_target_pairs={{0,2},{2,0},{1,3},{3,1},{4,6},{6,4},{5,7},{7,5},{8,10},{10,8},{9,1... | collective-permute-start | bytes 393224 | tf_op jit(solution)/shard_map/ppermute | solution.py:17
  16.5 0.7 constant_dynamic-update-slice_fusion.6
  17.2 0.7 constant_dynamic-update-slice_fusion.5
  17.8 0.7 constant_dynamic-update-slice_fusion.4
  18.5 0.7 constant_dynamic-update-slice_fusion.3
  19.2 0.7 constant_dynamic-update-slice_fusion.2
  19.9 1.0 %collective-permute-done.5 = bf16[8,8192]{1,0:T(8,128)(2,1)S(1)} collective-permute-done((bf16[8,8192]{1,0:T(8,128)(2,1)S(1)}, bf16[8,8192]{1,0:T(8,128)(2,1)S(1)}, u32[]{:S(2)}, u32[]{:S(2)}) %collective-permute-start.5) | collective-permute-done | bytes 131104 | tf_op jit(solution)/shard_map/ppermute | solution.py:17
  20.8 0.7 constant_dynamic-update-slice_fusion.1
  21.5 1.1 %collective-permute-done.6 = bf16[8,8192]{1,0:T(8,128)(2,1)S(1)} collective-permute-done((bf16[8,8192]{1,0:T(8,128)(2,1)S(1)}, bf16[8,8192]{1,0:T(8,128)(2,1)S(1)}, u32[]{:S(2)}, u32[]{:S(2)}) %collective-permute-start.6) | collective-permute-done | bytes 131104 | tf_op jit(solution)/shard_map/ppermute | solution.py:17
  24.1 2.1 %collective-permute-done.7 = bf16[64,8192]{1,0:T(8,128)(2,1)S(1)} collective-permute-done((bf16[64,8192]{1,0:T(8,128)(2,1)}, bf16[64,8192]{1,0:T(8,128)(2,1)S(1)}, u32[]{:S(2)}, u32[]{:S(2)}) %collective-permute-start.7) | collective-permute-done | bytes 1048608 | tf_op jit(solution)/shard_map/ppermute | solution.py:17
  26.2 3.4 %copy-done = bf16[512,8192]{1,0:T(8,128)(2,1)S(1)} copy-done((bf16[512,8192]{1,0:T(8,128)(2,1)S(1)}, bf16[512,8192]{1,0:T(8,128)(2,1)}, u32[]{:S(2)}) %copy-start) | copy-done | bytes 8388632
  29.6 2.2 %copy-done.1 = bf16[4,64,8192]{2,1,0:T(8,128)(2,1)S(1)} copy-done((bf16[4,64,8192]{2,1,0:T(8,128)(2,1)S(1)}, bf16[4,64,8192]{2,1,0:T(8,128)(2,1)}, u32[]{:S(2)}) %copy-start.1) | copy-done | bytes 4194328
  31.8 2.2 %copy-done.2 = bf16[4,64,8192]{2,1,0:T(8,128)(2,1)S(1)} copy-done((bf16[4,64,8192]{2,1,0:T(8,128)(2,1)S(1)}, bf16[4,64,8192]{2,1,0:T(8,128)(2,1)}, u32[]{:S(2)}) %copy-start.2) | copy-done | bytes 4194328
  34.0 6.0 %partial_rows.1 = (f32[64,8192]{1,0:T(8,128)S(1)}, bf16[64,8192]{1,0:T(8,128)(2,1)S(1)}) custom-call(s32[1]{0:T(128)} %bitcast.me_ref, s32[128,1]{1,0:T(8,128)S(1)} %reshape.49.slot_ref, bf16[128,8192]{1,0:T(8,128)(2,1)S(1)} %constant_dynamic-update-slice_fusion.8.x_ref, bf16[512,8192]{1,0:T(8,128)(2,1)S(1)} %copy-done, bf16[256,8192]{1,0:T(8,128)(2,1)S(1)} %bitcast.44, ...), custom_call_target="tpu_custom_call" | custom-call | tf_op jit(solution)/shard_map/partial_rows/pallas_call | solution.py:65
  40.2 2.5 %collective-permute-done.8 = bf16[64,8192]{1,0:T(8,128)(2,1)S(1)} collective-permute-done((bf16[64,8192]{1,0:T(8,128)(2,1)S(1)}, bf16[64,8192]{1,0:T(8,128)(2,1)S(1)}, u32[]{:S(2)}, u32[]{:S(2)}) %collective-permute-start.8) | collective-permute-done | bytes 1048608 | tf_op jit(solution)/shard_map/ppermute | solution.py:17
  43.0 1.6 %collective-permute-start.10 = (bf16[8,8192]{1,0:T(8,128)(2,1)S(1)}, bf16[8,8192]{1,0:T(8,128)(2,1)S(1)}, u32[]{:S(2)}, u32[]{:S(2)}) collective-permute-start(bf16[8,8192]{1,0:T(8,128)(2,1)S(1)} %get-tuple-element.15), channel_id=1, source_target_pairs={{0,2},{2,0},{1,3},{3,1},{4,6},{6,4},{5,7},{7,5},{8,10},{10,8},{9,1... | collective-permute-start | bytes 393224 | tf_op jit(solution)/shard_map/ppermute | solution.py:17
  45.1 1.5 %collective-permute-start.14 = (bf16[8,8192]{1,0:T(8,128)(2,1)S(1)}, bf16[8,8192]{1,0:T(8,128)(2,1)S(1)}, u32[]{:S(2)}, u32[]{:S(2)}) collective-permute-start(bf16[8,8192]{1,0:T(8,128)(2,1)S(1)} %get-tuple-element.13), channel_id=1, source_target_pairs={{0,2},{2,0},{1,3},{3,1},{4,6},{6,4},{5,7},{7,5},{8,10},{10,8},{9,1... | collective-permute-start | bytes 393224 | tf_op jit(solution)/shard_map/ppermute | solution.py:17
  47.1 2.3 %collective-permute-done.10 = bf16[8,8192]{1,0:T(8,128)(2,1)S(1)} collective-permute-done((bf16[8,8192]{1,0:T(8,128)(2,1)S(1)}, bf16[8,8192]{1,0:T(8,128)(2,1)S(1)}, u32[]{:S(2)}, u32[]{:S(2)}) %collective-permute-start.10) | collective-permute-done | bytes 131104 | tf_op jit(solution)/shard_map/ppermute | solution.py:17
  49.4 2.8 %collective-permute-done.12 = bf16[8,8192]{1,0:T(8,128)(2,1)S(1)} collective-permute-done((bf16[8,8192]{1,0:T(8,128)(2,1)S(1)}, bf16[8,8192]{1,0:T(8,128)(2,1)S(1)}, u32[]{:S(2)}, u32[]{:S(2)}) %collective-permute-start.12) | collective-permute-done | bytes 131104 | tf_op jit(solution)/shard_map/ppermute | solution.py:17
  52.2 2.8 %collective-permute-done.14 = bf16[8,8192]{1,0:T(8,128)(2,1)S(1)} collective-permute-done((bf16[8,8192]{1,0:T(8,128)(2,1)S(1)}, bf16[8,8192]{1,0:T(8,128)(2,1)S(1)}, u32[]{:S(2)}, u32[]{:S(2)}) %collective-permute-start.14) | collective-permute-done | bytes 131104 | tf_op jit(solution)/shard_map/ppermute | solution.py:17
  55.1 3.4 %collective-permute-start.11 = (bf16[8,8192]{1,0:T(8,128)(2,1)S(1)}, bf16[8,8192]{1,0:T(8,128)(2,1)S(1)}, u32[]{:S(2)}, u32[]{:S(2)}) collective-permute-start(bf16[8,8192]{1,0:T(8,128)(2,1)S(1)} %get-tuple-element.9), channel_id=1, source_target_pairs={{0,12},{4,0},{8,4},{12,8},{1,13},{5,1},{9,5},{13,9},{2,14},{6,2},{... | collective-permute-start | bytes 393224 | tf_op jit(solution)/shard_map/ppermute | solution.py:22
  58.7 0.9 %collective-permute-start.15 = (bf16[8,8192]{1,0:T(8,128)(2,1)S(1)}, bf16[8,8192]{1,0:T(8,128)(2,1)S(1)}, u32[]{:S(2)}, u32[]{:S(2)}) collective-permute-start(bf16[8,8192]{1,0:T(8,128)(2,1)S(1)} %get-tuple-element.10), channel_id=1, source_target_pairs={{0,4},{4,8},{8,12},{12,0},{1,5},{5,9},{9,13},{13,1},{2,6},{6,10},{... | collective-permute-start | bytes 393224 | tf_op jit(solution)/shard_map/ppermute | solution.py:22
  59.7 2.9 %collective-permute-done.11 = bf16[8,8192]{1,0:T(8,128)(2,1)S(1)} collective-permute-done((bf16[8,8192]{1,0:T(8,128)(2,1)S(1)}, bf16[8,8192]{1,0:T(8,128)(2,1)S(1)}, u32[]{:S(2)}, u32[]{:S(2)}) %collective-permute-start.11) | collective-permute-done | bytes 131104 | tf_op jit(solution)/shard_map/ppermute | solution.py:22
  62.5 6.9 %collective-permute-done.13 = bf16[8,8192]{1,0:T(8,128)(2,1)S(1)} collective-permute-done((bf16[8,8192]{1,0:T(8,128)(2,1)S(1)}, bf16[8,8192]{1,0:T(8,128)(2,1)S(1)}, u32[]{:S(2)}, u32[]{:S(2)}) %collective-permute-start.13) | collective-permute-done | bytes 131104 | tf_op jit(solution)/shard_map/ppermute | solution.py:22
  69.4 0.7 %fusion.10 = bf16[8,8192]{1,0:T(8,128)(2,1)} fusion(f32[2,4,8,8192]{3,2,1,0:T(8,128)S(1)} %bitcast.48, bf16[8,8192]{1,0:T(8,128)(2,1)S(1)} %collective-permute-done.15, bf16[8,8192]{1,0:T(8,128)(2,1)S(1)} %collective-permute-done.13, bf16[8,8192]{1,0:T(8,128)(2,1)S(1)} %collective-permute-done.11, bf16[8,8192]{1,0:T(8,128)(2,1)S(1)} %collective-permute-done.9), kind=kLoop, calls=%fused_computation.15 | loop fusion | flops 589824 | bytes 917504 | tf_op jit(solution)/shard_map/convert_element_type | solution.py:106
  (41 shorter events, 4.3 us)
Async XLA Ops:
  0.0 23.4 %copy-start.3 = (s32[64]{0:T(128)S(1)}, s32[64]{0:T(128)}, u32[]{:S(2)}) copy-start(s32[64]{0:T(128)} %param.11) | copy-start | bytes 772
  0.0 23.5 %copy-start.4 = (s32[64]{0:T(128)S(1)}, s32[64]{0:T(128)}, u32[]{:S(2)}) copy-start(s32[64]{0:T(128)} %param.12) | copy-start | bytes 772
  0.0 10.8 %collective-permute-start = (bf16[8,8192]{1,0:T(8,128)(2,1)}, bf16[8,8192]{1,0:T(8,128)(2,1)S(1)}, u32[]{:S(2)}, u32[]{:S(2)}) collective-permute-start(bf16[8,8192]{1,0:T(8,128)(2,1)} %param.7), channel_id=1, source_target_pairs={{0,4},{4,8},{8,12},{12,0},{1,5},{5,9},{9,13},{13,1},{2,6},{6,10},{... | collective-permute-start | bytes 393224 | tf_op jit(solution)/shard_map/ppermute | solution.py:22
  3.0 11.4 %collective-permute-start.1 = (bf16[8,8192]{1,0:T(8,128)(2,1)}, bf16[8,8192]{1,0:T(8,128)(2,1)S(1)}, u32[]{:S(2)}, u32[]{:S(2)}) collective-permute-start(bf16[8,8192]{1,0:T(8,128)(2,1)} %param.7), channel_id=1, source_target_pairs={{0,8},{4,12},{8,0},{12,4},{1,9},{5,13},{9,1},{13,5},{2,10},{6,14},... | collective-permute-start | bytes 393224 | tf_op jit(solution)/shard_map/ppermute | solution.py:22
  5.6 10.4 %collective-permute-start.2 = (bf16[8,8192]{1,0:T(8,128)(2,1)}, bf16[8,8192]{1,0:T(8,128)(2,1)S(1)}, u32[]{:S(2)}, u32[]{:S(2)}) collective-permute-start(bf16[8,8192]{1,0:T(8,128)(2,1)} %param.7), channel_id=1, source_target_pairs={{0,12},{4,0},{8,4},{12,8},{1,13},{5,1},{9,5},{13,9},{2,14},{6,2},{... | collective-permute-start | bytes 393224 | tf_op jit(solution)/shard_map/ppermute | solution.py:22
  7.0 11.6 %collective-permute-start.3 = (bf16[8,8192]{1,0:T(8,128)(2,1)}, bf16[8,8192]{1,0:T(8,128)(2,1)S(1)}, u32[]{:S(2)}, u32[]{:S(2)}) collective-permute-start(bf16[8,8192]{1,0:T(8,128)(2,1)} %param.7), channel_id=1, source_target_pairs={{0,2},{2,0},{1,3},{3,1},{4,6},{6,4},{5,7},{7,5},{8,10},{10,8},{9,1... | collective-permute-start | bytes 393224 | tf_op jit(solution)/shard_map/ppermute | solution.py:17
  10.8 8.4 %collective-permute-start.4 = (bf16[8,8192]{1,0:T(8,128)(2,1)S(1)}, bf16[8,8192]{1,0:T(8,128)(2,1)S(1)}, u32[]{:S(2)}, u32[]{:S(2)}) collective-permute-start(bf16[8,8192]{1,0:T(8,128)(2,1)S(1)} %collective-permute-done), channel_id=1, source_target_pairs={{0,2},{2,0},{1,3},{3,1},{4,6},{6,4},{5,7},{7,5},{8,10},{10,8},{9,1... | collective-permute-start | bytes 393224 | tf_op jit(solution)/shard_map/ppermute | solution.py:17
  14.5 6.4 %collective-permute-start.5 = (bf16[8,8192]{1,0:T(8,128)(2,1)S(1)}, bf16[8,8192]{1,0:T(8,128)(2,1)S(1)}, u32[]{:S(2)}, u32[]{:S(2)}) collective-permute-start(bf16[8,8192]{1,0:T(8,128)(2,1)S(1)} %collective-permute-done.1), channel_id=1, source_target_pairs={{0,2},{2,0},{1,3},{3,1},{4,6},{6,4},{5,7},{7,5},{8,10},{10,8},{9,1... | collective-permute-start | bytes 393224 | tf_op jit(solution)/shard_map/ppermute | solution.py:17
  16.0 6.6 %collective-permute-start.6 = (bf16[8,8192]{1,0:T(8,128)(2,1)S(1)}, bf16[8,8192]{1,0:T(8,128)(2,1)S(1)}, u32[]{:S(2)}, u32[]{:S(2)}) collective-permute-start(bf16[8,8192]{1,0:T(8,128)(2,1)S(1)} %collective-permute-done.2), channel_id=1, source_target_pairs={{0,2},{2,0},{1,3},{3,1},{4,6},{6,4},{5,7},{7,5},{8,10},{10,8},{9,1... | collective-permute-start | bytes 393224 | tf_op jit(solution)/shard_map/ppermute | solution.py:17
  23.3 2.9 %collective-permute-start.7 = (bf16[64,8192]{1,0:T(8,128)(2,1)}, bf16[64,8192]{1,0:T(8,128)(2,1)S(1)}, u32[]{:S(2)}, u32[]{:S(2)}) collective-permute-start(bf16[64,8192]{1,0:T(8,128)(2,1)} %get-tuple-element.16), channel_id=1, source_target_pairs={{0,1},{1,0},{2,3},{3,2},{4,5},{5,4},{6,7},{7,6},{8,9},{9,8},{10,11... | collective-permute-start | bytes 3145736 | tf_op jit(solution)/shard_map/ppermute | solution.py:17
  26.2 3.4 %copy-start = (bf16[512,8192]{1,0:T(8,128)(2,1)S(1)}, bf16[512,8192]{1,0:T(8,128)(2,1)}, u32[]{:S(2)}) copy-start(bf16[512,8192]{1,0:T(8,128)(2,1)} %w_ref.1) | copy-start | bytes 25165828
  29.6 2.2 %copy-start.1 = (bf16[4,64,8192]{2,1,0:T(8,128)(2,1)S(1)}, bf16[4,64,8192]{2,1,0:T(8,128)(2,1)}, u32[]{:S(2)}) copy-start(bf16[4,64,8192]{2,1,0:T(8,128)(2,1)} %param.9) | copy-start | bytes 12582916
  31.8 2.2 %copy-start.2 = (bf16[4,64,8192]{2,1,0:T(8,128)(2,1)S(1)}, bf16[4,64,8192]{2,1,0:T(8,128)(2,1)}, u32[]{:S(2)}) copy-start(bf16[4,64,8192]{2,1,0:T(8,128)(2,1)} %param.10) | copy-start | bytes 12582916
  40.0 2.7 %collective-permute-start.8 = (bf16[64,8192]{1,0:T(8,128)(2,1)S(1)}, bf16[64,8192]{1,0:T(8,128)(2,1)S(1)}, u32[]{:S(2)}, u32[]{:S(2)}) collective-permute-start(bf16[64,8192]{1,0:T(8,128)(2,1)S(1)} %get-tuple-element.8), channel_id=1, source_target_pairs={{0,1},{1,0},{2,3},{3,2},{4,5},{5,4},{6,7},{7,6},{8,9},{9,8},{10,11... | collective-permute-start | bytes 3145736 | tf_op jit(solution)/shard_map/ppermute | solution.py:17
  43.0 6.4 %collective-permute-start.10 = (bf16[8,8192]{1,0:T(8,128)(2,1)S(1)}, bf16[8,8192]{1,0:T(8,128)(2,1)S(1)}, u32[]{:S(2)}, u32[]{:S(2)}) collective-permute-start(bf16[8,8192]{1,0:T(8,128)(2,1)S(1)} %get-tuple-element.15), channel_id=1, source_target_pairs={{0,2},{2,0},{1,3},{3,1},{4,6},{6,4},{5,7},{7,5},{8,10},{10,8},{9,1... | collective-permute-start | bytes 393224 | tf_op jit(solution)/shard_map/ppermute | solution.py:17
  44.6 7.6 %collective-permute-start.12 = (bf16[8,8192]{1,0:T(8,128)(2,1)S(1)}, bf16[8,8192]{1,0:T(8,128)(2,1)S(1)}, u32[]{:S(2)}, u32[]{:S(2)}) collective-permute-start(bf16[8,8192]{1,0:T(8,128)(2,1)S(1)} %get-tuple-element.14), channel_id=1, source_target_pairs={{0,2},{2,0},{1,3},{3,1},{4,6},{6,4},{5,7},{7,5},{8,10},{10,8},{9,1... | collective-permute-start | bytes 393224 | tf_op jit(solution)/shard_map/ppermute | solution.py:17
  45.1 9.9 %collective-permute-start.14 = (bf16[8,8192]{1,0:T(8,128)(2,1)S(1)}, bf16[8,8192]{1,0:T(8,128)(2,1)S(1)}, u32[]{:S(2)}, u32[]{:S(2)}) collective-permute-start(bf16[8,8192]{1,0:T(8,128)(2,1)S(1)} %get-tuple-element.13), channel_id=1, source_target_pairs={{0,2},{2,0},{1,3},{3,1},{4,6},{6,4},{5,7},{7,5},{8,10},{10,8},{9,1... | collective-permute-start | bytes 393224 | tf_op jit(solution)/shard_map/ppermute | solution.py:17
  46.7 13.0 %collective-permute-start.9 = (bf16[8,8192]{1,0:T(8,128)(2,1)S(1)}, bf16[8,8192]{1,0:T(8,128)(2,1)S(1)}, u32[]{:S(2)}, u32[]{:S(2)}) collective-permute-start(bf16[8,8192]{1,0:T(8,128)(2,1)S(1)} %get-tuple-element.12), channel_id=1, source_target_pairs={{0,2},{2,0},{1,3},{3,1},{4,6},{6,4},{5,7},{7,5},{8,10},{10,8},{9,1... | collective-permute-start | bytes 393224 | tf_op jit(solution)/shard_map/ppermute | solution.py:17
  55.1 7.4 %collective-permute-start.11 = (bf16[8,8192]{1,0:T(8,128)(2,1)S(1)}, bf16[8,8192]{1,0:T(8,128)(2,1)S(1)}, u32[]{:S(2)}, u32[]{:S(2)}) collective-permute-start(bf16[8,8192]{1,0:T(8,128)(2,1)S(1)} %get-tuple-element.9), channel_id=1, source_target_pairs={{0,12},{4,0},{8,4},{12,8},{1,13},{5,1},{9,5},{13,9},{2,14},{6,2},{... | collective-permute-start | bytes 393224 | tf_op jit(solution)/shard_map/ppermute | solution.py:22
  58.6 10.8 %collective-permute-start.13 = (bf16[8,8192]{1,0:T(8,128)(2,1)S(1)}, bf16[8,8192]{1,0:T(8,128)(2,1)S(1)}, u32[]{:S(2)}, u32[]{:S(2)}) collective-permute-start(bf16[8,8192]{1,0:T(8,128)(2,1)S(1)} %get-tuple-element.11), channel_id=1, source_target_pairs={{0,8},{4,12},{8,0},{12,4},{1,9},{5,13},{9,1},{13,5},{2,10},{6,14},... | collective-permute-start | bytes 393224 | tf_op jit(solution)/shard_map/ppermute | solution.py:22
  58.7 10.7 %collective-permute-start.15 = (bf16[8,8192]{1,0:T(8,128)(2,1)S(1)}, bf16[8,8192]{1,0:T(8,128)(2,1)S(1)}, u32[]{:S(2)}, u32[]{:S(2)}) collective-permute-start(bf16[8,8192]{1,0:T(8,128)(2,1)S(1)} %get-tuple-element.10), channel_id=1, source_target_pairs={{0,4},{4,8},{8,12},{12,0},{1,5},{5,9},{9,13},{13,1},{2,6},{6,10},{... | collective-permute-start | bytes 393224 | tf_op jit(solution)/shard_map/ppermute | solution.py:22

commit v2 on v1

v2 whole, which is shorter than its diff:
```python
import functools

import jax
import jax.numpy as jnp
from jax import lax
from jax.experimental import pallas as pl
from jax.experimental.pallas import tpu as pltpu
from jax.sharding import Mesh, PartitionSpec as P

BF16 = jnp.bfloat16
F32 = jnp.float32
VMEM = pltpu.VMEM
SWAP = ((0, 1), (1, 0))
NAMED = 2
WEIGHT_COPIES = 4
WHOLE = pl.BlockSpec(memory_space=VMEM)
SCALAR = pl.BlockSpec(memory_space=pltpu.SMEM)
FAR = pl.BlockSpec(memory_space=pltpu.HBM)
PARAMS = pltpu.CompilerParams(vmem_limit_bytes=12 << 20)


def other(x, axis):
    return lax.ppermute(x, axis, SWAP)


def across(x, away):
    return lax.ppermute(x, "z", [(i, i ^ away) for i in range(lax.axis_size("z"))])


def after(x, *others):
    return lax.optimization_barrier((x, *others))[0]


def prepare_kernel(
    home_hbm, adapter_hbm, tokens_hbm, w_hbm, a_hbm, b_hbm, which_ref, w_ref, a_ref, b_ref,
    home_ref, adapter_ref, tokens_ref, table_sems, weight_sems, sems, *, tok_rows,
):
    store, rank, _ = a_hbm.shape
    requests, devices = tokens_hbm.shape
    z, y, core = lax.axis_index("z"), lax.axis_index("y"), lax.axis_index("core")
    first_position = ((z * 2 + y) * 2 + core) * store
    tables = []
    for i, (src, dst) in enumerate(((home_hbm, home_ref), (adapter_hbm, adapter_ref), (tokens_hbm, tokens_ref))):
        tables.append(pltpu.make_async_copy(src, dst, table_sems.at[i]))
    weights = []
    share = w_hbm.shape[0] // WEIGHT_COPIES
    for i in range(WEIGHT_COPIES):
        rows = pl.ds(i * share, share)
        weights.append(pltpu.make_async_copy(w_hbm.at[rows], w_ref.at[rows], weight_sems.at[i]))
    for copy in tables + weights:
        copy.start()
    for copy in tables:
        copy.wait()

    def slot_of(owner, i):
        return home_ref[adapter_ref[owner * requests + i]] - first_position

    def extremes(owner, carry):
        first, last = carry
        for i in range(requests):
            slot = slot_of(owner, i)
            here = (slot >= 0) & (slot < store)
            first = jnp.where(here, jnp.minimum(first, slot), first)
            last = jnp.where(here, jnp.maximum(last, slot), last)
        return first, last

    first, last = lax.fori_loop(0, devices, extremes, (jnp.int32(store - 1), jnp.int32(0)))
    copies = []
    for i, slot in enumerate((first, last)):
        rows = pl.ds(i * rank, rank)
        copies.append(pltpu.make_async_copy(a_hbm.at[slot], a_ref.at[rows], sems.at[2 * i]))
        copies.append(pltpu.make_async_copy(b_hbm.at[slot], b_ref.at[rows], sems.at[2 * i + 1]))
    for copy in copies:
        copy.start()

    def rows_of(owner, carry):
        block = (((owner // 4) ^ z) * 2 + ((owner % 2) ^ core)) * 2 + (((owner // 2) % 2) ^ y)
        places = lax.broadcasted_iota(jnp.int32, (tok_rows, 1), 0)
        wanted = jnp.full((tok_rows, 1), -1, jnp.int32)
        begin = jnp.int32(0)
        for i in range(requests):
            slot = slot_of(owner, i)
            one = jnp.where(slot == first, 0, jnp.where(slot == last, 1, -1))
            wanted = jnp.where(places >= begin, one, wanted)
            begin = begin + tokens_ref[i, owner]
        which_ref[pl.ds(pl.multiple_of(block * tok_rows, tok_rows), tok_rows), :] = wanted
        return carry

    lax.fori_loop(0, devices, rows_of, 0)
    for copy in copies + weights:
        copy.wait()


def prepare(home, adapter, tokens, w, a, b, tok_rows):
    _, rank, width = a.shape
    rows = tokens.shape[0] * tok_rows
    sources = (home, adapter, tokens.T, w, a, b)
    return pl.pallas_call(
        functools.partial(prepare_kernel, tok_rows=tok_rows),
        out_shape=(
            VMEM((rows, 1), jnp.int32),
            VMEM(w.shape, BF16),
            VMEM((NAMED * rank, width), BF16),
            VMEM((NAMED * rank, width), BF16),
        ),
        in_specs=[FAR] * len(sources),
        out_specs=(WHOLE,) * 4,
        scratch_shapes=[pltpu.SMEM(v.shape, jnp.int32) for v in sources[:3]]
        + [pltpu.SemaphoreType.DMA((n,)) for n in (3, WEIGHT_COPIES, 2 * NAMED)],
        compiler_params=PARAMS,
        cost_estimate=pl.CostEstimate(flops=0, bytes_accessed=12 << 20, transcendentals=0),
        name="prepare",
    )(*[pltpu.with_memory_space_constraint(v, pltpu.HBM) for v in sources])


def partial_kernel(which_ref, w_ref, a_ref, b_ref, *refs, parts, rank):
    xs, outs, x_ref = refs[: 4 * len(parts)], refs[4 * len(parts) : -1], refs[-1]
    tok_rows, width = xs[0].shape
    depth = w_ref.shape[0]
    step = 2048
    me = (lax.axis_index("z") * 2 + lax.axis_index("y")) * 2 + lax.axis_index("core")

    inputs = None
    for k in range(0, width, step):
        at = pl.ds(k, step)
        rows = jnp.concatenate([x[:, at].astype(F32) for x in xs], 0).astype(BF16)
        x_ref[:, at] = rows
        part = lax.dot_general(rows, a_ref[:, at], (((1,), (1,)), ((), ())), preferred_element_type=F32)
        inputs = part if inputs is None else inputs + part
    block = 4 * tok_rows
    which = jnp.concatenate([which_ref[pl.ds(s * block, block), :] for s in parts], 0)
    columns = lax.broadcasted_iota(jnp.int32, inputs.shape, 1) // rank
    inputs = jnp.where(columns == which, inputs, 0.0).astype(BF16)
    features = x_ref[:, pl.ds(pl.multiple_of(me * depth, depth), depth)]

    def body(i, carry):
        at = pl.ds(pl.multiple_of(i * step, step), step)
        total = jnp.dot(features, w_ref[:, at], preferred_element_type=F32)
        total += jnp.dot(inputs, b_ref[:, at], preferred_element_type=F32)
        half = block // 2
        for j in range(len(parts)):
            outs[2 * j][:, at] = total[j * block : j * block + half]
            outs[2 * j + 1][:, at] = total[j * block + half : (j + 1) * block].astype(BF16)
        return carry

    lax.fori_loop(0, width // step, body, 0)


def partial_rows(which, w, a, b, xs, parts, rank):
    rows, width = xs[0].shape
    held = [pltpu.with_memory_space_constraint(v, VMEM) for v in (which, w, a, b, *xs)]
    total = 4 * rows * len(parts)
    return pl.pallas_call(
        functools.partial(partial_kernel, parts=parts, rank=rank),
        out_shape=(VMEM((2 * rows, width), F32), VMEM((2 * rows, width), BF16)) * len(parts),
        in_specs=[WHOLE] * len(held),
        out_specs=(WHOLE,) * (2 * len(parts)),
        scratch_shapes=[VMEM((total, width), BF16)],
        compiler_params=PARAMS,
        cost_estimate=pl.CostEstimate(
            flops=2 * total * width * (w.shape[0] + 2 * a.shape[0]), bytes_accessed=16 << 20, transcendentals=0
        ),
        name="partial_rows",
    )(*held)


def shards(attention_out, o_weight, a_down, b_up, adapter_home, req_adapter, req_tokens):
    tok_rows, width = attention_out.shape
    rank = a_down.shape[1]
    planes = lax.axis_size("z")
    which, w, a, b = prepare(adapter_home, req_adapter, req_tokens, o_weight, a_down, b_up, tok_rows)

    far = {0: attention_out, 1: across(attention_out, 1)}
    for e in range(2, planes, 2):
        far[e] = after(across(attention_out, e), which)
        far[e + 1] = across(far[e], 1)
    near = {e: other(far[e], "y") for e in range(planes)}

    parts = tuple(range(planes))[::-1]
    xs = []
    for e in parts:
        xs += [far[e], near[e], other(far[e], "core"), other(near[e], "core")]
    sums = partial_rows(which, w, a, b, xs, parts, rank)
    out = None
    arriving = []
    before = ()
    for j, e in enumerate(parts):
        keep, got = sums[2 * j], other(sums[2 * j + 1], "core")
        here = keep[:tok_rows] + got[:tok_rows].astype(F32)
        there = (keep[tok_rows:] + got[tok_rows:].astype(F32)).astype(BF16)
        if e == 0:
            there = after(there, *before)
        received = other(there, "y")
        if e > 1:
            before = (received,)
        part = here + received.astype(F32)
        if e == 0:
            out = part
        else:
            arriving.append(across(part.astype(BF16), e))
    for part in arriving:
        out = out + part.astype(F32)
    return out.astype(BF16)


def solution(mesh):
    groups, wide = mesh.shape["groups"], mesh.shape["wide"]
    wide_axes = ("z", "y", "core")
    grid = Mesh(mesh.devices.reshape(groups, wide // 4, 2, 2), ("groups",) + wide_axes)
    every = ("groups",) + wide_axes
    in_specs = (
        P(every, None),
        P(wide_axes, None),
        P(every, None, None),
        P(every, None, None),
        P("groups"),
        P("groups"),
        P("groups", None),
    )
    return jax.shard_map(shards, mesh=grid, in_specs=in_specs, out_specs=P(every, None), check_vma=False)
```

time: 70.4 us -> 50.7 us (0.72)
  local copies, waits for them, and re-layouts: 14.5 us -> 0.01 us
  waiting for transfers between devices: 27.3 us -> 20.1 us
  Pallas kernels: 5.97 us -> 7.92 us
  starting transfers between devices: 20 us -> 21.4 us
  other arithmetic: 2.14 us -> 1.01 us
    unnamed x17 -> x2, local copies, waits for them, and re-layouts: 13.4 us -> 0.01 us
    ppermute x6, waiting for transfers between devices: 12.8 us -> 8.28 us  [across(): lax.ppermute(x, 'z', [(i, i ^ away) for i in range(lax.axis_size('z'))])]
    ppermute x10 -> x20, waiting for transfers between devices: 14.6 us -> 11.8 us  [other(): return lax.ppermute(x, axis, SWAP)]
    pallas_call x1 -> x2, Pallas kernels: 5.97 us -> 7.92 us  [the longest x1 4.95 us: prepare(): pl.pallas_call(functools.partial(prepare_kernel, tok_rows=tok_rows), out_...]
    ppermute x10 -> x20, starting transfers between devices: 8.5 us -> 9.41 us  [other(): return lax.ppermute(x, axis, SWAP)]
    another operation x2 -> x0, other arithmetic: 0.82 us -> none  [the longest x1 0.71 us: token_requests(): request_ends = jnp.cumsum(req_tokens, axis=1)]
    concatenate x2 -> x0, local copies, waits for them, and re-layouts: 0.73 us -> none  [the longest x1 0.66 us: shards(): mine = jnp.concatenate(zs + ys, 0)]
  transfers between devices with their start and end apart: 16 -> 26, of which waited for: 10 -> 12; matrix products, arithmetic and copies ran while one was open for 10% -> 1% of each run, Pallas kernels for 0% -> 10%
where the time goes in v2:
time: 50.7 us; the launch traced here: 50.5 us
  starting transfers between devices  21.4 us (42%)
  waiting for transfers between devices  20.1 us (40%)
  Pallas kernels  7.92 us (16%)
  other arithmetic  1.01 us (2%)
    ppermute x6, starting transfers between devices, across(): lax.ppermute(x, 'z', [(i, i ^ away) for i in range(lax.axis_size('z'))])  12 us
    ppermute x20, waiting for transfers between devices, other(): return lax.ppermute(x, axis, SWAP)  11.8 us
    ppermute x20, starting transfers between devices, other(): return lax.ppermute(x, axis, SWAP)  9.41 us
    ppermute x6, waiting for transfers between devices, across(): lax.ppermute(x, 'z', [(i, i ^ away) for i in range(lax.axis_size('z'))])  8.28 us
    pallas_call x1, Pallas kernels, prepare(): pl.pallas_call(functools.partial(prepare_kernel, tok_rows=tok_rows), out_...  4.95 us
    pallas_call x1, Pallas kernels, partial_rows(): pl.pallas_call(functools.partial(partial_kernel, parts=parts, rank=rank),...  2.97 us
  transfers between devices with their start and end apart: 26, of which 12 were waited for; matrix products, arithmetic and copies ran while one was open for 1% of the time, Pallas kernels for 10%

profile of v2, /device:TPU:0, one launch (start us, length us, event | category | flops | bytes accessed | tf_op | source)
XLA Modules:
  0.0 50.5 jit_solution(13923477543834365015)
XLA Ops:
  0.0 4.0 %collective-permute-start = (bf16[8,8192]{1,0:T(8,128)(2,1)}, bf16[8,8192]{1,0:T(8,128)(2,1)S(1)}, u32[]{:S(2)}, u32[]{:S(2)}) collective-permute-start(bf16[8,8192]{1,0:T(8,128)(2,1)} %refs_12_.1), channel_id=1, source_target_pairs={{0,8},{4,12},{8,0},{12,4},{1,9},{5,13},{9,1},{13,5},{2,10},{6,14},... | collective-permute-start | bytes 393224 | tf_op jit(solution)/shard_map/ppermute | solution.py:27
  4.0 1.5 %collective-permute-start.12 = (bf16[8,8192]{1,0:T(8,128)(2,1)}, bf16[8,8192]{1,0:T(8,128)(2,1)S(1)}, u32[]{:S(2)}, u32[]{:S(2)}) collective-permute-start(bf16[8,8192]{1,0:T(8,128)(2,1)} %refs_12_.1), channel_id=1, source_target_pairs={{0,2},{2,0},{1,3},{3,1},{4,6},{6,4},{5,7},{7,5},{8,10},{10,8},{9,1... | collective-permute-start | bytes 393224 | tf_op jit(solution)/shard_map/ppermute | solution.py:23
  5.6 1.6 %collective-permute-start.8 = (bf16[8,8192]{1,0:T(8,128)(2,1)}, bf16[8,8192]{1,0:T(8,128)(2,1)S(1)}, u32[]{:S(2)}, u32[]{:S(2)}) collective-permute-start(bf16[8,8192]{1,0:T(8,128)(2,1)} %refs_12_.1), channel_id=1, source_target_pairs={{0,4},{4,0},{8,12},{12,8},{1,5},{5,1},{9,13},{13,9},{2,6},{6,2},{1... | collective-permute-start | bytes 393224 | tf_op jit(solution)/shard_map/ppermute | solution.py:27
  7.1 5.0 %prepare.1 = (s32[128,1]{1,0:T(8,128)S(1)}, bf16[512,8192]{1,0:T(8,128)(2,1)S(1)}, bf16[128,8192]{1,0:T(8,128)(2,1)S(1)}, bf16[128,8192]{1,0:T(8,128)(2,1)S(1)}) custom-call(s32[64]{0:T(128)} %home_hbm.1, s32[64]{0:T(128)} %adapter_hbm.1, s32[4,16]{1,0:T(4,128)} %bitcast.1, bf16[512,8192]{1,0:T(8,128)(2,1)} %w_hbm.1, bf16[4,64,8192]{2,1,0:T(8,128)(2,1)} %a_hbm.1, ...), custom_call_target="tpu_custom_call" | custom-call | bytes 12582912 | tf_op jit(solution)/shard_map/prepare/pallas_call | solution.py:98
  12.1 0.5 %collective-permute-start.1 = (bf16[8,8192]{1,0:T(8,128)(2,1)S(1)}, bf16[8,8192]{1,0:T(8,128)(2,1)S(1)}, u32[]{:S(2)}, u32[]{:S(2)}) collective-permute-start(bf16[8,8192]{1,0:T(8,128)(2,1)S(1)} %collective-permute-done.refs_4_), channel_id=1, source_target_pairs={{0,4},{4,0},{8,12},{12,8},{1,5},{5,1},{9,13},{13,9},{2,6},{6,2},{1... | collective-permute-start | bytes 393224 | tf_op jit(solution)/shard_map/ppermute | solution.py:27
  12.9 0.3 collective-permute-start.10
  13.1 0.5 %collective-permute-start.9 = (bf16[8,8192]{1,0:T(8,128)(2,1)S(1)}, bf16[8,8192]{1,0:T(8,128)(2,1)S(1)}, u32[]{:S(2)}, u32[]{:S(2)}) collective-permute-start(bf16[8,8192]{1,0:T(8,128)(2,1)S(1)} %collective-permute-done.8.refs_8_), channel_id=1, source_target_pairs={{0,2},{2,0},{1,3},{3,1},{4,6},{6,4},{5,7},{7,5},{8,10},{10,8},{9,1... | collective-permute-start | bytes 393224 | tf_op jit(solution)/shard_map/ppermute | solution.py:23
  13.7 1.5 %collective-permute-start.5 = (bf16[8,8192]{1,0:T(8,128)(2,1)S(1)}, bf16[8,8192]{1,0:T(8,128)(2,1)S(1)}, u32[]{:S(2)}, u32[]{:S(2)}) collective-permute-start(bf16[8,8192]{1,0:T(8,128)(2,1)S(1)} %collective-permute-done.refs_4_), channel_id=1, source_target_pairs={{0,2},{2,0},{1,3},{3,1},{4,6},{6,4},{5,7},{7,5},{8,10},{10,8},{9,1... | collective-permute-start | bytes 393224 | tf_op jit(solution)/shard_map/ppermute | solution.py:23
  15.2 2.9 %collective-permute-done.1.refs_0_ = bf16[8,8192]{1,0:T(8,128)(2,1)S(1)} collective-permute-done((bf16[8,8192]{1,0:T(8,128)(2,1)S(1)}, bf16[8,8192]{1,0:T(8,128)(2,1)S(1)}, u32[]{:S(2)}, u32[]{:S(2)}) %collective-permute-start.1) | collective-permute-done | bytes 131104 | tf_op jit(solution)/shard_map/ppermute | solution.py:27
  18.1 0.5 %collective-permute-start.2 = (bf16[8,8192]{1,0:T(8,128)(2,1)S(1)}, bf16[8,8192]{1,0:T(8,128)(2,1)S(1)}, u32[]{:S(2)}, u32[]{:S(2)}) collective-permute-start(bf16[8,8192]{1,0:T(8,128)(2,1)S(1)} %collective-permute-done.1.refs_0_), channel_id=1, source_target_pairs={{0,2},{2,0},{1,3},{3,1},{4,6},{6,4},{5,7},{7,5},{8,10},{10,8},{9,1... | collective-permute-start | bytes 393224 | tf_op jit(solution)/shard_map/ppermute | solution.py:23
  18.6 0.5 %collective-permute-start.3 = (bf16[8,8192]{1,0:T(8,128)(2,1)S(1)}, bf16[8,8192]{1,0:T(8,128)(2,1)S(1)}, u32[]{:S(2)}, u32[]{:S(2)}) collective-permute-start(bf16[8,8192]{1,0:T(8,128)(2,1)S(1)} %collective-permute-done.1.refs_0_), channel_id=1, source_target_pairs={{0,1},{1,0},{2,3},{3,2},{4,5},{5,4},{6,7},{7,6},{8,9},{9,8},{10,11... | collective-permute-start | bytes 393224 | tf_op jit(solution)/shard_map/ppermute | solution.py:23
  19.1 0.4 collective-permute-done.9.refs_9_
  19.5 2.8 %collective-permute-done.5.refs_5_ = bf16[8,8192]{1,0:T(8,128)(2,1)S(1)} collective-permute-done((bf16[8,8192]{1,0:T(8,128)(2,1)S(1)}, bf16[8,8192]{1,0:T(8,128)(2,1)S(1)}, u32[]{:S(2)}, u32[]{:S(2)}) %collective-permute-start.5) | collective-permute-done | bytes 131104 | tf_op jit(solution)/shard_map/ppermute | solution.py:23
  22.3 2.1 %collective-permute-done.2.refs_1_ = bf16[8,8192]{1,0:T(8,128)(2,1)S(1)} collective-permute-done((bf16[8,8192]{1,0:T(8,128)(2,1)S(1)}, bf16[8,8192]{1,0:T(8,128)(2,1)S(1)}, u32[]{:S(2)}, u32[]{:S(2)}) %collective-permute-start.2) | collective-permute-done | bytes 131104 | tf_op jit(solution)/shard_map/ppermute | solution.py:23
  24.4 1.3 %collective-permute-done.4.refs_3_ = bf16[8,8192]{1,0:T(8,128)(2,1)S(1)} collective-permute-done((bf16[8,8192]{1,0:T(8,128)(2,1)S(1)}, bf16[8,8192]{1,0:T(8,128)(2,1)S(1)}, u32[]{:S(2)}, u32[]{:S(2)}) %collective-permute-start.4) | collective-permute-done | bytes 131104 | tf_op jit(solution)/shard_map/ppermute | solution.py:23
  25.7 3.0 %partial_rows.1 = (f32[16,8192]{1,0:T(8,128)S(1)}, bf16[16,8192]{1,0:T(8,128)(2,1)S(1)}, f32[16,8192]{1,0:T(8,128)S(1)}, bf16[16,8192]{1,0:T(8,128)(2,1)S(1)}, f...) custom-call(s32[128,1]{1,0:T(8,128)S(1)} %get-tuple-element.19.which, ...), custom_call_target="tpu_custom_call" | custom-call | flops 1610612736 | bytes 16777216 | tf_op jit(solution)/shard_map/partial_rows/pallas_call | solution.py:153
  28.9 0.4 collective-permute-start.15
  29.5 0.4 collective-permute-start.23
  29.8 0.5 %collective-permute-done.16 = bf16[16,8192]{1,0:T(8,128)(2,1)S(1)} collective-permute-done((bf16[16,8192]{1,0:T(8,128)(2,1)S(1)}, bf16[16,8192]{1,0:T(8,128)(2,1)S(1)}, u32[]{:S(2)}, u32[]{:S(2)}) %collective-permute-start.16) | collective-permute-done | bytes 262176 | tf_op jit(solution)/shard_map/ppermute | solution.py:23
  30.4 0.6 %collective-permute-start.17 = (bf16[8,8192]{1,0:T(8,128)(2,1)S(1)}, bf16[8,8192]{1,0:T(8,128)(2,1)S(1)}, u32[]{:S(2)}, u32[]{:S(2)}) collective-permute-start(bf16[8,8192]{1,0:T(8,128)(2,1)S(1)} %add_convert_fusion.6), channel_id=1, source_target_pairs={{0,2},{2,0},{1,3},{3,1},{4,6},{6,4},{5,7},{7,5},{8,10},{10,8},{9,1... | collective-permute-start | bytes 393224 | tf_op jit(solution)/shard_map/ppermute | solution.py:23
  31.1 1.4 %collective-permute-start.20 = (bf16[8,8192]{1,0:T(8,128)(2,1)S(1)}, bf16[8,8192]{1,0:T(8,128)(2,1)S(1)}, u32[]{:S(2)}, u32[]{:S(2)}) collective-permute-start(bf16[8,8192]{1,0:T(8,128)(2,1)S(1)} %add_convert_fusion.5), channel_id=1, source_target_pairs={{0,2},{2,0},{1,3},{3,1},{4,6},{6,4},{5,7},{7,5},{8,10},{10,8},{9,1... | collective-permute-start | bytes 393224 | tf_op jit(solution)/shard_map/ppermute | solution.py:23
  32.6 0.7 %collective-permute-start.24 = (bf16[8,8192]{1,0:T(8,128)(2,1)S(1)}, bf16[8,8192]{1,0:T(8,128)(2,1)S(1)}, u32[]{:S(2)}, u32[]{:S(2)}) collective-permute-start(bf16[8,8192]{1,0:T(8,128)(2,1)S(1)} %add_convert_fusion.2), channel_id=1, source_target_pairs={{0,2},{2,0},{1,3},{3,1},{4,6},{6,4},{5,7},{7,5},{8,10},{10,8},{9,1... | collective-permute-start | bytes 393224 | tf_op jit(solution)/shard_map/ppermute | solution.py:23
  33.3 3.4 %collective-permute-done.17 = bf16[8,8192]{1,0:T(8,128)(2,1)S(1)} collective-permute-done((bf16[8,8192]{1,0:T(8,128)(2,1)S(1)}, bf16[8,8192]{1,0:T(8,128)(2,1)S(1)}, u32[]{:S(2)}, u32[]{:S(2)}) %collective-permute-start.17) | collective-permute-done | bytes 131104 | tf_op jit(solution)/shard_map/ppermute | solution.py:23
  36.8 0.5 %collective-permute-start.18 = (bf16[8,8192]{1,0:T(8,128)(2,1)S(1)}, bf16[8,8192]{1,0:T(8,128)(2,1)S(1)}, u32[]{:S(2)}, u32[]{:S(2)}) collective-permute-start(bf16[8,8192]{1,0:T(8,128)(2,1)S(1)} %add_convert_fusion.7), channel_id=1, source_target_pairs={{0,2},{2,0},{1,3},{3,1},{4,6},{6,4},{5,7},{7,5},{8,10},{10,8},{9,1... | collective-permute-start | bytes 393224 | tf_op jit(solution)/shard_map/ppermute | solution.py:23
  37.3 2.9 %collective-permute-start.22 = (bf16[8,8192]{1,0:T(8,128)(2,1)S(1)}, bf16[8,8192]{1,0:T(8,128)(2,1)S(1)}, u32[]{:S(2)}, u32[]{:S(2)}) collective-permute-start(bf16[8,8192]{1,0:T(8,128)(2,1)S(1)} %add_convert_fusion.3), channel_id=1, source_target_pairs={{0,8},{4,12},{8,0},{12,4},{1,9},{5,13},{9,1},{13,5},{2,10},{6,14},... | collective-permute-start | bytes 393224 | tf_op jit(solution)/shard_map/ppermute | solution.py:27
  40.3 1.3 %collective-permute-start.21 = (bf16[8,8192]{1,0:T(8,128)(2,1)S(1)}, bf16[8,8192]{1,0:T(8,128)(2,1)S(1)}, u32[]{:S(2)}, u32[]{:S(2)}) collective-permute-start(bf16[8,8192]{1,0:T(8,128)(2,1)S(1)} %add_convert_fusion.4), channel_id=1, source_target_pairs={{0,12},{4,8},{8,4},{12,0},{1,13},{5,9},{9,5},{13,1},{2,14},{6,10},... | collective-permute-start | bytes 393224 | tf_op jit(solution)/shard_map/ppermute | solution.py:27
  41.6 0.7 %collective-permute-done.24 = bf16[8,8192]{1,0:T(8,128)(2,1)S(1)} collective-permute-done((bf16[8,8192]{1,0:T(8,128)(2,1)S(1)}, bf16[8,8192]{1,0:T(8,128)(2,1)S(1)}, u32[]{:S(2)}, u32[]{:S(2)}) %collective-permute-start.24) | collective-permute-done | bytes 131104 | tf_op jit(solution)/shard_map/ppermute | solution.py:23
  42.4 1.6 %collective-permute-start.25 = (bf16[8,8192]{1,0:T(8,128)(2,1)S(1)}, bf16[8,8192]{1,0:T(8,128)(2,1)S(1)}, u32[]{:S(2)}, u32[]{:S(2)}) collective-permute-start(bf16[8,8192]{1,0:T(8,128)(2,1)S(1)} %add_convert_fusion.1), channel_id=1, source_target_pairs={{0,4},{4,0},{8,12},{12,8},{1,5},{5,1},{9,13},{13,9},{2,6},{6,2},{1... | collective-permute-start | bytes 393224 | tf_op jit(solution)/shard_map/ppermute | solution.py:27
  44.1 0.3 collective-permute-done.18
  44.4 4.5 %collective-permute-done.22 = bf16[8,8192]{1,0:T(8,128)(2,1)S(1)} collective-permute-done((bf16[8,8192]{1,0:T(8,128)(2,1)S(1)}, bf16[8,8192]{1,0:T(8,128)(2,1)S(1)}, u32[]{:S(2)}, u32[]{:S(2)}) %collective-permute-start.22) | collective-permute-done | bytes 131104 | tf_op jit(solution)/shard_map/ppermute | solution.py:27
  48.9 0.8 %collective-permute-done.25 = bf16[8,8192]{1,0:T(8,128)(2,1)S(1)} collective-permute-done((bf16[8,8192]{1,0:T(8,128)(2,1)S(1)}, bf16[8,8192]{1,0:T(8,128)(2,1)S(1)}, u32[]{:S(2)}, u32[]{:S(2)}) %collective-permute-start.25) | collective-permute-done | bytes 131104 | tf_op jit(solution)/shard_map/ppermute | solution.py:27
  49.8 0.7 %add_convert_fusion = bf16[8,8192]{1,0:T(8,128)(2,1)} fusion(bf16[8,8192]{1,0:T(8,128)(2,1)S(1)} %collective-permute-done.25, bf16[8,8192]{1,0:T(8,128)(2,1)S(1)} %collective-permute-done.22, bf16[8,8192]{1,0:T(8,128)(2,1)S(1)} %collective-permute-done.21, bf16[8,8192]{1,0:T(8,128)(2,1)S(1)} %collective-permute-done.18, f32[16,8192]{1,0:T(8,128)S(1)} %get-tuple-element.24, ...), kind=kLoop, calls=%fused_computation | loop fusion | flops 720896 | bytes 1048576 | tf_op jit(solution)/shard_map/convert_element_type | solution.py:203
  (32 shorter events, 1.1 us)
Async XLA Ops:
  0.0 12.1 %collective-permute-start = (bf16[8,8192]{1,0:T(8,128)(2,1)}, bf16[8,8192]{1,0:T(8,128)(2,1)S(1)}, u32[]{:S(2)}, u32[]{:S(2)}) collective-permute-start(bf16[8,8192]{1,0:T(8,128)(2,1)} %refs_12_.1), channel_id=1, source_target_pairs={{0,8},{4,12},{8,0},{12,4},{1,9},{5,13},{9,1},{13,5},{2,10},{6,14},... | collective-permute-start | bytes 393224 | tf_op jit(solution)/shard_map/ppermute | solution.py:27
  4.0 8.6 %collective-permute-start.12 = (bf16[8,8192]{1,0:T(8,128)(2,1)}, bf16[8,8192]{1,0:T(8,128)(2,1)S(1)}, u32[]{:S(2)}, u32[]{:S(2)}) collective-permute-start(bf16[8,8192]{1,0:T(8,128)(2,1)} %refs_12_.1), channel_id=1, source_target_pairs={{0,2},{2,0},{1,3},{3,1},{4,6},{6,4},{5,7},{7,5},{8,10},{10,8},{9,1... | collective-permute-start | bytes 393224 | tf_op jit(solution)/shard_map/ppermute | solution.py:23
  5.6 7.3 %collective-permute-start.8 = (bf16[8,8192]{1,0:T(8,128)(2,1)}, bf16[8,8192]{1,0:T(8,128)(2,1)S(1)}, u32[]{:S(2)}, u32[]{:S(2)}) collective-permute-start(bf16[8,8192]{1,0:T(8,128)(2,1)} %refs_12_.1), channel_id=1, source_target_pairs={{0,4},{4,0},{8,12},{12,8},{1,5},{5,1},{9,13},{13,9},{2,6},{6,2},{1... | collective-permute-start | bytes 393224 | tf_op jit(solution)/shard_map/ppermute | solution.py:27
  7.1 6.5 %collective-permute-start.13 = (bf16[8,8192]{1,0:T(8,128)(2,1)}, bf16[8,8192]{1,0:T(8,128)(2,1)S(1)}, u32[]{:S(2)}, u32[]{:S(2)}) collective-permute-start(bf16[8,8192]{1,0:T(8,128)(2,1)} %refs_12_.1), channel_id=1, source_target_pairs={{0,1},{1,0},{2,3},{3,2},{4,5},{5,4},{6,7},{7,6},{8,9},{9,8},{10,11... | collective-permute-start | bytes 393224 | tf_op jit(solution)/shard_map/ppermute | solution.py:23
  7.1 18.6 %copy-start = (bf16[8,8192]{1,0:T(8,128)(2,1)S(1)}, bf16[8,8192]{1,0:T(8,128)(2,1)}, u32[]{:S(2)}) copy-start(bf16[8,8192]{1,0:T(8,128)(2,1)} %refs_12_.1) | copy-start | bytes 393220
  12.1 6.0 %collective-permute-start.1 = (bf16[8,8192]{1,0:T(8,128)(2,1)S(1)}, bf16[8,8192]{1,0:T(8,128)(2,1)S(1)}, u32[]{:S(2)}, u32[]{:S(2)}) collective-permute-start(bf16[8,8192]{1,0:T(8,128)(2,1)S(1)} %collective-permute-done.refs_4_), channel_id=1, source_target_pairs={{0,4},{4,0},{8,12},{12,8},{1,5},{5,1},{9,13},{13,9},{2,6},{6,2},{1... | collective-permute-start | bytes 393224 | tf_op jit(solution)/shard_map/ppermute | solution.py:27
  12.6 6.0 %collective-permute-start.14 = (bf16[8,8192]{1,0:T(8,128)(2,1)S(1)}, bf16[8,8192]{1,0:T(8,128)(2,1)S(1)}, u32[]{:S(2)}, u32[]{:S(2)}) collective-permute-start(bf16[8,8192]{1,0:T(8,128)(2,1)S(1)} %collective-permute-done.12.refs_13_), channel_id=1, source_target_pairs={{0,1},{1,0},{2,3},{3,2},{4,5},{5,4},{6,7},{7,6},{8,9},{9,8},{10,11... | collective-permute-start | bytes 393224 | tf_op jit(solution)/shard_map/ppermute | solution.py:23
  12.9 5.7 %collective-permute-start.10 = (bf16[8,8192]{1,0:T(8,128)(2,1)S(1)}, bf16[8,8192]{1,0:T(8,128)(2,1)S(1)}, u32[]{:S(2)}, u32[]{:S(2)}) collective-permute-start(bf16[8,8192]{1,0:T(8,128)(2,1)S(1)} %collective-permute-done.8.refs_8_), channel_id=1, source_target_pairs={{0,1},{1,0},{2,3},{3,2},{4,5},{5,4},{6,7},{7,6},{8,9},{9,8},{10,11... | collective-permute-start | bytes 393224 | tf_op jit(solution)/shard_map/ppermute | solution.py:23
  13.1 6.3 %collective-permute-start.9 = (bf16[8,8192]{1,0:T(8,128)(2,1)S(1)}, bf16[8,8192]{1,0:T(8,128)(2,1)S(1)}, u32[]{:S(2)}, u32[]{:S(2)}) collective-permute-start(bf16[8,8192]{1,0:T(8,128)(2,1)S(1)} %collective-permute-done.8.refs_8_), channel_id=1, source_target_pairs={{0,2},{2,0},{1,3},{3,1},{4,6},{6,4},{5,7},{7,5},{8,10},{10,8},{9,1... | collective-permute-start | bytes 393224 | tf_op jit(solution)/shard_map/ppermute | solution.py:23
  13.7 8.6 %collective-permute-start.5 = (bf16[8,8192]{1,0:T(8,128)(2,1)S(1)}, bf16[8,8192]{1,0:T(8,128)(2,1)S(1)}, u32[]{:S(2)}, u32[]{:S(2)}) collective-permute-start(bf16[8,8192]{1,0:T(8,128)(2,1)S(1)} %collective-permute-done.refs_4_), channel_id=1, source_target_pairs={{0,2},{2,0},{1,3},{3,1},{4,6},{6,4},{5,7},{7,5},{8,10},{10,8},{9,1... | collective-permute-start | bytes 393224 | tf_op jit(solution)/shard_map/ppermute | solution.py:23
  18.1 6.3 %collective-permute-start.2 = (bf16[8,8192]{1,0:T(8,128)(2,1)S(1)}, bf16[8,8192]{1,0:T(8,128)(2,1)S(1)}, u32[]{:S(2)}, u32[]{:S(2)}) collective-permute-start(bf16[8,8192]{1,0:T(8,128)(2,1)S(1)} %collective-permute-done.1.refs_0_), channel_id=1, source_target_pairs={{0,2},{2,0},{1,3},{3,1},{4,6},{6,4},{5,7},{7,5},{8,10},{10,8},{9,1... | collective-permute-start | bytes 393224 | tf_op jit(solution)/shard_map/ppermute | solution.py:23
  18.6 5.8 %collective-permute-start.6 = (bf16[8,8192]{1,0:T(8,128)(2,1)S(1)}, bf16[8,8192]{1,0:T(8,128)(2,1)S(1)}, u32[]{:S(2)}, u32[]{:S(2)}) collective-permute-start(bf16[8,8192]{1,0:T(8,128)(2,1)S(1)} %collective-permute-done.refs_4_), channel_id=1, source_target_pairs={{0,1},{1,0},{2,3},{3,2},{4,5},{5,4},{6,7},{7,6},{8,9},{9,8},{10,11... | collective-permute-start | bytes 393224 | tf_op jit(solution)/shard_map/ppermute | solution.py:23
  18.6 5.8 %collective-permute-start.3 = (bf16[8,8192]{1,0:T(8,128)(2,1)S(1)}, bf16[8,8192]{1,0:T(8,128)(2,1)S(1)}, u32[]{:S(2)}, u32[]{:S(2)}) collective-permute-start(bf16[8,8192]{1,0:T(8,128)(2,1)S(1)} %collective-permute-done.1.refs_0_), channel_id=1, source_target_pairs={{0,1},{1,0},{2,3},{3,2},{4,5},{5,4},{6,7},{7,6},{8,9},{9,8},{10,11... | collective-permute-start | bytes 393224 | tf_op jit(solution)/shard_map/ppermute | solution.py:23
  19.5 4.9 %collective-permute-start.11 = (bf16[8,8192]{1,0:T(8,128)(2,1)S(1)}, bf16[8,8192]{1,0:T(8,128)(2,1)S(1)}, u32[]{:S(2)}, u32[]{:S(2)}) collective-permute-start(bf16[8,8192]{1,0:T(8,128)(2,1)S(1)} %collective-permute-done.9.refs_9_), channel_id=1, source_target_pairs={{0,1},{1,0},{2,3},{3,2},{4,5},{5,4},{6,7},{7,6},{8,9},{9,8},{10,11... | collective-permute-start | bytes 393224 | tf_op jit(solution)/shard_map/ppermute | solution.py:23
  22.3 2.1 %collective-permute-start.7 = (bf16[8,8192]{1,0:T(8,128)(2,1)S(1)}, bf16[8,8192]{1,0:T(8,128)(2,1)S(1)}, u32[]{:S(2)}, u32[]{:S(2)}) collective-permute-start(bf16[8,8192]{1,0:T(8,128)(2,1)S(1)} %collective-permute-done.5.refs_5_), channel_id=1, source_target_pairs={{0,1},{1,0},{2,3},{3,2},{4,5},{5,4},{6,7},{7,6},{8,9},{9,8},{10,11... | collective-permute-start | bytes 393224 | tf_op jit(solution)/shard_map/ppermute | solution.py:23
  24.4 1.3 %collective-permute-start.4 = (bf16[8,8192]{1,0:T(8,128)(2,1)S(1)}, bf16[8,8192]{1,0:T(8,128)(2,1)S(1)}, u32[]{:S(2)}, u32[]{:S(2)}) collective-permute-start(bf16[8,8192]{1,0:T(8,128)(2,1)S(1)} %collective-permute-done.2.refs_1_), channel_id=1, source_target_pairs={{0,1},{1,0},{2,3},{3,2},{4,5},{5,4},{6,7},{7,6},{8,9},{9,8},{10,11... | collective-permute-start | bytes 393224 | tf_op jit(solution)/shard_map/ppermute | solution.py:23
  28.7 1.6 %collective-permute-start.16 = (bf16[16,8192]{1,0:T(8,128)(2,1)S(1)}, bf16[16,8192]{1,0:T(8,128)(2,1)S(1)}, u32[]{:S(2)}, u32[]{:S(2)}) collective-permute-start(bf16[16,8192]{1,0:T(8,128)(2,1)S(1)} %get-tuple-element.27), channel_id=1, source_target_pairs={{0,1},{1,0},{2,3},{3,2},{4,5},{5,4},{6,7},{7,6},{8,9},{9,8},{10,11... | collective-permute-start | bytes 786440 | tf_op jit(solution)/shard_map/ppermute | solution.py:23
  28.9 4.4 %collective-permute-start.15 = (bf16[16,8192]{1,0:T(8,128)(2,1)S(1)}, bf16[16,8192]{1,0:T(8,128)(2,1)S(1)}, u32[]{:S(2)}, u32[]{:S(2)}) collective-permute-start(bf16[16,8192]{1,0:T(8,128)(2,1)S(1)} %get-tuple-element.25), channel_id=1, source_target_pairs={{0,1},{1,0},{2,3},{3,2},{4,5},{5,4},{6,7},{7,6},{8,9},{9,8},{10,11... | collective-permute-start | bytes 786440 | tf_op jit(solution)/shard_map/ppermute | solution.py:23
  29.3 1.8 %collective-permute-start.19 = (bf16[16,8192]{1,0:T(8,128)(2,1)S(1)}, bf16[16,8192]{1,0:T(8,128)(2,1)S(1)}, u32[]{:S(2)}, u32[]{:S(2)}) collective-permute-start(bf16[16,8192]{1,0:T(8,128)(2,1)S(1)} %get-tuple-element.30), channel_id=1, source_target_pairs={{0,1},{1,0},{2,3},{3,2},{4,5},{5,4},{6,7},{7,6},{8,9},{9,8},{10,11... | collective-permute-start | bytes 786440 | tf_op jit(solution)/shard_map/ppermute | solution.py:23
  29.5 3.1 %collective-permute-start.23 = (bf16[16,8192]{1,0:T(8,128)(2,1)S(1)}, bf16[16,8192]{1,0:T(8,128)(2,1)S(1)}, u32[]{:S(2)}, u32[]{:S(2)}) collective-permute-start(bf16[16,8192]{1,0:T(8,128)(2,1)S(1)} %get-tuple-element.32), channel_id=1, source_target_pairs={{0,1},{1,0},{2,3},{3,2},{4,5},{5,4},{6,7},{7,6},{8,9},{9,8},{10,11... | collective-permute-start | bytes 786440 | tf_op jit(solution)/shard_map/ppermute | solution.py:23
  30.4 6.4 %collective-permute-start.17 = (bf16[8,8192]{1,0:T(8,128)(2,1)S(1)}, bf16[8,8192]{1,0:T(8,128)(2,1)S(1)}, u32[]{:S(2)}, u32[]{:S(2)}) collective-permute-start(bf16[8,8192]{1,0:T(8,128)(2,1)S(1)} %add_convert_fusion.6), channel_id=1, source_target_pairs={{0,2},{2,0},{1,3},{3,1},{4,6},{6,4},{5,7},{7,5},{8,10},{10,8},{9,1... | collective-permute-start | bytes 393224 | tf_op jit(solution)/shard_map/ppermute | solution.py:23
  31.1 9.2 %collective-permute-start.20 = (bf16[8,8192]{1,0:T(8,128)(2,1)S(1)}, bf16[8,8192]{1,0:T(8,128)(2,1)S(1)}, u32[]{:S(2)}, u32[]{:S(2)}) collective-permute-start(bf16[8,8192]{1,0:T(8,128)(2,1)S(1)} %add_convert_fusion.5), channel_id=1, source_target_pairs={{0,2},{2,0},{1,3},{3,1},{4,6},{6,4},{5,7},{7,5},{8,10},{10,8},{9,1... | collective-permute-start | bytes 393224 | tf_op jit(solution)/shard_map/ppermute | solution.py:23
  32.6 9.8 %collective-permute-start.24 = (bf16[8,8192]{1,0:T(8,128)(2,1)S(1)}, bf16[8,8192]{1,0:T(8,128)(2,1)S(1)}, u32[]{:S(2)}, u32[]{:S(2)}) collective-permute-start(bf16[8,8192]{1,0:T(8,128)(2,1)S(1)} %add_convert_fusion.2), channel_id=1, source_target_pairs={{0,2},{2,0},{1,3},{3,1},{4,6},{6,4},{5,7},{7,5},{8,10},{10,8},{9,1... | collective-permute-start | bytes 393224 | tf_op jit(solution)/shard_map/ppermute | solution.py:23
  36.8 7.6 %collective-permute-start.18 = (bf16[8,8192]{1,0:T(8,128)(2,1)S(1)}, bf16[8,8192]{1,0:T(8,128)(2,1)S(1)}, u32[]{:S(2)}, u32[]{:S(2)}) collective-permute-start(bf16[8,8192]{1,0:T(8,128)(2,1)S(1)} %add_convert_fusion.7), channel_id=1, source_target_pairs={{0,2},{2,0},{1,3},{3,1},{4,6},{6,4},{5,7},{7,5},{8,10},{10,8},{9,1... | collective-permute-start | bytes 393224 | tf_op jit(solution)/shard_map/ppermute | solution.py:23
  37.3 11.6 %collective-permute-start.22 = (bf16[8,8192]{1,0:T(8,128)(2,1)S(1)}, bf16[8,8192]{1,0:T(8,128)(2,1)S(1)}, u32[]{:S(2)}, u32[]{:S(2)}) collective-permute-start(bf16[8,8192]{1,0:T(8,128)(2,1)S(1)} %add_convert_fusion.3), channel_id=1, source_target_pairs={{0,8},{4,12},{8,0},{12,4},{1,9},{5,13},{9,1},{13,5},{2,10},{6,14},... | collective-permute-start | bytes 393224 | tf_op jit(solution)/shard_map/ppermute | solution.py:27
  40.3 8.6 %collective-permute-start.21 = (bf16[8,8192]{1,0:T(8,128)(2,1)S(1)}, bf16[8,8192]{1,0:T(8,128)(2,1)S(1)}, u32[]{:S(2)}, u32[]{:S(2)}) collective-permute-start(bf16[8,8192]{1,0:T(8,128)(2,1)S(1)} %add_convert_fusion.4), channel_id=1, source_target_pairs={{0,12},{4,8},{8,4},{12,0},{1,13},{5,9},{9,5},{13,1},{2,14},{6,10},... | collective-permute-start | bytes 393224 | tf_op jit(solution)/shard_map/ppermute | solution.py:27
  42.4 7.3 %collective-permute-start.25 = (bf16[8,8192]{1,0:T(8,128)(2,1)S(1)}, bf16[8,8192]{1,0:T(8,128)(2,1)S(1)}, u32[]{:S(2)}, u32[]{:S(2)}) collective-permute-start(bf16[8,8192]{1,0:T(8,128)(2,1)S(1)} %add_convert_fusion.1), channel_id=1, source_target_pairs={{0,4},{4,0},{8,12},{12,8},{1,5},{5,1},{9,13},{13,9},{2,6},{6,2},{1... | collective-permute-start | bytes 393224 | tf_op jit(solution)/shard_map/ppermute | solution.py:27

commit v3 on v2

--- a/solution.py
+++ b/solution.py
@@ -12,11 +12,10 @@
 VMEM = pltpu.VMEM
 SWAP = ((0, 1), (1, 0))
 NAMED = 2
-WEIGHT_COPIES = 4
 WHOLE = pl.BlockSpec(memory_space=VMEM)
 SCALAR = pl.BlockSpec(memory_space=pltpu.SMEM)
 FAR = pl.BlockSpec(memory_space=pltpu.HBM)
-PARAMS = pltpu.CompilerParams(vmem_limit_bytes=12 << 20)
+PARAMS = pltpu.CompilerParams(vmem_limit_bytes=24 << 20)
 
 
 def other(x, axis):
@@ -32,8 +31,8 @@
 
 
 def prepare_kernel(
-    home_hbm, adapter_hbm, tokens_hbm, w_hbm, a_hbm, b_hbm, which_ref, w_ref, a_ref, b_ref,
-    home_ref, adapter_ref, tokens_ref, table_sems, weight_sems, sems, *, tok_rows,
+    home_hbm, adapter_hbm, tokens_hbm, a_hbm, b_hbm, x_hbm, which_ref, a_ref, b_ref, x_ref,
+    home_ref, adapter_ref, tokens_ref, table_sems, sems, *, tok_rows,
 ):
     store, rank, _ = a_hbm.shape
     requests, devices = tokens_hbm.shape
@@ -42,12 +41,8 @@
     tables = []
     for i, (src, dst) in enumerate(((home_hbm, home_ref), (adapter_hbm, adapter_ref), (tokens_hbm, tokens_ref))):
         tables.append(pltpu.make_async_copy(src, dst, table_sems.at[i]))
-    weights = []
-    share = w_hbm.shape[0] // WEIGHT_COPIES
-    for i in range(WEIGHT_COPIES):
-        rows = pl.ds(i * share, share)
-        weights.append(pltpu.make_async_copy(w_hbm.at[rows], w_ref.at[rows], weight_sems.at[i]))
-    for copy in tables + weights:
+    own = pltpu.make_async_copy(x_hbm, x_ref, sems.at[2 * NAMED])
+    for copy in (*tables, own):
         copy.start()
     for copy in tables:
         copy.wait()
@@ -87,28 +82,28 @@
         return carry
 
     lax.fori_loop(0, devices, rows_of, 0)
-    for copy in copies + weights:
+    for copy in (*copies, own):
         copy.wait()
 
 
-def prepare(home, adapter, tokens, w, a, b, tok_rows):
+def prepare(home, adapter, tokens, a, b, x, tok_rows):
     _, rank, width = a.shape
     rows = tokens.shape[0] * tok_rows
-    sources = (home, adapter, tokens.T, w, a, b)
+    sources = (home, adapter, tokens.T, a, b, x)
     return pl.pallas_call(
         functools.partial(prepare_kernel, tok_rows=tok_rows),
         out_shape=(
             VMEM((rows, 1), jnp.int32),
-            VMEM(w.shape, BF16),
             VMEM((NAMED * rank, width), BF16),
             VMEM((NAMED * rank, width), BF16),
+            VMEM(x.shape, BF16),
         ),
         in_specs=[FAR] * len(sources),
         out_specs=(WHOLE,) * 4,
         scratch_shapes=[pltpu.SMEM(v.shape, jnp.int32) for v in sources[:3]]
-        + [pltpu.SemaphoreType.DMA((n,)) for n in (3, WEIGHT_COPIES, 2 * NAMED)],
+        + [pltpu.SemaphoreType.DMA((n,)) for n in (3, 2 * NAMED + 1)],
         compiler_params=PARAMS,
-        cost_estimate=pl.CostEstimate(flops=0, bytes_accessed=12 << 20, transcendentals=0),
+        cost_estimate=pl.CostEstimate(flops=0, bytes_accessed=4 << 20, transcendentals=0),
         name="prepare",
     )(*[pltpu.with_memory_space_constraint(v, pltpu.HBM) for v in sources])
 
@@ -148,12 +143,12 @@
 
 def partial_rows(which, w, a, b, xs, parts, rank):
     rows, width = xs[0].shape
-    held = [pltpu.with_memory_space_constraint(v, VMEM) for v in (which, w, a, b, *xs)]
+    which, a, b, *xs = [pltpu.with_memory_space_constraint(v, VMEM) for v in (which, a, b, *xs)]
     total = 4 * rows * len(parts)
     return pl.pallas_call(
         functools.partial(partial_kernel, parts=parts, rank=rank),
         out_shape=(VMEM((2 * rows, width), F32), VMEM((2 * rows, width), BF16)) * len(parts),
-        in_specs=[WHOLE] * len(held),
+        in_specs=[WHOLE] * (4 + len(xs)),
         out_specs=(WHOLE,) * (2 * len(parts)),
         scratch_shapes=[VMEM((total, width), BF16)],
         compiler_params=PARAMS,
@@ -161,14 +156,14 @@
             flops=2 * total * width * (w.shape[0] + 2 * a.shape[0]), bytes_accessed=16 << 20, transcendentals=0
         ),
         name="partial_rows",
-    )(*held)
+    )(which, w, a, b, *xs)
 
 
 def shards(attention_out, o_weight, a_down, b_up, adapter_home, req_adapter, req_tokens):
     tok_rows, width = attention_out.shape
     rank = a_down.shape[1]
     planes = lax.axis_size("z")
-    which, w, a, b = prepare(adapter_home, req_adapter, req_tokens, o_weight, a_down, b_up, tok_rows)
+    which, a, b, own = prepare(adapter_home, req_adapter, req_tokens, a_down, b_up, attention_out, tok_rows)
 
     far = {0: attention_out, 1: across(attention_out, 1)}
     for e in range(2, planes, 2):
@@ -179,8 +174,8 @@
     parts = tuple(range(planes))[::-1]
     xs = []
     for e in parts:
-        xs += [far[e], near[e], other(far[e], "core"), other(near[e], "core")]
-    sums = partial_rows(which, w, a, b, xs, parts, rank)
+        xs += [far[e] if e else own, near[e], other(far[e], "core"), other(near[e], "core")]
+    sums = partial_rows(which, o_weight, a, b, xs, parts, rank)
     out = None
     arriving = []
     before = ()

time: 50.7 us -> 50 us (0.986)
  starting transfers between devices: 21.4 us -> 23 us
  Pallas kernels: 7.92 us -> 6.68 us
  waiting for transfers between devices: 20.1 us -> 19.1 us
    ppermute x20, starting transfers between devices: 9.41 us -> 11.3 us  [other(): return lax.ppermute(x, axis, SWAP)]
    ppermute x20, waiting for transfers between devices: 11.8 us -> 9.94 us  [other(): return lax.ppermute(x, axis, SWAP)]
    pallas_call x1, Pallas kernels: 4.95 us -> 3.71 us  [prepare(): pl.pallas_call(functools.partial(prepare_kernel, tok_rows=tok_rows), out_...]
    ppermute x6, waiting for transfers between devices: 8.28 us -> 9.13 us  [across(): lax.ppermute(x, 'z', [(i, i ^ away) for i in range(lax.axis_size('z'))])]
  transfers between devices with their start and end apart: 26 -> 26, of which waited for: 12 -> 10; matrix products, arithmetic and copies ran while one was open for 1% -> 1% of each run, Pallas kernels for 10% -> 7%
where the time goes in v3:
time: 50 us; the launch traced here: 49.9 us
  starting transfers between devices  23 us (46%)
  waiting for transfers between devices  19.1 us (38%)
  Pallas kernels  6.68 us (13%)
  other arithmetic  1.01 us (2%)
    ppermute x6, starting transfers between devices, across(): lax.ppermute(x, 'z', [(i, i ^ away) for i in range(lax.axis_size('z'))])  11.8 us
    ppermute x20, starting transfers between devices, other(): return lax.ppermute(x, axis, SWAP)  11.3 us
    ppermute x20, waiting for transfers between devices, other(): return lax.ppermute(x, axis, SWAP)  9.94 us
    ppermute x6, waiting for transfers between devices, across(): lax.ppermute(x, 'z', [(i, i ^ away) for i in range(lax.axis_size('z'))])  9.13 us
    pallas_call x1, Pallas kernels, prepare(): pl.pallas_call(functools.partial(prepare_kernel, tok_rows=tok_rows), out_...  3.71 us
    pallas_call x1, Pallas kernels, partial_rows(): pl.pallas_call(functools.partial(partial_kernel, parts=parts, rank=rank),...  2.97 us
  transfers between devices with their start and end apart: 26, of which 10 were waited for; matrix products, arithmetic and copies ran while one was open for 1% of the time, Pallas kernels for 7%

profile of v3, /device:TPU:0, one launch (start us, length us, event | category | flops | bytes accessed | tf_op | source)
XLA Modules:
  0.0 49.9 jit_solution(7632476918525296690)
XLA Ops:
  0.0 4.0 %collective-permute-start = (bf16[8,8192]{1,0:T(8,128)(2,1)}, bf16[8,8192]{1,0:T(8,128)(2,1)S(1)}, u32[]{:S(2)}, u32[]{:S(2)}) collective-permute-start(bf16[8,8192]{1,0:T(8,128)(2,1)} %x_hbm.1), channel_id=1, source_target_pairs={{0,8},{4,12},{8,0},{12,4},{1,9},{5,13},{9,1},{13,5},{2,10},{6,14},... | collective-permute-start | bytes 393224 | tf_op jit(solution)/shard_map/ppermute | solution.py:26
  4.0 1.6 %collective-permute-start.8 = (bf16[8,8192]{1,0:T(8,128)(2,1)}, bf16[8,8192]{1,0:T(8,128)(2,1)S(1)}, u32[]{:S(2)}, u32[]{:S(2)}) collective-permute-start(bf16[8,8192]{1,0:T(8,128)(2,1)} %x_hbm.1), channel_id=1, source_target_pairs={{0,4},{4,0},{8,12},{12,8},{1,5},{5,1},{9,13},{13,9},{2,6},{6,2},{1... | collective-permute-start | bytes 393224 | tf_op jit(solution)/shard_map/ppermute | solution.py:26
  5.6 1.5 %collective-permute-start.12 = (bf16[8,8192]{1,0:T(8,128)(2,1)}, bf16[8,8192]{1,0:T(8,128)(2,1)S(1)}, u32[]{:S(2)}, u32[]{:S(2)}) collective-permute-start(bf16[8,8192]{1,0:T(8,128)(2,1)} %x_hbm.1), channel_id=1, source_target_pairs={{0,2},{2,0},{1,3},{3,1},{4,6},{6,4},{5,7},{7,5},{8,10},{10,8},{9,1... | collective-permute-start | bytes 393224 | tf_op jit(solution)/shard_map/ppermute | solution.py:22
  7.1 3.7 %prepare.1 = (s32[128,1]{1,0:T(8,128)S(1)}, bf16[128,8192]{1,0:T(8,128)(2,1)S(1)}, bf16[128,8192]{1,0:T(8,128)(2,1)S(1)}, bf16[8,8192]{1,0:T(8,128)(2,1)S(1)}) custom-call(s32[64]{0:T(128)} %home_hbm.1, s32[64]{0:T(128)} %adapter_hbm.1, s32[4,16]{1,0:T(4,128)} %bitcast.1, bf16[4,64,8192]{2,1,0:T(8,128)(2,1)} %a_hbm.1, bf16[4,64,8192]{2,1,0:T(8,128)(2,1)} %b_hbm.1, ...), custom_call_target="tpu_custom_call" | custom-call | bytes 4194304 | tf_op jit(solution)/shard_map/prepare/pallas_call | solution.py:93
  10.9 0.5 %collective-permute-start.1 = (bf16[8,8192]{1,0:T(8,128)(2,1)S(1)}, bf16[8,8192]{1,0:T(8,128)(2,1)S(1)}, u32[]{:S(2)}, u32[]{:S(2)}) collective-permute-start(bf16[8,8192]{1,0:T(8,128)(2,1)S(1)} %collective-permute-done.refs_4_), channel_id=1, source_target_pairs={{0,4},{4,0},{8,12},{12,8},{1,5},{5,1},{9,13},{13,9},{2,6},{6,2},{1... | collective-permute-start | bytes 393224 | tf_op jit(solution)/shard_map/ppermute | solution.py:26
  11.4 1.5 %collective-permute-start.9 = (bf16[8,8192]{1,0:T(8,128)(2,1)S(1)}, bf16[8,8192]{1,0:T(8,128)(2,1)S(1)}, u32[]{:S(2)}, u32[]{:S(2)}) collective-permute-start(bf16[8,8192]{1,0:T(8,128)(2,1)S(1)} %collective-permute-done.8.refs_8_), channel_id=1, source_target_pairs={{0,2},{2,0},{1,3},{3,1},{4,6},{6,4},{5,7},{7,5},{8,10},{10,8},{9,1... | collective-permute-start | bytes 393224 | tf_op jit(solution)/shard_map/ppermute | solution.py:22
  12.9 0.2 collective-permute-start.14
  13.1 0.5 %collective-permute-start.5 = (bf16[8,8192]{1,0:T(8,128)(2,1)S(1)}, bf16[8,8192]{1,0:T(8,128)(2,1)S(1)}, u32[]{:S(2)}, u32[]{:S(2)}) collective-permute-start(bf16[8,8192]{1,0:T(8,128)(2,1)S(1)} %collective-permute-done.refs_4_), channel_id=1, source_target_pairs={{0,2},{2,0},{1,3},{3,1},{4,6},{6,4},{5,7},{7,5},{8,10},{10,8},{9,1... | collective-permute-start | bytes 393224 | tf_op jit(solution)/shard_map/ppermute | solution.py:22
  13.7 2.9 %collective-permute-done.1.refs_0_ = bf16[8,8192]{1,0:T(8,128)(2,1)S(1)} collective-permute-done((bf16[8,8192]{1,0:T(8,128)(2,1)S(1)}, bf16[8,8192]{1,0:T(8,128)(2,1)S(1)}, u32[]{:S(2)}, u32[]{:S(2)}) %collective-permute-start.1) | collective-permute-done | bytes 131104 | tf_op jit(solution)/shard_map/ppermute | solution.py:26
  16.6 0.6 %collective-permute-start.2 = (bf16[8,8192]{1,0:T(8,128)(2,1)S(1)}, bf16[8,8192]{1,0:T(8,128)(2,1)S(1)}, u32[]{:S(2)}, u32[]{:S(2)}) collective-permute-start(bf16[8,8192]{1,0:T(8,128)(2,1)S(1)} %collective-permute-done.1.refs_0_), channel_id=1, source_target_pairs={{0,2},{2,0},{1,3},{3,1},{4,6},{6,4},{5,7},{7,5},{8,10},{10,8},{9,1... | collective-permute-start | bytes 393224 | tf_op jit(solution)/shard_map/ppermute | solution.py:22
  17.2 0.5 collective-permute-done.9.refs_9_
  17.7 0.5 collective-permute-start.11
  18.2 2.3 %collective-permute-done.5.refs_5_ = bf16[8,8192]{1,0:T(8,128)(2,1)S(1)} collective-permute-done((bf16[8,8192]{1,0:T(8,128)(2,1)S(1)}, bf16[8,8192]{1,0:T(8,128)(2,1)S(1)}, u32[]{:S(2)}, u32[]{:S(2)}) %collective-permute-start.5) | collective-permute-done | bytes 131104 | tf_op jit(solution)/shard_map/ppermute | solution.py:22
  20.5 2.4 %collective-permute-done.2.refs_1_ = bf16[8,8192]{1,0:T(8,128)(2,1)S(1)} collective-permute-done((bf16[8,8192]{1,0:T(8,128)(2,1)S(1)}, bf16[8,8192]{1,0:T(8,128)(2,1)S(1)}, u32[]{:S(2)}, u32[]{:S(2)}) %collective-permute-start.2) | collective-permute-done | bytes 131104 | tf_op jit(solution)/shard_map/ppermute | solution.py:22
  23.0 1.3 %collective-permute-done.4.refs_3_ = bf16[8,8192]{1,0:T(8,128)(2,1)S(1)} collective-permute-done((bf16[8,8192]{1,0:T(8,128)(2,1)S(1)}, bf16[8,8192]{1,0:T(8,128)(2,1)S(1)}, u32[]{:S(2)}, u32[]{:S(2)}) %collective-permute-start.4) | collective-permute-done | bytes 131104 | tf_op jit(solution)/shard_map/ppermute | solution.py:22
  24.3 3.0 %partial_rows.1 = (f32[16,8192]{1,0:T(8,128)S(1)}, bf16[16,8192]{1,0:T(8,128)(2,1)S(1)}, f32[16,8192]{1,0:T(8,128)S(1)}, bf16[16,8192]{1,0:T(8,128)(2,1)S(1)}, f...) custom-call(s32[128,1]{1,0:T(8,128)S(1)} %get-tuple-element.19.which, ...), custom_call_target="tpu_custom_call" | custom-call | flops 1610612736 | bytes 16777216 | tf_op jit(solution)/shard_map/partial_rows/pallas_call | solution.py:148
  27.2 0.2 collective-permute-start.16
  27.5 0.4 collective-permute-start.15
  28.0 0.4 collective-permute-start.23
  28.3 0.5 %collective-permute-done.16 = bf16[16,8192]{1,0:T(8,128)(2,1)S(1)} collective-permute-done((bf16[16,8192]{1,0:T(8,128)(2,1)S(1)}, bf16[16,8192]{1,0:T(8,128)(2,1)S(1)}, u32[]{:S(2)}, u32[]{:S(2)}) %collective-permute-start.16) | collective-permute-done | bytes 262176 | tf_op jit(solution)/shard_map/ppermute | solution.py:22
  28.9 1.6 %collective-permute-start.17 = (bf16[8,8192]{1,0:T(8,128)(2,1)S(1)}, bf16[8,8192]{1,0:T(8,128)(2,1)S(1)}, u32[]{:S(2)}, u32[]{:S(2)}) collective-permute-start(bf16[8,8192]{1,0:T(8,128)(2,1)S(1)} %add_convert_fusion.6), channel_id=1, source_target_pairs={{0,2},{2,0},{1,3},{3,1},{4,6},{6,4},{5,7},{7,5},{8,10},{10,8},{9,1... | collective-permute-start | bytes 393224 | tf_op jit(solution)/shard_map/ppermute | solution.py:22
  30.5 0.7 %collective-permute-start.20 = (bf16[8,8192]{1,0:T(8,128)(2,1)S(1)}, bf16[8,8192]{1,0:T(8,128)(2,1)S(1)}, u32[]{:S(2)}, u32[]{:S(2)}) collective-permute-start(bf16[8,8192]{1,0:T(8,128)(2,1)S(1)} %add_convert_fusion.5), channel_id=1, source_target_pairs={{0,2},{2,0},{1,3},{3,1},{4,6},{6,4},{5,7},{7,5},{8,10},{10,8},{9,1... | collective-permute-start | bytes 393224 | tf_op jit(solution)/shard_map/ppermute | solution.py:22
  31.3 1.4 %collective-permute-start.24 = (bf16[8,8192]{1,0:T(8,128)(2,1)S(1)}, bf16[8,8192]{1,0:T(8,128)(2,1)S(1)}, u32[]{:S(2)}, u32[]{:S(2)}) collective-permute-start(bf16[8,8192]{1,0:T(8,128)(2,1)S(1)} %add_convert_fusion.2), channel_id=1, source_target_pairs={{0,2},{2,0},{1,3},{3,1},{4,6},{6,4},{5,7},{7,5},{8,10},{10,8},{9,1... | collective-permute-start | bytes 393224 | tf_op jit(solution)/shard_map/ppermute | solution.py:22
  32.7 2.6 %collective-permute-done.17 = bf16[8,8192]{1,0:T(8,128)(2,1)S(1)} collective-permute-done((bf16[8,8192]{1,0:T(8,128)(2,1)S(1)}, bf16[8,8192]{1,0:T(8,128)(2,1)S(1)}, u32[]{:S(2)}, u32[]{:S(2)}) %collective-permute-start.17) | collective-permute-done | bytes 131104 | tf_op jit(solution)/shard_map/ppermute | solution.py:22
  35.3 1.5 %collective-permute-start.18 = (bf16[8,8192]{1,0:T(8,128)(2,1)S(1)}, bf16[8,8192]{1,0:T(8,128)(2,1)S(1)}, u32[]{:S(2)}, u32[]{:S(2)}) collective-permute-start(bf16[8,8192]{1,0:T(8,128)(2,1)S(1)} %add_convert_fusion.7), channel_id=1, source_target_pairs={{0,2},{2,0},{1,3},{3,1},{4,6},{6,4},{5,7},{7,5},{8,10},{10,8},{9,1... | collective-permute-start | bytes 393224 | tf_op jit(solution)/shard_map/ppermute | solution.py:22
  36.9 3.3 %collective-permute-start.22 = (bf16[8,8192]{1,0:T(8,128)(2,1)S(1)}, bf16[8,8192]{1,0:T(8,128)(2,1)S(1)}, u32[]{:S(2)}, u32[]{:S(2)}) collective-permute-start(bf16[8,8192]{1,0:T(8,128)(2,1)S(1)} %add_convert_fusion.3), channel_id=1, source_target_pairs={{0,8},{4,12},{8,0},{12,4},{1,9},{5,13},{9,1},{13,5},{2,10},{6,14},... | collective-permute-start | bytes 393224 | tf_op jit(solution)/shard_map/ppermute | solution.py:26
  40.3 0.7 %collective-permute-start.21 = (bf16[8,8192]{1,0:T(8,128)(2,1)S(1)}, bf16[8,8192]{1,0:T(8,128)(2,1)S(1)}, u32[]{:S(2)}, u32[]{:S(2)}) collective-permute-start(bf16[8,8192]{1,0:T(8,128)(2,1)S(1)} %add_convert_fusion.4), channel_id=1, source_target_pairs={{0,12},{4,8},{8,4},{12,0},{1,13},{5,9},{9,5},{13,1},{2,14},{6,10},... | collective-permute-start | bytes 393224 | tf_op jit(solution)/shard_map/ppermute | solution.py:26
  41.0 1.6 %collective-permute-start.25 = (bf16[8,8192]{1,0:T(8,128)(2,1)S(1)}, bf16[8,8192]{1,0:T(8,128)(2,1)S(1)}, u32[]{:S(2)}, u32[]{:S(2)}) collective-permute-start(bf16[8,8192]{1,0:T(8,128)(2,1)S(1)} %add_convert_fusion.1), channel_id=1, source_target_pairs={{0,4},{4,0},{8,12},{12,8},{1,5},{5,1},{9,13},{13,9},{2,6},{6,2},{1... | collective-permute-start | bytes 393224 | tf_op jit(solution)/shard_map/ppermute | solution.py:26
  42.6 0.3 collective-permute-done.18
  42.9 5.9 %collective-permute-done.22 = bf16[8,8192]{1,0:T(8,128)(2,1)S(1)} collective-permute-done((bf16[8,8192]{1,0:T(8,128)(2,1)S(1)}, bf16[8,8192]{1,0:T(8,128)(2,1)S(1)}, u32[]{:S(2)}, u32[]{:S(2)}) %collective-permute-start.22) | collective-permute-done | bytes 131104 | tf_op jit(solution)/shard_map/ppermute | solution.py:26
  48.8 0.3 collective-permute-done.25
  49.1 0.7 %add_convert_fusion = bf16[8,8192]{1,0:T(8,128)(2,1)} fusion(bf16[8,8192]{1,0:T(8,128)(2,1)S(1)} %collective-permute-done.25, bf16[8,8192]{1,0:T(8,128)(2,1)S(1)} %collective-permute-done.22, bf16[8,8192]{1,0:T(8,128)(2,1)S(1)} %collective-permute-done.21, bf16[8,8192]{1,0:T(8,128)(2,1)S(1)} %collective-permute-done.18, f32[16,8192]{1,0:T(8,128)S(1)} %get-tuple-element.24, ...), kind=kLoop, calls=%fused_computation | loop fusion | flops 720896 | bytes 1048576 | tf_op jit(solution)/shard_map/convert_element_type | solution.py:198
  (32 shorter events, 0.5 us)
Async XLA Ops:
  0.0 10.9 %collective-permute-start = (bf16[8,8192]{1,0:T(8,128)(2,1)}, bf16[8,8192]{1,0:T(8,128)(2,1)S(1)}, u32[]{:S(2)}, u32[]{:S(2)}) collective-permute-start(bf16[8,8192]{1,0:T(8,128)(2,1)} %x_hbm.1), channel_id=1, source_target_pairs={{0,8},{4,12},{8,0},{12,4},{1,9},{5,13},{9,1},{13,5},{2,10},{6,14},... | collective-permute-start | bytes 393224 | tf_op jit(solution)/shard_map/ppermute | solution.py:26
  4.0 7.3 %collective-permute-start.8 = (bf16[8,8192]{1,0:T(8,128)(2,1)}, bf16[8,8192]{1,0:T(8,128)(2,1)S(1)}, u32[]{:S(2)}, u32[]{:S(2)}) collective-permute-start(bf16[8,8192]{1,0:T(8,128)(2,1)} %x_hbm.1), channel_id=1, source_target_pairs={{0,4},{4,0},{8,12},{12,8},{1,5},{5,1},{9,13},{13,9},{2,6},{6,2},{1... | collective-permute-start | bytes 393224 | tf_op jit(solution)/shard_map/ppermute | solution.py:26
  5.6 7.5 %collective-permute-start.13 = (bf16[8,8192]{1,0:T(8,128)(2,1)}, bf16[8,8192]{1,0:T(8,128)(2,1)S(1)}, u32[]{:S(2)}, u32[]{:S(2)}) collective-permute-start(bf16[8,8192]{1,0:T(8,128)(2,1)} %x_hbm.1), channel_id=1, source_target_pairs={{0,1},{1,0},{2,3},{3,2},{4,5},{5,4},{6,7},{7,6},{8,9},{9,8},{10,11... | collective-permute-start | bytes 393224 | tf_op jit(solution)/shard_map/ppermute | solution.py:22
  5.6 7.3 %collective-permute-start.12 = (bf16[8,8192]{1,0:T(8,128)(2,1)}, bf16[8,8192]{1,0:T(8,128)(2,1)S(1)}, u32[]{:S(2)}, u32[]{:S(2)}) collective-permute-start(bf16[8,8192]{1,0:T(8,128)(2,1)} %x_hbm.1), channel_id=1, source_target_pairs={{0,2},{2,0},{1,3},{3,1},{4,6},{6,4},{5,7},{7,5},{8,10},{10,8},{9,1... | collective-permute-start | bytes 393224 | tf_op jit(solution)/shard_map/ppermute | solution.py:22
  7.1 17.1 %copy-start = (bf16[512,8192]{1,0:T(8,128)(2,1)S(1)}, bf16[512,8192]{1,0:T(8,128)(2,1)}, u32[]{:S(2)}) copy-start(bf16[512,8192]{1,0:T(8,128)(2,1)} %w_ref.1) | copy-start | bytes 25165828
  10.9 5.7 %collective-permute-start.1 = (bf16[8,8192]{1,0:T(8,128)(2,1)S(1)}, bf16[8,8192]{1,0:T(8,128)(2,1)S(1)}, u32[]{:S(2)}, u32[]{:S(2)}) collective-permute-start(bf16[8,8192]{1,0:T(8,128)(2,1)S(1)} %collective-permute-done.refs_4_), channel_id=1, source_target_pairs={{0,4},{4,0},{8,12},{12,8},{1,5},{5,1},{9,13},{13,9},{2,6},{6,2},{1... | collective-permute-start | bytes 393224 | tf_op jit(solution)/shard_map/ppermute | solution.py:26
  11.4 5.8 %collective-permute-start.10 = (bf16[8,8192]{1,0:T(8,128)(2,1)S(1)}, bf16[8,8192]{1,0:T(8,128)(2,1)S(1)}, u32[]{:S(2)}, u32[]{:S(2)}) collective-permute-start(bf16[8,8192]{1,0:T(8,128)(2,1)S(1)} %collective-permute-done.8.refs_8_), channel_id=1, source_target_pairs={{0,1},{1,0},{2,3},{3,2},{4,5},{5,4},{6,7},{7,6},{8,9},{9,8},{10,11... | collective-permute-start | bytes 393224 | tf_op jit(solution)/shard_map/ppermute | solution.py:22
  11.4 6.3 %collective-permute-start.9 = (bf16[8,8192]{1,0:T(8,128)(2,1)S(1)}, bf16[8,8192]{1,0:T(8,128)(2,1)S(1)}, u32[]{:S(2)}, u32[]{:S(2)}) collective-permute-start(bf16[8,8192]{1,0:T(8,128)(2,1)S(1)} %collective-permute-done.8.refs_8_), channel_id=1, source_target_pairs={{0,2},{2,0},{1,3},{3,1},{4,6},{6,4},{5,7},{7,5},{8,10},{10,8},{9,1... | collective-permute-start | bytes 393224 | tf_op jit(solution)/shard_map/ppermute | solution.py:22
  12.9 4.8 %collective-permute-start.14 = (bf16[8,8192]{1,0:T(8,128)(2,1)S(1)}, bf16[8,8192]{1,0:T(8,128)(2,1)S(1)}, u32[]{:S(2)}, u32[]{:S(2)}) collective-permute-start(bf16[8,8192]{1,0:T(8,128)(2,1)S(1)} %collective-permute-done.12.refs_13_), channel_id=1, source_target_pairs={{0,1},{1,0},{2,3},{3,2},{4,5},{5,4},{6,7},{7,6},{8,9},{9,8},{10,11... | collective-permute-start | bytes 393224 | tf_op jit(solution)/shard_map/ppermute | solution.py:22
  13.1 7.3 %collective-permute-start.5 = (bf16[8,8192]{1,0:T(8,128)(2,1)S(1)}, bf16[8,8192]{1,0:T(8,128)(2,1)S(1)}, u32[]{:S(2)}, u32[]{:S(2)}) collective-permute-start(bf16[8,8192]{1,0:T(8,128)(2,1)S(1)} %collective-permute-done.refs_4_), channel_id=1, source_target_pairs={{0,2},{2,0},{1,3},{3,1},{4,6},{6,4},{5,7},{7,5},{8,10},{10,8},{9,1... | collective-permute-start | bytes 393224 | tf_op jit(solution)/shard_map/ppermute | solution.py:22
  16.6 6.4 %collective-permute-start.2 = (bf16[8,8192]{1,0:T(8,128)(2,1)S(1)}, bf16[8,8192]{1,0:T(8,128)(2,1)S(1)}, u32[]{:S(2)}, u32[]{:S(2)}) collective-permute-start(bf16[8,8192]{1,0:T(8,128)(2,1)S(1)} %collective-permute-done.1.refs_0_), channel_id=1, source_target_pairs={{0,2},{2,0},{1,3},{3,1},{4,6},{6,4},{5,7},{7,5},{8,10},{10,8},{9,1... | collective-permute-start | bytes 393224 | tf_op jit(solution)/shard_map/ppermute | solution.py:22
  17.2 5.7 %collective-permute-start.6 = (bf16[8,8192]{1,0:T(8,128)(2,1)S(1)}, bf16[8,8192]{1,0:T(8,128)(2,1)S(1)}, u32[]{:S(2)}, u32[]{:S(2)}) collective-permute-start(bf16[8,8192]{1,0:T(8,128)(2,1)S(1)} %collective-permute-done.refs_4_), channel_id=1, source_target_pairs={{0,1},{1,0},{2,3},{3,2},{4,5},{5,4},{6,7},{7,6},{8,9},{9,8},{10,11... | collective-permute-start | bytes 393224 | tf_op jit(solution)/shard_map/ppermute | solution.py:22
  17.7 5.3 %collective-permute-start.3 = (bf16[8,8192]{1,0:T(8,128)(2,1)S(1)}, bf16[8,8192]{1,0:T(8,128)(2,1)S(1)}, u32[]{:S(2)}, u32[]{:S(2)}) collective-permute-start(bf16[8,8192]{1,0:T(8,128)(2,1)S(1)} %collective-permute-done.1.refs_0_), channel_id=1, source_target_pairs={{0,1},{1,0},{2,3},{3,2},{4,5},{5,4},{6,7},{7,6},{8,9},{9,8},{10,11... | collective-permute-start | bytes 393224 | tf_op jit(solution)/shard_map/ppermute | solution.py:22
  17.7 5.2 %collective-permute-start.11 = (bf16[8,8192]{1,0:T(8,128)(2,1)S(1)}, bf16[8,8192]{1,0:T(8,128)(2,1)S(1)}, u32[]{:S(2)}, u32[]{:S(2)}) collective-permute-start(bf16[8,8192]{1,0:T(8,128)(2,1)S(1)} %collective-permute-done.9.refs_9_), channel_id=1, source_target_pairs={{0,1},{1,0},{2,3},{3,2},{4,5},{5,4},{6,7},{7,6},{8,9},{9,8},{10,11... | collective-permute-start | bytes 393224 | tf_op jit(solution)/shard_map/ppermute | solution.py:22
  20.5 2.4 %collective-permute-start.7 = (bf16[8,8192]{1,0:T(8,128)(2,1)S(1)}, bf16[8,8192]{1,0:T(8,128)(2,1)S(1)}, u32[]{:S(2)}, u32[]{:S(2)}) collective-permute-start(bf16[8,8192]{1,0:T(8,128)(2,1)S(1)} %collective-permute-done.5.refs_5_), channel_id=1, source_target_pairs={{0,1},{1,0},{2,3},{3,2},{4,5},{5,4},{6,7},{7,6},{8,9},{9,8},{10,11... | collective-permute-start | bytes 393224 | tf_op jit(solution)/shard_map/ppermute | solution.py:22
  22.9 1.3 %collective-permute-start.4 = (bf16[8,8192]{1,0:T(8,128)(2,1)S(1)}, bf16[8,8192]{1,0:T(8,128)(2,1)S(1)}, u32[]{:S(2)}, u32[]{:S(2)}) collective-permute-start(bf16[8,8192]{1,0:T(8,128)(2,1)S(1)} %collective-permute-done.2.refs_1_), channel_id=1, source_target_pairs={{0,1},{1,0},{2,3},{3,2},{4,5},{5,4},{6,7},{7,6},{8,9},{9,8},{10,11... | collective-permute-start | bytes 393224 | tf_op jit(solution)/shard_map/ppermute | solution.py:22
  27.2 1.6 %collective-permute-start.16 = (bf16[16,8192]{1,0:T(8,128)(2,1)S(1)}, bf16[16,8192]{1,0:T(8,128)(2,1)S(1)}, u32[]{:S(2)}, u32[]{:S(2)}) collective-permute-start(bf16[16,8192]{1,0:T(8,128)(2,1)S(1)} %get-tuple-element.27), channel_id=1, source_target_pairs={{0,1},{1,0},{2,3},{3,2},{4,5},{5,4},{6,7},{7,6},{8,9},{9,8},{10,11... | collective-permute-start | bytes 786440 | tf_op jit(solution)/shard_map/ppermute | solution.py:22
  27.5 5.2 %collective-permute-start.15 = (bf16[16,8192]{1,0:T(8,128)(2,1)S(1)}, bf16[16,8192]{1,0:T(8,128)(2,1)S(1)}, u32[]{:S(2)}, u32[]{:S(2)}) collective-permute-start(bf16[16,8192]{1,0:T(8,128)(2,1)S(1)} %get-tuple-element.25), channel_id=1, source_target_pairs={{0,1},{1,0},{2,3},{3,2},{4,5},{5,4},{6,7},{7,6},{8,9},{9,8},{10,11... | collective-permute-start | bytes 786440 | tf_op jit(solution)/shard_map/ppermute | solution.py:22
  27.8 2.6 %collective-permute-start.19 = (bf16[16,8192]{1,0:T(8,128)(2,1)S(1)}, bf16[16,8192]{1,0:T(8,128)(2,1)S(1)}, u32[]{:S(2)}, u32[]{:S(2)}) collective-permute-start(bf16[16,8192]{1,0:T(8,128)(2,1)S(1)} %get-tuple-element.30), channel_id=1, source_target_pairs={{0,1},{1,0},{2,3},{3,2},{4,5},{5,4},{6,7},{7,6},{8,9},{9,8},{10,11... | collective-permute-start | bytes 786440 | tf_op jit(solution)/shard_map/ppermute | solution.py:22
  28.0 3.2 %collective-permute-start.23 = (bf16[16,8192]{1,0:T(8,128)(2,1)S(1)}, bf16[16,8192]{1,0:T(8,128)(2,1)S(1)}, u32[]{:S(2)}, u32[]{:S(2)}) collective-permute-start(bf16[16,8192]{1,0:T(8,128)(2,1)S(1)} %get-tuple-element.32), channel_id=1, source_target_pairs={{0,1},{1,0},{2,3},{3,2},{4,5},{5,4},{6,7},{7,6},{8,9},{9,8},{10,11... | collective-permute-start | bytes 786440 | tf_op jit(solution)/shard_map/ppermute | solution.py:22
  28.9 6.4 %collective-permute-start.17 = (bf16[8,8192]{1,0:T(8,128)(2,1)S(1)}, bf16[8,8192]{1,0:T(8,128)(2,1)S(1)}, u32[]{:S(2)}, u32[]{:S(2)}) collective-permute-start(bf16[8,8192]{1,0:T(8,128)(2,1)S(1)} %add_convert_fusion.6), channel_id=1, source_target_pairs={{0,2},{2,0},{1,3},{3,1},{4,6},{6,4},{5,7},{7,5},{8,10},{10,8},{9,1... | collective-permute-start | bytes 393224 | tf_op jit(solution)/shard_map/ppermute | solution.py:22
  30.5 9.7 %collective-permute-start.20 = (bf16[8,8192]{1,0:T(8,128)(2,1)S(1)}, bf16[8,8192]{1,0:T(8,128)(2,1)S(1)}, u32[]{:S(2)}, u32[]{:S(2)}) collective-permute-start(bf16[8,8192]{1,0:T(8,128)(2,1)S(1)} %add_convert_fusion.5), channel_id=1, source_target_pairs={{0,2},{2,0},{1,3},{3,1},{4,6},{6,4},{5,7},{7,5},{8,10},{10,8},{9,1... | collective-permute-start | bytes 393224 | tf_op jit(solution)/shard_map/ppermute | solution.py:22
  31.3 9.7 %collective-permute-start.24 = (bf16[8,8192]{1,0:T(8,128)(2,1)S(1)}, bf16[8,8192]{1,0:T(8,128)(2,1)S(1)}, u32[]{:S(2)}, u32[]{:S(2)}) collective-permute-start(bf16[8,8192]{1,0:T(8,128)(2,1)S(1)} %add_convert_fusion.2), channel_id=1, source_target_pairs={{0,2},{2,0},{1,3},{3,1},{4,6},{6,4},{5,7},{7,5},{8,10},{10,8},{9,1... | collective-permute-start | bytes 393224 | tf_op jit(solution)/shard_map/ppermute | solution.py:22
  35.3 7.6 %collective-permute-start.18 = (bf16[8,8192]{1,0:T(8,128)(2,1)S(1)}, bf16[8,8192]{1,0:T(8,128)(2,1)S(1)}, u32[]{:S(2)}, u32[]{:S(2)}) collective-permute-start(bf16[8,8192]{1,0:T(8,128)(2,1)S(1)} %add_convert_fusion.7), channel_id=1, source_target_pairs={{0,2},{2,0},{1,3},{3,1},{4,6},{6,4},{5,7},{7,5},{8,10},{10,8},{9,1... | collective-permute-start | bytes 393224 | tf_op jit(solution)/shard_map/ppermute | solution.py:22
  36.9 12.0 %collective-permute-start.22 = (bf16[8,8192]{1,0:T(8,128)(2,1)S(1)}, bf16[8,8192]{1,0:T(8,128)(2,1)S(1)}, u32[]{:S(2)}, u32[]{:S(2)}) collective-permute-start(bf16[8,8192]{1,0:T(8,128)(2,1)S(1)} %add_convert_fusion.3), channel_id=1, source_target_pairs={{0,8},{4,12},{8,0},{12,4},{1,9},{5,13},{9,1},{13,5},{2,10},{6,14},... | collective-permute-start | bytes 393224 | tf_op jit(solution)/shard_map/ppermute | solution.py:26
  40.3 8.6 %collective-permute-start.21 = (bf16[8,8192]{1,0:T(8,128)(2,1)S(1)}, bf16[8,8192]{1,0:T(8,128)(2,1)S(1)}, u32[]{:S(2)}, u32[]{:S(2)}) collective-permute-start(bf16[8,8192]{1,0:T(8,128)(2,1)S(1)} %add_convert_fusion.4), channel_id=1, source_target_pairs={{0,12},{4,8},{8,4},{12,0},{1,13},{5,9},{9,5},{13,1},{2,14},{6,10},... | collective-permute-start | bytes 393224 | tf_op jit(solution)/shard_map/ppermute | solution.py:26
  41.0 8.2 %collective-permute-start.25 = (bf16[8,8192]{1,0:T(8,128)(2,1)S(1)}, bf16[8,8192]{1,0:T(8,128)(2,1)S(1)}, u32[]{:S(2)}, u32[]{:S(2)}) collective-permute-start(bf16[8,8192]{1,0:T(8,128)(2,1)S(1)} %add_convert_fusion.1), channel_id=1, source_target_pairs={{0,4},{4,0},{8,12},{12,8},{1,5},{5,1},{9,13},{13,9},{2,6},{6,2},{1... | collective-permute-start | bytes 393224 | tf_op jit(solution)/shard_map/ppermute | solution.py:26

commit v4 on v3

--- a/solution.py
+++ b/solution.py
@@ -166,10 +166,11 @@
     which, a, b, own = prepare(adapter_home, req_adapter, req_tokens, a_down, b_up, attention_out, tok_rows)
 
     far = {0: attention_out, 1: across(attention_out, 1)}
+    near = {e: other(far[e], "y") for e in range(2)}
     for e in range(2, planes, 2):
         far[e] = after(across(attention_out, e), which)
-        far[e + 1] = across(far[e], 1)
-    near = {e: other(far[e], "y") for e in range(planes)}
+        near[e] = other(far[e], "y")
+        far[e + 1], near[e + 1] = across(far[e], 1), across(near[e], 1)
 
     parts = tuple(range(planes))[::-1]
     xs = []

time: 50 us -> 48.7 us (0.974)
  starting transfers between devices: 23 us -> 21.7 us
    ppermute x20 -> x19, starting transfers between devices: 11.3 us -> 9.85 us  [other(): return lax.ppermute(x, axis, SWAP)]
    ppermute x6 -> x7, waiting for transfers between devices: 9.13 us -> 7.8 us  [across(): lax.ppermute(x, 'z', [(i, i ^ away) for i in range(lax.axis_size('z'))])]
    ppermute x20 -> x19, waiting for transfers between devices: 9.94 us -> 11.2 us  [other(): return lax.ppermute(x, axis, SWAP)]
    ppermute x6 -> x7, starting transfers between devices: 11.8 us -> 11.9 us  [across(): lax.ppermute(x, 'z', [(i, i ^ away) for i in range(lax.axis_size('z'))])]
  transfers between devices with their start and end apart: 26 -> 26, of which waited for: 10 -> 9; matrix products, arithmetic and copies ran while one was open for 1% -> 1% of each run, Pallas kernels for 7% -> 8%
where the time goes in v4:
time: 48.7 us; the launch traced here: 48.5 us
  starting transfers between devices  21.7 us (45%)
  waiting for transfers between devices  19 us (39%)
  Pallas kernels  6.68 us (14%)
  other arithmetic  1.01 us (2%)
    ppermute x7, starting transfers between devices, across(): lax.ppermute(x, 'z', [(i, i ^ away) for i in range(lax.axis_size('z'))])  11.9 us
    ppermute x19, waiting for transfers between devices, other(): return lax.ppermute(x, axis, SWAP)  11.2 us
    ppermute x19, starting transfers between devices, other(): return lax.ppermute(x, axis, SWAP)  9.85 us
    ppermute x7, waiting for transfers between devices, across(): lax.ppermute(x, 'z', [(i, i ^ away) for i in range(lax.axis_size('z'))])  7.8 us
    pallas_call x1, Pallas kernels, prepare(): pl.pallas_call(functools.partial(prepare_kernel, tok_rows=tok_rows), out_...  3.71 us
    pallas_call x1, Pallas kernels, partial_rows(): pl.pallas_call(functools.partial(partial_kernel, parts=parts, rank=rank),...  2.97 us
  transfers between devices with their start and end apart: 26, of which 9 were waited for; matrix products, arithmetic and copies ran while one was open for 1% of the time, Pallas kernels for 8%

profile of v4, /device:TPU:0, one launch (start us, length us, event | category | flops | bytes accessed | tf_op | source)
XLA Modules:
  0.0 48.5 jit_solution(11589426436593538321)
XLA Ops:
  0.0 4.0 %collective-permute-start = (bf16[8,8192]{1,0:T(8,128)(2,1)}, bf16[8,8192]{1,0:T(8,128)(2,1)S(1)}, u32[]{:S(2)}, u32[]{:S(2)}) collective-permute-start(bf16[8,8192]{1,0:T(8,128)(2,1)} %x_hbm.1), channel_id=1, source_target_pairs={{0,8},{4,12},{8,0},{12,4},{1,9},{5,13},{9,1},{13,5},{2,10},{6,14},... | collective-permute-start | bytes 393224 | tf_op jit(solution)/shard_map/ppermute | solution.py:26
  4.0 1.6 %collective-permute-start.8 = (bf16[8,8192]{1,0:T(8,128)(2,1)}, bf16[8,8192]{1,0:T(8,128)(2,1)S(1)}, u32[]{:S(2)}, u32[]{:S(2)}) collective-permute-start(bf16[8,8192]{1,0:T(8,128)(2,1)} %x_hbm.1), channel_id=1, source_target_pairs={{0,4},{4,0},{8,12},{12,8},{1,5},{5,1},{9,13},{13,9},{2,6},{6,2},{1... | collective-permute-start | bytes 393224 | tf_op jit(solution)/shard_map/ppermute | solution.py:26
  5.6 1.5 %collective-permute-start.12 = (bf16[8,8192]{1,0:T(8,128)(2,1)}, bf16[8,8192]{1,0:T(8,128)(2,1)S(1)}, u32[]{:S(2)}, u32[]{:S(2)}) collective-permute-start(bf16[8,8192]{1,0:T(8,128)(2,1)} %x_hbm.1), channel_id=1, source_target_pairs={{0,2},{2,0},{1,3},{3,1},{4,6},{6,4},{5,7},{7,5},{8,10},{10,8},{9,1... | collective-permute-start | bytes 393224 | tf_op jit(solution)/shard_map/ppermute | solution.py:22
  7.1 3.7 %prepare.1 = (s32[128,1]{1,0:T(8,128)S(1)}, bf16[128,8192]{1,0:T(8,128)(2,1)S(1)}, bf16[128,8192]{1,0:T(8,128)(2,1)S(1)}, bf16[8,8192]{1,0:T(8,128)(2,1)S(1)}) custom-call(s32[64]{0:T(128)} %home_hbm.1, s32[64]{0:T(128)} %adapter_hbm.1, s32[4,16]{1,0:T(4,128)} %bitcast.1, bf16[4,64,8192]{2,1,0:T(8,128)(2,1)} %a_hbm.1, bf16[4,64,8192]{2,1,0:T(8,128)(2,1)} %b_hbm.1, ...), custom_call_target="tpu_custom_call" | custom-call | bytes 4194304 | tf_op jit(solution)/shard_map/prepare/pallas_call | solution.py:93
  10.9 1.4 %collective-permute-start.2 = (bf16[8,8192]{1,0:T(8,128)(2,1)S(1)}, bf16[8,8192]{1,0:T(8,128)(2,1)S(1)}, u32[]{:S(2)}, u32[]{:S(2)}) collective-permute-start(bf16[8,8192]{1,0:T(8,128)(2,1)S(1)} %collective-permute-done.refs_4_), channel_id=1, source_target_pairs={{0,2},{2,0},{1,3},{3,1},{4,6},{6,4},{5,7},{7,5},{8,10},{10,8},{9,1... | collective-permute-start | bytes 393224 | tf_op jit(solution)/shard_map/ppermute | solution.py:22
  12.2 0.7 %collective-permute-start.9 = (bf16[8,8192]{1,0:T(8,128)(2,1)S(1)}, bf16[8,8192]{1,0:T(8,128)(2,1)S(1)}, u32[]{:S(2)}, u32[]{:S(2)}) collective-permute-start(bf16[8,8192]{1,0:T(8,128)(2,1)S(1)} %collective-permute-done.8.refs_8_), channel_id=1, source_target_pairs={{0,2},{2,0},{1,3},{3,1},{4,6},{6,4},{5,7},{7,5},{8,10},{10,8},{9,1... | collective-permute-start | bytes 393224 | tf_op jit(solution)/shard_map/ppermute | solution.py:22
  13.0 0.2 collective-permute-start.14
  13.2 0.9 %collective-permute-start.1 = (bf16[8,8192]{1,0:T(8,128)(2,1)S(1)}, bf16[8,8192]{1,0:T(8,128)(2,1)S(1)}, u32[]{:S(2)}, u32[]{:S(2)}) collective-permute-start(bf16[8,8192]{1,0:T(8,128)(2,1)S(1)} %collective-permute-done.refs_4_), channel_id=1, source_target_pairs={{0,4},{4,0},{8,12},{12,8},{1,5},{5,1},{9,13},{13,9},{2,6},{6,2},{1... | collective-permute-start | bytes 393224 | tf_op jit(solution)/shard_map/ppermute | solution.py:26
  14.1 3.2 %collective-permute-done.2.refs_5_ = bf16[8,8192]{1,0:T(8,128)(2,1)S(1)} collective-permute-done((bf16[8,8192]{1,0:T(8,128)(2,1)S(1)}, bf16[8,8192]{1,0:T(8,128)(2,1)S(1)}, u32[]{:S(2)}, u32[]{:S(2)}) %collective-permute-start.2) | collective-permute-done | bytes 131104 | tf_op jit(solution)/shard_map/ppermute | solution.py:22
  17.3 0.4 collective-permute-start.3
  17.7 1.6 %collective-permute-done.9.refs_9_ = bf16[8,8192]{1,0:T(8,128)(2,1)S(1)} collective-permute-done((bf16[8,8192]{1,0:T(8,128)(2,1)S(1)}, bf16[8,8192]{1,0:T(8,128)(2,1)S(1)}, u32[]{:S(2)}, u32[]{:S(2)}) %collective-permute-start.9) | collective-permute-done | bytes 131104 | tf_op jit(solution)/shard_map/ppermute | solution.py:22
  19.4 0.5 %collective-permute-start.11 = (bf16[8,8192]{1,0:T(8,128)(2,1)S(1)}, bf16[8,8192]{1,0:T(8,128)(2,1)S(1)}, u32[]{:S(2)}, u32[]{:S(2)}) collective-permute-start(bf16[8,8192]{1,0:T(8,128)(2,1)S(1)} %collective-permute-done.9.refs_9_), channel_id=1, source_target_pairs={{0,1},{1,0},{2,3},{3,2},{4,5},{5,4},{6,7},{7,6},{8,9},{9,8},{10,11... | collective-permute-start | bytes 393224 | tf_op jit(solution)/shard_map/ppermute | solution.py:22
  20.0 2.3 %collective-permute-done.3.refs_1_ = bf16[8,8192]{1,0:T(8,128)(2,1)S(1)} collective-permute-done((bf16[8,8192]{1,0:T(8,128)(2,1)S(1)}, bf16[8,8192]{1,0:T(8,128)(2,1)S(1)}, u32[]{:S(2)}, u32[]{:S(2)}) %collective-permute-start.3) | collective-permute-done | bytes 131104 | tf_op jit(solution)/shard_map/ppermute | solution.py:26
  22.3 1.3 %collective-permute-done.5.refs_3_ = bf16[8,8192]{1,0:T(8,128)(2,1)S(1)} collective-permute-done((bf16[8,8192]{1,0:T(8,128)(2,1)S(1)}, bf16[8,8192]{1,0:T(8,128)(2,1)S(1)}, u32[]{:S(2)}, u32[]{:S(2)}) %collective-permute-start.5) | collective-permute-done | bytes 131104 | tf_op jit(solution)/shard_map/ppermute | solution.py:22
  23.6 3.0 %partial_rows.1 = (f32[16,8192]{1,0:T(8,128)S(1)}, bf16[16,8192]{1,0:T(8,128)(2,1)S(1)}, f32[16,8192]{1,0:T(8,128)S(1)}, bf16[16,8192]{1,0:T(8,128)(2,1)S(1)}, f...) custom-call(s32[128,1]{1,0:T(8,128)S(1)} %get-tuple-element.19.which, ...), custom_call_target="tpu_custom_call" | custom-call | flops 1610612736 | bytes 16777216 | tf_op jit(solution)/shard_map/partial_rows/pallas_call | solution.py:148
  26.6 0.2 collective-permute-start.16
  26.8 0.4 collective-permute-start.15
  27.1 0.2 collective-permute-start.19
  27.3 0.4 collective-permute-start.23
  27.7 0.5 %collective-permute-done.16 = bf16[16,8192]{1,0:T(8,128)(2,1)S(1)} collective-permute-done((bf16[16,8192]{1,0:T(8,128)(2,1)S(1)}, bf16[16,8192]{1,0:T(8,128)(2,1)S(1)}, u32[]{:S(2)}, u32[]{:S(2)}) %collective-permute-start.16) | collective-permute-done | bytes 262176 | tf_op jit(solution)/shard_map/ppermute | solution.py:22
  28.2 1.1 %collective-permute-start.17 = (bf16[8,8192]{1,0:T(8,128)(2,1)S(1)}, bf16[8,8192]{1,0:T(8,128)(2,1)S(1)}, u32[]{:S(2)}, u32[]{:S(2)}) collective-permute-start(bf16[8,8192]{1,0:T(8,128)(2,1)S(1)} %add_convert_fusion.6), channel_id=1, source_target_pairs={{0,2},{2,0},{1,3},{3,1},{4,6},{6,4},{5,7},{7,5},{8,10},{10,8},{9,1... | collective-permute-start | bytes 393224 | tf_op jit(solution)/shard_map/ppermute | solution.py:22
  29.4 1.0 %collective-permute-start.20 = (bf16[8,8192]{1,0:T(8,128)(2,1)S(1)}, bf16[8,8192]{1,0:T(8,128)(2,1)S(1)}, u32[]{:S(2)}, u32[]{:S(2)}) collective-permute-start(bf16[8,8192]{1,0:T(8,128)(2,1)S(1)} %add_convert_fusion.5), channel_id=1, source_target_pairs={{0,2},{2,0},{1,3},{3,1},{4,6},{6,4},{5,7},{7,5},{8,10},{10,8},{9,1... | collective-permute-start | bytes 393224 | tf_op jit(solution)/shard_map/ppermute | solution.py:22
  30.4 1.1 %collective-permute-start.24 = (bf16[8,8192]{1,0:T(8,128)(2,1)S(1)}, bf16[8,8192]{1,0:T(8,128)(2,1)S(1)}, u32[]{:S(2)}, u32[]{:S(2)}) collective-permute-start(bf16[8,8192]{1,0:T(8,128)(2,1)S(1)} %add_convert_fusion.2), channel_id=1, source_target_pairs={{0,2},{2,0},{1,3},{3,1},{4,6},{6,4},{5,7},{7,5},{8,10},{10,8},{9,1... | collective-permute-start | bytes 393224 | tf_op jit(solution)/shard_map/ppermute | solution.py:22
  31.6 3.0 %collective-permute-done.17 = bf16[8,8192]{1,0:T(8,128)(2,1)S(1)} collective-permute-done((bf16[8,8192]{1,0:T(8,128)(2,1)S(1)}, bf16[8,8192]{1,0:T(8,128)(2,1)S(1)}, u32[]{:S(2)}, u32[]{:S(2)}) %collective-permute-start.17) | collective-permute-done | bytes 131104 | tf_op jit(solution)/shard_map/ppermute | solution.py:22
  34.6 1.1 %collective-permute-start.18 = (bf16[8,8192]{1,0:T(8,128)(2,1)S(1)}, bf16[8,8192]{1,0:T(8,128)(2,1)S(1)}, u32[]{:S(2)}, u32[]{:S(2)}) collective-permute-start(bf16[8,8192]{1,0:T(8,128)(2,1)S(1)} %add_convert_fusion.7), channel_id=1, source_target_pairs={{0,2},{2,0},{1,3},{3,1},{4,6},{6,4},{5,7},{7,5},{8,10},{10,8},{9,1... | collective-permute-start | bytes 393224 | tf_op jit(solution)/shard_map/ppermute | solution.py:22
  35.7 2.2 %collective-permute-start.22 = (bf16[8,8192]{1,0:T(8,128)(2,1)S(1)}, bf16[8,8192]{1,0:T(8,128)(2,1)S(1)}, u32[]{:S(2)}, u32[]{:S(2)}) collective-permute-start(bf16[8,8192]{1,0:T(8,128)(2,1)S(1)} %add_convert_fusion.3), channel_id=1, source_target_pairs={{0,8},{4,12},{8,0},{12,4},{1,9},{5,13},{9,1},{13,5},{2,10},{6,14},... | collective-permute-start | bytes 393224 | tf_op jit(solution)/shard_map/ppermute | solution.py:26
  38.0 2.5 %collective-permute-start.21 = (bf16[8,8192]{1,0:T(8,128)(2,1)S(1)}, bf16[8,8192]{1,0:T(8,128)(2,1)S(1)}, u32[]{:S(2)}, u32[]{:S(2)}) collective-permute-start(bf16[8,8192]{1,0:T(8,128)(2,1)S(1)} %add_convert_fusion.4), channel_id=1, source_target_pairs={{0,12},{4,8},{8,4},{12,0},{1,13},{5,9},{9,5},{13,1},{2,14},{6,10},... | collective-permute-start | bytes 393224 | tf_op jit(solution)/shard_map/ppermute | solution.py:26
  40.6 0.2 collective-permute-start.25
  40.8 1.5 %collective-permute-done.18 = bf16[8,8192]{1,0:T(8,128)(2,1)S(1)} collective-permute-done((bf16[8,8192]{1,0:T(8,128)(2,1)S(1)}, bf16[8,8192]{1,0:T(8,128)(2,1)S(1)}, u32[]{:S(2)}, u32[]{:S(2)}) %collective-permute-start.18) | collective-permute-done | bytes 131104 | tf_op jit(solution)/shard_map/ppermute | solution.py:22
  42.3 5.1 %collective-permute-done.22 = bf16[8,8192]{1,0:T(8,128)(2,1)S(1)} collective-permute-done((bf16[8,8192]{1,0:T(8,128)(2,1)S(1)}, bf16[8,8192]{1,0:T(8,128)(2,1)S(1)}, u32[]{:S(2)}, u32[]{:S(2)}) %collective-permute-start.22) | collective-permute-done | bytes 131104 | tf_op jit(solution)/shard_map/ppermute | solution.py:26
  47.3 0.4 collective-permute-done.25
  47.8 0.7 %add_convert_fusion = bf16[8,8192]{1,0:T(8,128)(2,1)} fusion(bf16[8,8192]{1,0:T(8,128)(2,1)S(1)} %collective-permute-done.25, bf16[8,8192]{1,0:T(8,128)(2,1)S(1)} %collective-permute-done.22, bf16[8,8192]{1,0:T(8,128)(2,1)S(1)} %collective-permute-done.21, bf16[8,8192]{1,0:T(8,128)(2,1)S(1)} %collective-permute-done.18, f32[16,8192]{1,0:T(8,128)S(1)} %get-tuple-element.24, ...), kind=kLoop, calls=%fused_computation | loop fusion | flops 720896 | bytes 1048576 | tf_op jit(solution)/shard_map/convert_element_type | solution.py:199
  (32 shorter events, 0.4 us)
Async XLA Ops:
  0.0 10.9 %collective-permute-start = (bf16[8,8192]{1,0:T(8,128)(2,1)}, bf16[8,8192]{1,0:T(8,128)(2,1)S(1)}, u32[]{:S(2)}, u32[]{:S(2)}) collective-permute-start(bf16[8,8192]{1,0:T(8,128)(2,1)} %x_hbm.1), channel_id=1, source_target_pairs={{0,8},{4,12},{8,0},{12,4},{1,9},{5,13},{9,1},{13,5},{2,10},{6,14},... | collective-permute-start | bytes 393224 | tf_op jit(solution)/shard_map/ppermute | solution.py:26
  4.0 8.2 %collective-permute-start.8 = (bf16[8,8192]{1,0:T(8,128)(2,1)}, bf16[8,8192]{1,0:T(8,128)(2,1)S(1)}, u32[]{:S(2)}, u32[]{:S(2)}) collective-permute-start(bf16[8,8192]{1,0:T(8,128)(2,1)} %x_hbm.1), channel_id=1, source_target_pairs={{0,4},{4,0},{8,12},{12,8},{1,5},{5,1},{9,13},{13,9},{2,6},{6,2},{1... | collective-permute-start | bytes 393224 | tf_op jit(solution)/shard_map/ppermute | solution.py:26
  5.6 7.6 %collective-permute-start.13 = (bf16[8,8192]{1,0:T(8,128)(2,1)}, bf16[8,8192]{1,0:T(8,128)(2,1)S(1)}, u32[]{:S(2)}, u32[]{:S(2)}) collective-permute-start(bf16[8,8192]{1,0:T(8,128)(2,1)} %x_hbm.1), channel_id=1, source_target_pairs={{0,1},{1,0},{2,3},{3,2},{4,5},{5,4},{6,7},{7,6},{8,9},{9,8},{10,11... | collective-permute-start | bytes 393224 | tf_op jit(solution)/shard_map/ppermute | solution.py:22
  5.6 7.4 %collective-permute-start.12 = (bf16[8,8192]{1,0:T(8,128)(2,1)}, bf16[8,8192]{1,0:T(8,128)(2,1)S(1)}, u32[]{:S(2)}, u32[]{:S(2)}) collective-permute-start(bf16[8,8192]{1,0:T(8,128)(2,1)} %x_hbm.1), channel_id=1, source_target_pairs={{0,2},{2,0},{1,3},{3,1},{4,6},{6,4},{5,7},{7,5},{8,10},{10,8},{9,1... | collective-permute-start | bytes 393224 | tf_op jit(solution)/shard_map/ppermute | solution.py:22
  7.1 16.4 %copy-start = (bf16[512,8192]{1,0:T(8,128)(2,1)S(1)}, bf16[512,8192]{1,0:T(8,128)(2,1)}, u32[]{:S(2)}) copy-start(bf16[512,8192]{1,0:T(8,128)(2,1)} %w_ref.1) | copy-start | bytes 25165828
  10.9 6.4 %collective-permute-start.2 = (bf16[8,8192]{1,0:T(8,128)(2,1)S(1)}, bf16[8,8192]{1,0:T(8,128)(2,1)S(1)}, u32[]{:S(2)}, u32[]{:S(2)}) collective-permute-start(bf16[8,8192]{1,0:T(8,128)(2,1)S(1)} %collective-permute-done.refs_4_), channel_id=1, source_target_pairs={{0,2},{2,0},{1,3},{3,1},{4,6},{6,4},{5,7},{7,5},{8,10},{10,8},{9,1... | collective-permute-start | bytes 393224 | tf_op jit(solution)/shard_map/ppermute | solution.py:22
  12.2 5.5 %collective-permute-start.10 = (bf16[8,8192]{1,0:T(8,128)(2,1)S(1)}, bf16[8,8192]{1,0:T(8,128)(2,1)S(1)}, u32[]{:S(2)}, u32[]{:S(2)}) collective-permute-start(bf16[8,8192]{1,0:T(8,128)(2,1)S(1)} %collective-permute-done.8.refs_8_), channel_id=1, source_target_pairs={{0,1},{1,0},{2,3},{3,2},{4,5},{5,4},{6,7},{7,6},{8,9},{9,8},{10,11... | collective-permute-start | bytes 393224 | tf_op jit(solution)/shard_map/ppermute | solution.py:22
  12.2 7.1 %collective-permute-start.9 = (bf16[8,8192]{1,0:T(8,128)(2,1)S(1)}, bf16[8,8192]{1,0:T(8,128)(2,1)S(1)}, u32[]{:S(2)}, u32[]{:S(2)}) collective-permute-start(bf16[8,8192]{1,0:T(8,128)(2,1)S(1)} %collective-permute-done.8.refs_8_), channel_id=1, source_target_pairs={{0,2},{2,0},{1,3},{3,1},{4,6},{6,4},{5,7},{7,5},{8,10},{10,8},{9,1... | collective-permute-start | bytes 393224 | tf_op jit(solution)/shard_map/ppermute | solution.py:22
  13.0 6.4 %collective-permute-start.14 = (bf16[8,8192]{1,0:T(8,128)(2,1)S(1)}, bf16[8,8192]{1,0:T(8,128)(2,1)S(1)}, u32[]{:S(2)}, u32[]{:S(2)}) collective-permute-start(bf16[8,8192]{1,0:T(8,128)(2,1)S(1)} %collective-permute-done.12.refs_13_), channel_id=1, source_target_pairs={{0,1},{1,0},{2,3},{3,2},{4,5},{5,4},{6,7},{7,6},{8,9},{9,8},{10,11... | collective-permute-start | bytes 393224 | tf_op jit(solution)/shard_map/ppermute | solution.py:22
  13.2 6.7 %collective-permute-start.1 = (bf16[8,8192]{1,0:T(8,128)(2,1)S(1)}, bf16[8,8192]{1,0:T(8,128)(2,1)S(1)}, u32[]{:S(2)}, u32[]{:S(2)}) collective-permute-start(bf16[8,8192]{1,0:T(8,128)(2,1)S(1)} %collective-permute-done.refs_4_), channel_id=1, source_target_pairs={{0,4},{4,0},{8,12},{12,8},{1,5},{5,1},{9,13},{13,9},{2,6},{6,2},{1... | collective-permute-start | bytes 393224 | tf_op jit(solution)/shard_map/ppermute | solution.py:26
  17.3 5.0 %collective-permute-start.3 = (bf16[8,8192]{1,0:T(8,128)(2,1)S(1)}, bf16[8,8192]{1,0:T(8,128)(2,1)S(1)}, u32[]{:S(2)}, u32[]{:S(2)}) collective-permute-start(bf16[8,8192]{1,0:T(8,128)(2,1)S(1)} %collective-permute-done.2.refs_5_), channel_id=1, source_target_pairs={{0,4},{4,0},{8,12},{12,8},{1,5},{5,1},{9,13},{13,9},{2,6},{6,2},{1... | collective-permute-start | bytes 393224 | tf_op jit(solution)/shard_map/ppermute | solution.py:26
  17.7 4.5 %collective-permute-start.6 = (bf16[8,8192]{1,0:T(8,128)(2,1)S(1)}, bf16[8,8192]{1,0:T(8,128)(2,1)S(1)}, u32[]{:S(2)}, u32[]{:S(2)}) collective-permute-start(bf16[8,8192]{1,0:T(8,128)(2,1)S(1)} %collective-permute-done.refs_4_), channel_id=1, source_target_pairs={{0,1},{1,0},{2,3},{3,2},{4,5},{5,4},{6,7},{7,6},{8,9},{9,8},{10,11... | collective-permute-start | bytes 393224 | tf_op jit(solution)/shard_map/ppermute | solution.py:22
  19.4 2.9 %collective-permute-start.7 = (bf16[8,8192]{1,0:T(8,128)(2,1)S(1)}, bf16[8,8192]{1,0:T(8,128)(2,1)S(1)}, u32[]{:S(2)}, u32[]{:S(2)}) collective-permute-start(bf16[8,8192]{1,0:T(8,128)(2,1)S(1)} %collective-permute-done.2.refs_5_), channel_id=1, source_target_pairs={{0,1},{1,0},{2,3},{3,2},{4,5},{5,4},{6,7},{7,6},{8,9},{9,8},{10,11... | collective-permute-start | bytes 393224 | tf_op jit(solution)/shard_map/ppermute | solution.py:22
  19.4 2.9 %collective-permute-start.11 = (bf16[8,8192]{1,0:T(8,128)(2,1)S(1)}, bf16[8,8192]{1,0:T(8,128)(2,1)S(1)}, u32[]{:S(2)}, u32[]{:S(2)}) collective-permute-start(bf16[8,8192]{1,0:T(8,128)(2,1)S(1)} %collective-permute-done.9.refs_9_), channel_id=1, source_target_pairs={{0,1},{1,0},{2,3},{3,2},{4,5},{5,4},{6,7},{7,6},{8,9},{9,8},{10,11... | collective-permute-start | bytes 393224 | tf_op jit(solution)/shard_map/ppermute | solution.py:22
  19.9 2.4 %collective-permute-start.4 = (bf16[8,8192]{1,0:T(8,128)(2,1)S(1)}, bf16[8,8192]{1,0:T(8,128)(2,1)S(1)}, u32[]{:S(2)}, u32[]{:S(2)}) collective-permute-start(bf16[8,8192]{1,0:T(8,128)(2,1)S(1)} %collective-permute-done.1.refs_0_), channel_id=1, source_target_pairs={{0,1},{1,0},{2,3},{3,2},{4,5},{5,4},{6,7},{7,6},{8,9},{9,8},{10,11... | collective-permute-start | bytes 393224 | tf_op jit(solution)/shard_map/ppermute | solution.py:22
  22.2 1.3 %collective-permute-start.5 = (bf16[8,8192]{1,0:T(8,128)(2,1)S(1)}, bf16[8,8192]{1,0:T(8,128)(2,1)S(1)}, u32[]{:S(2)}, u32[]{:S(2)}) collective-permute-start(bf16[8,8192]{1,0:T(8,128)(2,1)S(1)} %collective-permute-done.3.refs_1_), channel_id=1, source_target_pairs={{0,1},{1,0},{2,3},{3,2},{4,5},{5,4},{6,7},{7,6},{8,9},{9,8},{10,11... | collective-permute-start | bytes 393224 | tf_op jit(solution)/shard_map/ppermute | solution.py:22
  26.6 1.6 %collective-permute-start.16 = (bf16[16,8192]{1,0:T(8,128)(2,1)S(1)}, bf16[16,8192]{1,0:T(8,128)(2,1)S(1)}, u32[]{:S(2)}, u32[]{:S(2)}) collective-permute-start(bf16[16,8192]{1,0:T(8,128)(2,1)S(1)} %get-tuple-element.27), channel_id=1, source_target_pairs={{0,1},{1,0},{2,3},{3,2},{4,5},{5,4},{6,7},{7,6},{8,9},{9,8},{10,11... | collective-permute-start | bytes 786440 | tf_op jit(solution)/shard_map/ppermute | solution.py:22
  26.8 4.8 %collective-permute-start.15 = (bf16[16,8192]{1,0:T(8,128)(2,1)S(1)}, bf16[16,8192]{1,0:T(8,128)(2,1)S(1)}, u32[]{:S(2)}, u32[]{:S(2)}) collective-permute-start(bf16[16,8192]{1,0:T(8,128)(2,1)S(1)} %get-tuple-element.25), channel_id=1, source_target_pairs={{0,1},{1,0},{2,3},{3,2},{4,5},{5,4},{6,7},{7,6},{8,9},{9,8},{10,11... | collective-permute-start | bytes 786440 | tf_op jit(solution)/shard_map/ppermute | solution.py:22
  27.1 2.2 %collective-permute-start.19 = (bf16[16,8192]{1,0:T(8,128)(2,1)S(1)}, bf16[16,8192]{1,0:T(8,128)(2,1)S(1)}, u32[]{:S(2)}, u32[]{:S(2)}) collective-permute-start(bf16[16,8192]{1,0:T(8,128)(2,1)S(1)} %get-tuple-element.30), channel_id=1, source_target_pairs={{0,1},{1,0},{2,3},{3,2},{4,5},{5,4},{6,7},{7,6},{8,9},{9,8},{10,11... | collective-permute-start | bytes 786440 | tf_op jit(solution)/shard_map/ppermute | solution.py:22
  27.3 3.1 %collective-permute-start.23 = (bf16[16,8192]{1,0:T(8,128)(2,1)S(1)}, bf16[16,8192]{1,0:T(8,128)(2,1)S(1)}, u32[]{:S(2)}, u32[]{:S(2)}) collective-permute-start(bf16[16,8192]{1,0:T(8,128)(2,1)S(1)} %get-tuple-element.32), channel_id=1, source_target_pairs={{0,1},{1,0},{2,3},{3,2},{4,5},{5,4},{6,7},{7,6},{8,9},{9,8},{10,11... | collective-permute-start | bytes 786440 | tf_op jit(solution)/shard_map/ppermute | solution.py:22
  28.2 6.4 %collective-permute-start.17 = (bf16[8,8192]{1,0:T(8,128)(2,1)S(1)}, bf16[8,8192]{1,0:T(8,128)(2,1)S(1)}, u32[]{:S(2)}, u32[]{:S(2)}) collective-permute-start(bf16[8,8192]{1,0:T(8,128)(2,1)S(1)} %add_convert_fusion.6), channel_id=1, source_target_pairs={{0,2},{2,0},{1,3},{3,1},{4,6},{6,4},{5,7},{7,5},{8,10},{10,8},{9,1... | collective-permute-start | bytes 393224 | tf_op jit(solution)/shard_map/ppermute | solution.py:22
  29.4 8.6 %collective-permute-start.20 = (bf16[8,8192]{1,0:T(8,128)(2,1)S(1)}, bf16[8,8192]{1,0:T(8,128)(2,1)S(1)}, u32[]{:S(2)}, u32[]{:S(2)}) collective-permute-start(bf16[8,8192]{1,0:T(8,128)(2,1)S(1)} %add_convert_fusion.5), channel_id=1, source_target_pairs={{0,2},{2,0},{1,3},{3,1},{4,6},{6,4},{5,7},{7,5},{8,10},{10,8},{9,1... | collective-permute-start | bytes 393224 | tf_op jit(solution)/shard_map/ppermute | solution.py:22
  30.4 10.1 %collective-permute-start.24 = (bf16[8,8192]{1,0:T(8,128)(2,1)S(1)}, bf16[8,8192]{1,0:T(8,128)(2,1)S(1)}, u32[]{:S(2)}, u32[]{:S(2)}) collective-permute-start(bf16[8,8192]{1,0:T(8,128)(2,1)S(1)} %add_convert_fusion.2), channel_id=1, source_target_pairs={{0,2},{2,0},{1,3},{3,1},{4,6},{6,4},{5,7},{7,5},{8,10},{10,8},{9,1... | collective-permute-start | bytes 393224 | tf_op jit(solution)/shard_map/ppermute | solution.py:22
  34.6 7.6 %collective-permute-start.18 = (bf16[8,8192]{1,0:T(8,128)(2,1)S(1)}, bf16[8,8192]{1,0:T(8,128)(2,1)S(1)}, u32[]{:S(2)}, u32[]{:S(2)}) collective-permute-start(bf16[8,8192]{1,0:T(8,128)(2,1)S(1)} %add_convert_fusion.7), channel_id=1, source_target_pairs={{0,2},{2,0},{1,3},{3,1},{4,6},{6,4},{5,7},{7,5},{8,10},{10,8},{9,1... | collective-permute-start | bytes 393224 | tf_op jit(solution)/shard_map/ppermute | solution.py:22
  35.7 11.6 %collective-permute-start.22 = (bf16[8,8192]{1,0:T(8,128)(2,1)S(1)}, bf16[8,8192]{1,0:T(8,128)(2,1)S(1)}, u32[]{:S(2)}, u32[]{:S(2)}) collective-permute-start(bf16[8,8192]{1,0:T(8,128)(2,1)S(1)} %add_convert_fusion.3), channel_id=1, source_target_pairs={{0,8},{4,12},{8,0},{12,4},{1,9},{5,13},{9,1},{13,5},{2,10},{6,14},... | collective-permute-start | bytes 393224 | tf_op jit(solution)/shard_map/ppermute | solution.py:26
  38.0 9.3 %collective-permute-start.21 = (bf16[8,8192]{1,0:T(8,128)(2,1)S(1)}, bf16[8,8192]{1,0:T(8,128)(2,1)S(1)}, u32[]{:S(2)}, u32[]{:S(2)}) collective-permute-start(bf16[8,8192]{1,0:T(8,128)(2,1)S(1)} %add_convert_fusion.4), channel_id=1, source_target_pairs={{0,12},{4,8},{8,4},{12,0},{1,13},{5,9},{9,5},{13,1},{2,14},{6,10},... | collective-permute-start | bytes 393224 | tf_op jit(solution)/shard_map/ppermute | solution.py:26
  40.6 7.2 %collective-permute-start.25 = (bf16[8,8192]{1,0:T(8,128)(2,1)S(1)}, bf16[8,8192]{1,0:T(8,128)(2,1)S(1)}, u32[]{:S(2)}, u32[]{:S(2)}) collective-permute-start(bf16[8,8192]{1,0:T(8,128)(2,1)S(1)} %add_convert_fusion.1), channel_id=1, source_target_pairs={{0,4},{4,0},{8,12},{12,8},{1,5},{5,1},{9,13},{13,9},{2,6},{6,2},{1... | collective-permute-start | bytes 393224 | tf_op jit(solution)/shard_map/ppermute | solution.py:26

commit v5 on v4

--- a/solution.py
+++ b/solution.py
@@ -112,7 +112,7 @@
     xs, outs, x_ref = refs[: 4 * len(parts)], refs[4 * len(parts) : -1], refs[-1]
     tok_rows, width = xs[0].shape
     depth = w_ref.shape[0]
-    step = 2048
+    step = 4096
     me = (lax.axis_index("z") * 2 + lax.axis_index("y")) * 2 + lax.axis_index("core")
 
     inputs = None

time: 48.7 us -> 48.3 us (level)
  no operation moved by 1% of the time
where the time goes in v5:
time: 48.3 us; the launch traced here: 48.2 us
  starting transfers between devices  21.7 us (45%)
  waiting for transfers between devices  19 us (39%)
  Pallas kernels  6.38 us (13%)
  other arithmetic  1.01 us (2%)
    ppermute x7, starting transfers between devices, across(): lax.ppermute(x, 'z', [(i, i ^ away) for i in range(lax.axis_size('z'))])  11.9 us
    ppermute x19, waiting for transfers between devices, other(): return lax.ppermute(x, axis, SWAP)  11.2 us
    ppermute x19, starting transfers between devices, other(): return lax.ppermute(x, axis, SWAP)  9.84 us
    ppermute x7, waiting for transfers between devices, across(): lax.ppermute(x, 'z', [(i, i ^ away) for i in range(lax.axis_size('z'))])  7.79 us
    pallas_call x1, Pallas kernels, prepare(): pl.pallas_call(functools.partial(prepare_kernel, tok_rows=tok_rows), out_...  3.71 us
    pallas_call x1, Pallas kernels, partial_rows(): pl.pallas_call(functools.partial(partial_kernel, parts=parts, rank=rank),...  2.67 us
  transfers between devices with their start and end apart: 26, of which 9 were waited for; matrix products, arithmetic and copies ran while one was open for 1% of the time, Pallas kernels for 8%

profile of v5, /device:TPU:0, one launch (start us, length us, event | category | flops | bytes accessed | tf_op | source)
XLA Modules:
  0.0 48.2 jit_solution(7075793786622085814)
XLA Ops:
  0.0 4.0 %collective-permute-start = (bf16[8,8192]{1,0:T(8,128)(2,1)}, bf16[8,8192]{1,0:T(8,128)(2,1)S(1)}, u32[]{:S(2)}, u32[]{:S(2)}) collective-permute-start(bf16[8,8192]{1,0:T(8,128)(2,1)} %x_hbm.1), channel_id=1, source_target_pairs={{0,8},{4,12},{8,0},{12,4},{1,9},{5,13},{9,1},{13,5},{2,10},{6,14},... | collective-permute-start | bytes 393224 | tf_op jit(solution)/shard_map/ppermute | solution.py:26
  4.0 1.6 %collective-permute-start.8 = (bf16[8,8192]{1,0:T(8,128)(2,1)}, bf16[8,8192]{1,0:T(8,128)(2,1)S(1)}, u32[]{:S(2)}, u32[]{:S(2)}) collective-permute-start(bf16[8,8192]{1,0:T(8,128)(2,1)} %x_hbm.1), channel_id=1, source_target_pairs={{0,4},{4,0},{8,12},{12,8},{1,5},{5,1},{9,13},{13,9},{2,6},{6,2},{1... | collective-permute-start | bytes 393224 | tf_op jit(solution)/shard_map/ppermute | solution.py:26
  5.6 1.5 %collective-permute-start.12 = (bf16[8,8192]{1,0:T(8,128)(2,1)}, bf16[8,8192]{1,0:T(8,128)(2,1)S(1)}, u32[]{:S(2)}, u32[]{:S(2)}) collective-permute-start(bf16[8,8192]{1,0:T(8,128)(2,1)} %x_hbm.1), channel_id=1, source_target_pairs={{0,2},{2,0},{1,3},{3,1},{4,6},{6,4},{5,7},{7,5},{8,10},{10,8},{9,1... | collective-permute-start | bytes 393224 | tf_op jit(solution)/shard_map/ppermute | solution.py:22
  7.1 3.7 %prepare.1 = (s32[128,1]{1,0:T(8,128)S(1)}, bf16[128,8192]{1,0:T(8,128)(2,1)S(1)}, bf16[128,8192]{1,0:T(8,128)(2,1)S(1)}, bf16[8,8192]{1,0:T(8,128)(2,1)S(1)}) custom-call(s32[64]{0:T(128)} %home_hbm.1, s32[64]{0:T(128)} %adapter_hbm.1, s32[4,16]{1,0:T(4,128)} %bitcast.1, bf16[4,64,8192]{2,1,0:T(8,128)(2,1)} %a_hbm.1, bf16[4,64,8192]{2,1,0:T(8,128)(2,1)} %b_hbm.1, ...), custom_call_target="tpu_custom_call" | custom-call | bytes 4194304 | tf_op jit(solution)/shard_map/prepare/pallas_call | solution.py:93
  10.9 1.4 %collective-permute-start.2 = (bf16[8,8192]{1,0:T(8,128)(2,1)S(1)}, bf16[8,8192]{1,0:T(8,128)(2,1)S(1)}, u32[]{:S(2)}, u32[]{:S(2)}) collective-permute-start(bf16[8,8192]{1,0:T(8,128)(2,1)S(1)} %collective-permute-done.refs_4_), channel_id=1, source_target_pairs={{0,2},{2,0},{1,3},{3,1},{4,6},{6,4},{5,7},{7,5},{8,10},{10,8},{9,1... | collective-permute-start | bytes 393224 | tf_op jit(solution)/shard_map/ppermute | solution.py:22
  12.2 0.7 %collective-permute-start.9 = (bf16[8,8192]{1,0:T(8,128)(2,1)S(1)}, bf16[8,8192]{1,0:T(8,128)(2,1)S(1)}, u32[]{:S(2)}, u32[]{:S(2)}) collective-permute-start(bf16[8,8192]{1,0:T(8,128)(2,1)S(1)} %collective-permute-done.8.refs_8_), channel_id=1, source_target_pairs={{0,2},{2,0},{1,3},{3,1},{4,6},{6,4},{5,7},{7,5},{8,10},{10,8},{9,1... | collective-permute-start | bytes 393224 | tf_op jit(solution)/shard_map/ppermute | solution.py:22
  13.0 0.2 collective-permute-start.14
  13.2 0.9 %collective-permute-start.1 = (bf16[8,8192]{1,0:T(8,128)(2,1)S(1)}, bf16[8,8192]{1,0:T(8,128)(2,1)S(1)}, u32[]{:S(2)}, u32[]{:S(2)}) collective-permute-start(bf16[8,8192]{1,0:T(8,128)(2,1)S(1)} %collective-permute-done.refs_4_), channel_id=1, source_target_pairs={{0,4},{4,0},{8,12},{12,8},{1,5},{5,1},{9,13},{13,9},{2,6},{6,2},{1... | collective-permute-start | bytes 393224 | tf_op jit(solution)/shard_map/ppermute | solution.py:26
  14.1 3.2 %collective-permute-done.2.refs_5_ = bf16[8,8192]{1,0:T(8,128)(2,1)S(1)} collective-permute-done((bf16[8,8192]{1,0:T(8,128)(2,1)S(1)}, bf16[8,8192]{1,0:T(8,128)(2,1)S(1)}, u32[]{:S(2)}, u32[]{:S(2)}) %collective-permute-start.2) | collective-permute-done | bytes 131104 | tf_op jit(solution)/shard_map/ppermute | solution.py:22
  17.3 0.4 collective-permute-start.3
  17.7 1.6 %collective-permute-done.9.refs_9_ = bf16[8,8192]{1,0:T(8,128)(2,1)S(1)} collective-permute-done((bf16[8,8192]{1,0:T(8,128)(2,1)S(1)}, bf16[8,8192]{1,0:T(8,128)(2,1)S(1)}, u32[]{:S(2)}, u32[]{:S(2)}) %collective-permute-start.9) | collective-permute-done | bytes 131104 | tf_op jit(solution)/shard_map/ppermute | solution.py:22
  19.4 0.5 %collective-permute-start.11 = (bf16[8,8192]{1,0:T(8,128)(2,1)S(1)}, bf16[8,8192]{1,0:T(8,128)(2,1)S(1)}, u32[]{:S(2)}, u32[]{:S(2)}) collective-permute-start(bf16[8,8192]{1,0:T(8,128)(2,1)S(1)} %collective-permute-done.9.refs_9_), channel_id=1, source_target_pairs={{0,1},{1,0},{2,3},{3,2},{4,5},{5,4},{6,7},{7,6},{8,9},{9,8},{10,11... | collective-permute-start | bytes 393224 | tf_op jit(solution)/shard_map/ppermute | solution.py:22
  20.0 2.3 %collective-permute-done.3.refs_1_ = bf16[8,8192]{1,0:T(8,128)(2,1)S(1)} collective-permute-done((bf16[8,8192]{1,0:T(8,128)(2,1)S(1)}, bf16[8,8192]{1,0:T(8,128)(2,1)S(1)}, u32[]{:S(2)}, u32[]{:S(2)}) %collective-permute-start.3) | collective-permute-done | bytes 131104 | tf_op jit(solution)/shard_map/ppermute | solution.py:26
  22.3 1.3 %collective-permute-done.5.refs_3_ = bf16[8,8192]{1,0:T(8,128)(2,1)S(1)} collective-permute-done((bf16[8,8192]{1,0:T(8,128)(2,1)S(1)}, bf16[8,8192]{1,0:T(8,128)(2,1)S(1)}, u32[]{:S(2)}, u32[]{:S(2)}) %collective-permute-start.5) | collective-permute-done | bytes 131104 | tf_op jit(solution)/shard_map/ppermute | solution.py:22
  23.6 2.7 %partial_rows.1 = (f32[16,8192]{1,0:T(8,128)S(1)}, bf16[16,8192]{1,0:T(8,128)(2,1)S(1)}, f32[16,8192]{1,0:T(8,128)S(1)}, bf16[16,8192]{1,0:T(8,128)(2,1)S(1)}, f...) custom-call(s32[128,1]{1,0:T(8,128)S(1)} %get-tuple-element.19.which, ...), custom_call_target="tpu_custom_call" | custom-call | flops 1610612736 | bytes 16777216 | tf_op jit(solution)/shard_map/partial_rows/pallas_call | solution.py:148
  26.3 0.2 collective-permute-start.16
  26.5 0.4 collective-permute-start.15
  26.8 0.2 collective-permute-start.19
  27.0 0.4 collective-permute-start.23
  27.3 0.5 %collective-permute-done.16 = bf16[16,8192]{1,0:T(8,128)(2,1)S(1)} collective-permute-done((bf16[16,8192]{1,0:T(8,128)(2,1)S(1)}, bf16[16,8192]{1,0:T(8,128)(2,1)S(1)}, u32[]{:S(2)}, u32[]{:S(2)}) %collective-permute-start.16) | collective-permute-done | bytes 262176 | tf_op jit(solution)/shard_map/ppermute | solution.py:22
  27.9 1.1 %collective-permute-start.17 = (bf16[8,8192]{1,0:T(8,128)(2,1)S(1)}, bf16[8,8192]{1,0:T(8,128)(2,1)S(1)}, u32[]{:S(2)}, u32[]{:S(2)}) collective-permute-start(bf16[8,8192]{1,0:T(8,128)(2,1)S(1)} %add_convert_fusion.6), channel_id=1, source_target_pairs={{0,2},{2,0},{1,3},{3,1},{4,6},{6,4},{5,7},{7,5},{8,10},{10,8},{9,1... | collective-permute-start | bytes 393224 | tf_op jit(solution)/shard_map/ppermute | solution.py:22
  29.1 1.0 %collective-permute-start.20 = (bf16[8,8192]{1,0:T(8,128)(2,1)S(1)}, bf16[8,8192]{1,0:T(8,128)(2,1)S(1)}, u32[]{:S(2)}, u32[]{:S(2)}) collective-permute-start(bf16[8,8192]{1,0:T(8,128)(2,1)S(1)} %add_convert_fusion.5), channel_id=1, source_target_pairs={{0,2},{2,0},{1,3},{3,1},{4,6},{6,4},{5,7},{7,5},{8,10},{10,8},{9,1... | collective-permute-start | bytes 393224 | tf_op jit(solution)/shard_map/ppermute | solution.py:22
  30.1 1.1 %collective-permute-start.24 = (bf16[8,8192]{1,0:T(8,128)(2,1)S(1)}, bf16[8,8192]{1,0:T(8,128)(2,1)S(1)}, u32[]{:S(2)}, u32[]{:S(2)}) collective-permute-start(bf16[8,8192]{1,0:T(8,128)(2,1)S(1)} %add_convert_fusion.2), channel_id=1, source_target_pairs={{0,2},{2,0},{1,3},{3,1},{4,6},{6,4},{5,7},{7,5},{8,10},{10,8},{9,1... | collective-permute-start | bytes 393224 | tf_op jit(solution)/shard_map/ppermute | solution.py:22
  31.3 3.0 %collective-permute-done.17 = bf16[8,8192]{1,0:T(8,128)(2,1)S(1)} collective-permute-done((bf16[8,8192]{1,0:T(8,128)(2,1)S(1)}, bf16[8,8192]{1,0:T(8,128)(2,1)S(1)}, u32[]{:S(2)}, u32[]{:S(2)}) %collective-permute-start.17) | collective-permute-done | bytes 131104 | tf_op jit(solution)/shard_map/ppermute | solution.py:22
  34.3 1.1 %collective-permute-start.18 = (bf16[8,8192]{1,0:T(8,128)(2,1)S(1)}, bf16[8,8192]{1,0:T(8,128)(2,1)S(1)}, u32[]{:S(2)}, u32[]{:S(2)}) collective-permute-start(bf16[8,8192]{1,0:T(8,128)(2,1)S(1)} %add_convert_fusion.7), channel_id=1, source_target_pairs={{0,2},{2,0},{1,3},{3,1},{4,6},{6,4},{5,7},{7,5},{8,10},{10,8},{9,1... | collective-permute-start | bytes 393224 | tf_op jit(solution)/shard_map/ppermute | solution.py:22
  35.4 2.3 %collective-permute-start.22 = (bf16[8,8192]{1,0:T(8,128)(2,1)S(1)}, bf16[8,8192]{1,0:T(8,128)(2,1)S(1)}, u32[]{:S(2)}, u32[]{:S(2)}) collective-permute-start(bf16[8,8192]{1,0:T(8,128)(2,1)S(1)} %add_convert_fusion.3), channel_id=1, source_target_pairs={{0,8},{4,12},{8,0},{12,4},{1,9},{5,13},{9,1},{13,5},{2,10},{6,14},... | collective-permute-start | bytes 393224 | tf_op jit(solution)/shard_map/ppermute | solution.py:26
  37.7 2.5 %collective-permute-start.21 = (bf16[8,8192]{1,0:T(8,128)(2,1)S(1)}, bf16[8,8192]{1,0:T(8,128)(2,1)S(1)}, u32[]{:S(2)}, u32[]{:S(2)}) collective-permute-start(bf16[8,8192]{1,0:T(8,128)(2,1)S(1)} %add_convert_fusion.4), channel_id=1, source_target_pairs={{0,12},{4,8},{8,4},{12,0},{1,13},{5,9},{9,5},{13,1},{2,14},{6,10},... | collective-permute-start | bytes 393224 | tf_op jit(solution)/shard_map/ppermute | solution.py:26
  40.3 0.2 collective-permute-start.25
  40.5 1.5 %collective-permute-done.18 = bf16[8,8192]{1,0:T(8,128)(2,1)S(1)} collective-permute-done((bf16[8,8192]{1,0:T(8,128)(2,1)S(1)}, bf16[8,8192]{1,0:T(8,128)(2,1)S(1)}, u32[]{:S(2)}, u32[]{:S(2)}) %collective-permute-start.18) | collective-permute-done | bytes 131104 | tf_op jit(solution)/shard_map/ppermute | solution.py:22
  41.9 5.1 %collective-permute-done.22 = bf16[8,8192]{1,0:T(8,128)(2,1)S(1)} collective-permute-done((bf16[8,8192]{1,0:T(8,128)(2,1)S(1)}, bf16[8,8192]{1,0:T(8,128)(2,1)S(1)}, u32[]{:S(2)}, u32[]{:S(2)}) %collective-permute-start.22) | collective-permute-done | bytes 131104 | tf_op jit(solution)/shard_map/ppermute | solution.py:26
  47.0 0.4 collective-permute-done.25
  47.5 0.7 %add_convert_fusion = bf16[8,8192]{1,0:T(8,128)(2,1)} fusion(bf16[8,8192]{1,0:T(8,128)(2,1)S(1)} %collective-permute-done.25, bf16[8,8192]{1,0:T(8,128)(2,1)S(1)} %collective-permute-done.22, bf16[8,8192]{1,0:T(8,128)(2,1)S(1)} %collective-permute-done.21, bf16[8,8192]{1,0:T(8,128)(2,1)S(1)} %collective-permute-done.18, f32[16,8192]{1,0:T(8,128)S(1)} %get-tuple-element.24, ...), kind=kLoop, calls=%fused_computation | loop fusion | flops 720896 | bytes 1048576 | tf_op jit(solution)/shard_map/convert_element_type | solution.py:199
  (32 shorter events, 0.4 us)
Async XLA Ops:
  0.0 10.9 %collective-permute-start = (bf16[8,8192]{1,0:T(8,128)(2,1)}, bf16[8,8192]{1,0:T(8,128)(2,1)S(1)}, u32[]{:S(2)}, u32[]{:S(2)}) collective-permute-start(bf16[8,8192]{1,0:T(8,128)(2,1)} %x_hbm.1), channel_id=1, source_target_pairs={{0,8},{4,12},{8,0},{12,4},{1,9},{5,13},{9,1},{13,5},{2,10},{6,14},... | collective-permute-start | bytes 393224 | tf_op jit(solution)/shard_map/ppermute | solution.py:26
  4.0 8.2 %collective-permute-start.8 = (bf16[8,8192]{1,0:T(8,128)(2,1)}, bf16[8,8192]{1,0:T(8,128)(2,1)S(1)}, u32[]{:S(2)}, u32[]{:S(2)}) collective-permute-start(bf16[8,8192]{1,0:T(8,128)(2,1)} %x_hbm.1), channel_id=1, source_target_pairs={{0,4},{4,0},{8,12},{12,8},{1,5},{5,1},{9,13},{13,9},{2,6},{6,2},{1... | collective-permute-start | bytes 393224 | tf_op jit(solution)/shard_map/ppermute | solution.py:26
  5.6 7.6 %collective-permute-start.13 = (bf16[8,8192]{1,0:T(8,128)(2,1)}, bf16[8,8192]{1,0:T(8,128)(2,1)S(1)}, u32[]{:S(2)}, u32[]{:S(2)}) collective-permute-start(bf16[8,8192]{1,0:T(8,128)(2,1)} %x_hbm.1), channel_id=1, source_target_pairs={{0,1},{1,0},{2,3},{3,2},{4,5},{5,4},{6,7},{7,6},{8,9},{9,8},{10,11... | collective-permute-start | bytes 393224 | tf_op jit(solution)/shard_map/ppermute | solution.py:22
  5.6 7.4 %collective-permute-start.12 = (bf16[8,8192]{1,0:T(8,128)(2,1)}, bf16[8,8192]{1,0:T(8,128)(2,1)S(1)}, u32[]{:S(2)}, u32[]{:S(2)}) collective-permute-start(bf16[8,8192]{1,0:T(8,128)(2,1)} %x_hbm.1), channel_id=1, source_target_pairs={{0,2},{2,0},{1,3},{3,1},{4,6},{6,4},{5,7},{7,5},{8,10},{10,8},{9,1... | collective-permute-start | bytes 393224 | tf_op jit(solution)/shard_map/ppermute | solution.py:22
  7.1 16.4 %copy-start = (bf16[512,8192]{1,0:T(8,128)(2,1)S(1)}, bf16[512,8192]{1,0:T(8,128)(2,1)}, u32[]{:S(2)}) copy-start(bf16[512,8192]{1,0:T(8,128)(2,1)} %w_ref.1) | copy-start | bytes 25165828
  10.9 6.4 %collective-permute-start.2 = (bf16[8,8192]{1,0:T(8,128)(2,1)S(1)}, bf16[8,8192]{1,0:T(8,128)(2,1)S(1)}, u32[]{:S(2)}, u32[]{:S(2)}) collective-permute-start(bf16[8,8192]{1,0:T(8,128)(2,1)S(1)} %collective-permute-done.refs_4_), channel_id=1, source_target_pairs={{0,2},{2,0},{1,3},{3,1},{4,6},{6,4},{5,7},{7,5},{8,10},{10,8},{9,1... | collective-permute-start | bytes 393224 | tf_op jit(solution)/shard_map/ppermute | solution.py:22
  12.2 5.5 %collective-permute-start.10 = (bf16[8,8192]{1,0:T(8,128)(2,1)S(1)}, bf16[8,8192]{1,0:T(8,128)(2,1)S(1)}, u32[]{:S(2)}, u32[]{:S(2)}) collective-permute-start(bf16[8,8192]{1,0:T(8,128)(2,1)S(1)} %collective-permute-done.8.refs_8_), channel_id=1, source_target_pairs={{0,1},{1,0},{2,3},{3,2},{4,5},{5,4},{6,7},{7,6},{8,9},{9,8},{10,11... | collective-permute-start | bytes 393224 | tf_op jit(solution)/shard_map/ppermute | solution.py:22
  12.2 7.1 %collective-permute-start.9 = (bf16[8,8192]{1,0:T(8,128)(2,1)S(1)}, bf16[8,8192]{1,0:T(8,128)(2,1)S(1)}, u32[]{:S(2)}, u32[]{:S(2)}) collective-permute-start(bf16[8,8192]{1,0:T(8,128)(2,1)S(1)} %collective-permute-done.8.refs_8_), channel_id=1, source_target_pairs={{0,2},{2,0},{1,3},{3,1},{4,6},{6,4},{5,7},{7,5},{8,10},{10,8},{9,1... | collective-permute-start | bytes 393224 | tf_op jit(solution)/shard_map/ppermute | solution.py:22
  13.0 6.4 %collective-permute-start.14 = (bf16[8,8192]{1,0:T(8,128)(2,1)S(1)}, bf16[8,8192]{1,0:T(8,128)(2,1)S(1)}, u32[]{:S(2)}, u32[]{:S(2)}) collective-permute-start(bf16[8,8192]{1,0:T(8,128)(2,1)S(1)} %collective-permute-done.12.refs_13_), channel_id=1, source_target_pairs={{0,1},{1,0},{2,3},{3,2},{4,5},{5,4},{6,7},{7,6},{8,9},{9,8},{10,11... | collective-permute-start | bytes 393224 | tf_op jit(solution)/shard_map/ppermute | solution.py:22
  13.2 6.7 %collective-permute-start.1 = (bf16[8,8192]{1,0:T(8,128)(2,1)S(1)}, bf16[8,8192]{1,0:T(8,128)(2,1)S(1)}, u32[]{:S(2)}, u32[]{:S(2)}) collective-permute-start(bf16[8,8192]{1,0:T(8,128)(2,1)S(1)} %collective-permute-done.refs_4_), channel_id=1, source_target_pairs={{0,4},{4,0},{8,12},{12,8},{1,5},{5,1},{9,13},{13,9},{2,6},{6,2},{1... | collective-permute-start | bytes 393224 | tf_op jit(solution)/shard_map/ppermute | solution.py:26
  17.3 5.0 %collective-permute-start.3 = (bf16[8,8192]{1,0:T(8,128)(2,1)S(1)}, bf16[8,8192]{1,0:T(8,128)(2,1)S(1)}, u32[]{:S(2)}, u32[]{:S(2)}) collective-permute-start(bf16[8,8192]{1,0:T(8,128)(2,1)S(1)} %collective-permute-done.2.refs_5_), channel_id=1, source_target_pairs={{0,4},{4,0},{8,12},{12,8},{1,5},{5,1},{9,13},{13,9},{2,6},{6,2},{1... | collective-permute-start | bytes 393224 | tf_op jit(solution)/shard_map/ppermute | solution.py:26
  17.7 4.5 %collective-permute-start.6 = (bf16[8,8192]{1,0:T(8,128)(2,1)S(1)}, bf16[8,8192]{1,0:T(8,128)(2,1)S(1)}, u32[]{:S(2)}, u32[]{:S(2)}) collective-permute-start(bf16[8,8192]{1,0:T(8,128)(2,1)S(1)} %collective-permute-done.refs_4_), channel_id=1, source_target_pairs={{0,1},{1,0},{2,3},{3,2},{4,5},{5,4},{6,7},{7,6},{8,9},{9,8},{10,11... | collective-permute-start | bytes 393224 | tf_op jit(solution)/shard_map/ppermute | solution.py:22
  19.4 2.9 %collective-permute-start.7 = (bf16[8,8192]{1,0:T(8,128)(2,1)S(1)}, bf16[8,8192]{1,0:T(8,128)(2,1)S(1)}, u32[]{:S(2)}, u32[]{:S(2)}) collective-permute-start(bf16[8,8192]{1,0:T(8,128)(2,1)S(1)} %collective-permute-done.2.refs_5_), channel_id=1, source_target_pairs={{0,1},{1,0},{2,3},{3,2},{4,5},{5,4},{6,7},{7,6},{8,9},{9,8},{10,11... | collective-permute-start | bytes 393224 | tf_op jit(solution)/shard_map/ppermute | solution.py:22
  19.4 2.9 %collective-permute-start.11 = (bf16[8,8192]{1,0:T(8,128)(2,1)S(1)}, bf16[8,8192]{1,0:T(8,128)(2,1)S(1)}, u32[]{:S(2)}, u32[]{:S(2)}) collective-permute-start(bf16[8,8192]{1,0:T(8,128)(2,1)S(1)} %collective-permute-done.9.refs_9_), channel_id=1, source_target_pairs={{0,1},{1,0},{2,3},{3,2},{4,5},{5,4},{6,7},{7,6},{8,9},{9,8},{10,11... | collective-permute-start | bytes 393224 | tf_op jit(solution)/shard_map/ppermute | solution.py:22
  19.9 2.4 %collective-permute-start.4 = (bf16[8,8192]{1,0:T(8,128)(2,1)S(1)}, bf16[8,8192]{1,0:T(8,128)(2,1)S(1)}, u32[]{:S(2)}, u32[]{:S(2)}) collective-permute-start(bf16[8,8192]{1,0:T(8,128)(2,1)S(1)} %collective-permute-done.1.refs_0_), channel_id=1, source_target_pairs={{0,1},{1,0},{2,3},{3,2},{4,5},{5,4},{6,7},{7,6},{8,9},{9,8},{10,11... | collective-permute-start | bytes 393224 | tf_op jit(solution)/shard_map/ppermute | solution.py:22
  22.2 1.3 %collective-permute-start.5 = (bf16[8,8192]{1,0:T(8,128)(2,1)S(1)}, bf16[8,8192]{1,0:T(8,128)(2,1)S(1)}, u32[]{:S(2)}, u32[]{:S(2)}) collective-permute-start(bf16[8,8192]{1,0:T(8,128)(2,1)S(1)} %collective-permute-done.3.refs_1_), channel_id=1, source_target_pairs={{0,1},{1,0},{2,3},{3,2},{4,5},{5,4},{6,7},{7,6},{8,9},{9,8},{10,11... | collective-permute-start | bytes 393224 | tf_op jit(solution)/shard_map/ppermute | solution.py:22
  26.3 1.6 %collective-permute-start.16 = (bf16[16,8192]{1,0:T(8,128)(2,1)S(1)}, bf16[16,8192]{1,0:T(8,128)(2,1)S(1)}, u32[]{:S(2)}, u32[]{:S(2)}) collective-permute-start(bf16[16,8192]{1,0:T(8,128)(2,1)S(1)} %get-tuple-element.27), channel_id=1, source_target_pairs={{0,1},{1,0},{2,3},{3,2},{4,5},{5,4},{6,7},{7,6},{8,9},{9,8},{10,11... | collective-permute-start | bytes 786440 | tf_op jit(solution)/shard_map/ppermute | solution.py:22
  26.5 4.8 %collective-permute-start.15 = (bf16[16,8192]{1,0:T(8,128)(2,1)S(1)}, bf16[16,8192]{1,0:T(8,128)(2,1)S(1)}, u32[]{:S(2)}, u32[]{:S(2)}) collective-permute-start(bf16[16,8192]{1,0:T(8,128)(2,1)S(1)} %get-tuple-element.25), channel_id=1, source_target_pairs={{0,1},{1,0},{2,3},{3,2},{4,5},{5,4},{6,7},{7,6},{8,9},{9,8},{10,11... | collective-permute-start | bytes 786440 | tf_op jit(solution)/shard_map/ppermute | solution.py:22
  26.8 2.2 %collective-permute-start.19 = (bf16[16,8192]{1,0:T(8,128)(2,1)S(1)}, bf16[16,8192]{1,0:T(8,128)(2,1)S(1)}, u32[]{:S(2)}, u32[]{:S(2)}) collective-permute-start(bf16[16,8192]{1,0:T(8,128)(2,1)S(1)} %get-tuple-element.30), channel_id=1, source_target_pairs={{0,1},{1,0},{2,3},{3,2},{4,5},{5,4},{6,7},{7,6},{8,9},{9,8},{10,11... | collective-permute-start | bytes 786440 | tf_op jit(solution)/shard_map/ppermute | solution.py:22
  27.0 3.1 %collective-permute-start.23 = (bf16[16,8192]{1,0:T(8,128)(2,1)S(1)}, bf16[16,8192]{1,0:T(8,128)(2,1)S(1)}, u32[]{:S(2)}, u32[]{:S(2)}) collective-permute-start(bf16[16,8192]{1,0:T(8,128)(2,1)S(1)} %get-tuple-element.32), channel_id=1, source_target_pairs={{0,1},{1,0},{2,3},{3,2},{4,5},{5,4},{6,7},{7,6},{8,9},{9,8},{10,11... | collective-permute-start | bytes 786440 | tf_op jit(solution)/shard_map/ppermute | solution.py:22
  27.9 6.4 %collective-permute-start.17 = (bf16[8,8192]{1,0:T(8,128)(2,1)S(1)}, bf16[8,8192]{1,0:T(8,128)(2,1)S(1)}, u32[]{:S(2)}, u32[]{:S(2)}) collective-permute-start(bf16[8,8192]{1,0:T(8,128)(2,1)S(1)} %add_convert_fusion.6), channel_id=1, source_target_pairs={{0,2},{2,0},{1,3},{3,1},{4,6},{6,4},{5,7},{7,5},{8,10},{10,8},{9,1... | collective-permute-start | bytes 393224 | tf_op jit(solution)/shard_map/ppermute | solution.py:22
  29.1 8.6 %collective-permute-start.20 = (bf16[8,8192]{1,0:T(8,128)(2,1)S(1)}, bf16[8,8192]{1,0:T(8,128)(2,1)S(1)}, u32[]{:S(2)}, u32[]{:S(2)}) collective-permute-start(bf16[8,8192]{1,0:T(8,128)(2,1)S(1)} %add_convert_fusion.5), channel_id=1, source_target_pairs={{0,2},{2,0},{1,3},{3,1},{4,6},{6,4},{5,7},{7,5},{8,10},{10,8},{9,1... | collective-permute-start | bytes 393224 | tf_op jit(solution)/shard_map/ppermute | solution.py:22
  30.1 10.1 %collective-permute-start.24 = (bf16[8,8192]{1,0:T(8,128)(2,1)S(1)}, bf16[8,8192]{1,0:T(8,128)(2,1)S(1)}, u32[]{:S(2)}, u32[]{:S(2)}) collective-permute-start(bf16[8,8192]{1,0:T(8,128)(2,1)S(1)} %add_convert_fusion.2), channel_id=1, source_target_pairs={{0,2},{2,0},{1,3},{3,1},{4,6},{6,4},{5,7},{7,5},{8,10},{10,8},{9,1... | collective-permute-start | bytes 393224 | tf_op jit(solution)/shard_map/ppermute | solution.py:22
  34.3 7.6 %collective-permute-start.18 = (bf16[8,8192]{1,0:T(8,128)(2,1)S(1)}, bf16[8,8192]{1,0:T(8,128)(2,1)S(1)}, u32[]{:S(2)}, u32[]{:S(2)}) collective-permute-start(bf16[8,8192]{1,0:T(8,128)(2,1)S(1)} %add_convert_fusion.7), channel_id=1, source_target_pairs={{0,2},{2,0},{1,3},{3,1},{4,6},{6,4},{5,7},{7,5},{8,10},{10,8},{9,1... | collective-permute-start | bytes 393224 | tf_op jit(solution)/shard_map/ppermute | solution.py:22
  35.4 11.6 %collective-permute-start.22 = (bf16[8,8192]{1,0:T(8,128)(2,1)S(1)}, bf16[8,8192]{1,0:T(8,128)(2,1)S(1)}, u32[]{:S(2)}, u32[]{:S(2)}) collective-permute-start(bf16[8,8192]{1,0:T(8,128)(2,1)S(1)} %add_convert_fusion.3), channel_id=1, source_target_pairs={{0,8},{4,12},{8,0},{12,4},{1,9},{5,13},{9,1},{13,5},{2,10},{6,14},... | collective-permute-start | bytes 393224 | tf_op jit(solution)/shard_map/ppermute | solution.py:26
  37.7 9.3 %collective-permute-start.21 = (bf16[8,8192]{1,0:T(8,128)(2,1)S(1)}, bf16[8,8192]{1,0:T(8,128)(2,1)S(1)}, u32[]{:S(2)}, u32[]{:S(2)}) collective-permute-start(bf16[8,8192]{1,0:T(8,128)(2,1)S(1)} %add_convert_fusion.4), channel_id=1, source_target_pairs={{0,12},{4,8},{8,4},{12,0},{1,13},{5,9},{9,5},{13,1},{2,14},{6,10},... | collective-permute-start | bytes 393224 | tf_op jit(solution)/shard_map/ppermute | solution.py:26
  40.3 7.1 %collective-permute-start.25 = (bf16[8,8192]{1,0:T(8,128)(2,1)S(1)}, bf16[8,8192]{1,0:T(8,128)(2,1)S(1)}, u32[]{:S(2)}, u32[]{:S(2)}) collective-permute-start(bf16[8,8192]{1,0:T(8,128)(2,1)S(1)} %add_convert_fusion.1), channel_id=1, source_target_pairs={{0,4},{4,0},{8,12},{12,8},{1,5},{5,1},{9,13},{13,9},{2,6},{6,2},{1... | collective-permute-start | bytes 393224 | tf_op jit(solution)/shard_map/ppermute | solution.py:26

commit v6 on v5

--- a/solution.py
+++ b/solution.py
@@ -24,6 +24,11 @@
 
 def across(x, away):
     return lax.ppermute(x, "z", [(i, i ^ away) for i in range(lax.axis_size("z"))])
+
+
+def diagonal(x, away):
+    places = [(i, j) for i in range(lax.axis_size("z")) for j in range(2)]
+    return lax.ppermute(x, ("z", "y"), [(2 * i + j, 2 * (i ^ away) + 1 - j) for i, j in places])
 
 
 def after(x, *others):
@@ -166,16 +171,17 @@
     which, a, b, own = prepare(adapter_home, req_adapter, req_tokens, a_down, b_up, attention_out, tok_rows)
 
     far = {0: attention_out, 1: across(attention_out, 1)}
-    near = {e: other(far[e], "y") for e in range(2)}
+    near = {0: other(attention_out, "y"), 1: diagonal(attention_out, 1)}
     for e in range(2, planes, 2):
-        far[e] = after(across(attention_out, e), which)
-        near[e] = other(far[e], "y")
+        far[e] = across(attention_out, e)
+        near[e] = other(after(far[e], which), "y")
         far[e + 1], near[e + 1] = across(far[e], 1), across(near[e], 1)
 
     parts = tuple(range(planes))[::-1]
     xs = []
     for e in parts:
-        xs += [far[e] if e else own, near[e], other(far[e], "core"), other(near[e], "core")]
+        waits = near[e] if e != 1 else after(near[e], far[planes - 1])
+        xs += [far[e] if e else own, near[e], other(far[e], "core"), other(waits, "core")]
     sums = partial_rows(which, o_weight, a, b, xs, parts, rank)
     out = None
     arriving = []

time: 48.3 us -> 47.8 us (0.990)
  waiting for transfers between devices: 19 us -> 13.9 us
  starting transfers between devices: 21.7 us -> 25.9 us
    ppermute x19 -> x18, waiting for transfers between devices: 11.2 us -> 5.79 us  [other(): return lax.ppermute(x, axis, SWAP)]
    ppermute x0 -> x1, starting transfers between devices: none -> 2.53 us  [diagonal(): lax.ppermute(x, ('z', 'y'), [(2 * i + j, 2 * (i ^ away) + 1 - j) for i, j...]
    ppermute x7, starting transfers between devices: 11.9 us -> 13.4 us  [across(): lax.ppermute(x, 'z', [(i, i ^ away) for i in range(lax.axis_size('z'))])]
    ppermute x19 -> x18, starting transfers between devices: 9.84 us -> 9.99 us  [other(): return lax.ppermute(x, axis, SWAP)]
where the time goes in v6:
time: 47.8 us; the launch traced here: 47.7 us
  starting transfers between devices  25.9 us (54%)
  waiting for transfers between devices  13.9 us (29%)
  Pallas kernels  6.7 us (14%)
  other arithmetic  1.01 us (2%)
    ppermute x7, starting transfers between devices, across(): lax.ppermute(x, 'z', [(i, i ^ away) for i in range(lax.axis_size('z'))])  13.4 us
    ppermute x18, starting transfers between devices, other(): return lax.ppermute(x, axis, SWAP)  9.99 us
    ppermute x7, waiting for transfers between devices, across(): lax.ppermute(x, 'z', [(i, i ^ away) for i in range(lax.axis_size('z'))])  8.15 us
    ppermute x18, waiting for transfers between devices, other(): return lax.ppermute(x, axis, SWAP)  5.79 us
    pallas_call x1, Pallas kernels, prepare(): pl.pallas_call(functools.partial(prepare_kernel, tok_rows=tok_rows), out_...  4.03 us
    pallas_call x1, Pallas kernels, partial_rows(): pl.pallas_call(functools.partial(partial_kernel, parts=parts, rank=rank),...  2.67 us
    ppermute x1, starting transfers between devices, diagonal(): lax.ppermute(x, ('z', 'y'), [(2 * i + j, 2 * (i ^ away) + 1 - j) for i, j...  2.53 us
  transfers between devices with their start and end apart: 26, of which 9 were waited for; matrix products, arithmetic and copies ran while one was open for 1% of the time, Pallas kernels for 8%

profile of v6, /device:TPU:0, one launch (start us, length us, event | category | flops | bytes accessed | tf_op | source)
XLA Modules:
  0.0 47.7 jit_solution(17070877051254820184)
XLA Ops:
  0.0 4.0 %collective-permute-start = (bf16[8,8192]{1,0:T(8,128)(2,1)}, bf16[8,8192]{1,0:T(8,128)(2,1)S(1)}, u32[]{:S(2)}, u32[]{:S(2)}) collective-permute-start(bf16[8,8192]{1,0:T(8,128)(2,1)} %x_hbm.1), channel_id=1, source_target_pairs={{0,8},{4,12},{8,0},{12,4},{1,9},{5,13},{9,1},{13,5},{2,10},{6,14},... | collective-permute-start | bytes 393224 | tf_op jit(solution)/shard_map/ppermute | solution.py:26
  4.0 2.5 %collective-permute-start.9 = (bf16[8,8192]{1,0:T(8,128)(2,1)}, bf16[8,8192]{1,0:T(8,128)(2,1)S(1)}, u32[]{:S(2)}, u32[]{:S(2)}) collective-permute-start(bf16[8,8192]{1,0:T(8,128)(2,1)} %x_hbm.1), channel_id=1, source_target_pairs={{0,6},{2,4},{4,2},{6,0},{8,14},{10,12},{12,10},{14,8},{1,7},{3,5},... | collective-permute-start | bytes 393224 | tf_op jit(solution)/shard_map/ppermute | solution.py:31
  6.6 0.4 collective-permute-start.8
  7.0 0.5 %collective-permute-start.12 = (bf16[8,8192]{1,0:T(8,128)(2,1)}, bf16[8,8192]{1,0:T(8,128)(2,1)S(1)}, u32[]{:S(2)}, u32[]{:S(2)}) collective-permute-start(bf16[8,8192]{1,0:T(8,128)(2,1)} %x_hbm.1), channel_id=1, source_target_pairs={{0,2},{2,0},{1,3},{3,1},{4,6},{6,4},{5,7},{7,5},{8,10},{10,8},{9,1... | collective-permute-start | bytes 393224 | tf_op jit(solution)/shard_map/ppermute | solution.py:22
  7.5 4.0 %prepare.1 = (s32[128,1]{1,0:T(8,128)S(1)}, bf16[128,8192]{1,0:T(8,128)(2,1)S(1)}, bf16[128,8192]{1,0:T(8,128)(2,1)S(1)}, bf16[8,8192]{1,0:T(8,128)(2,1)S(1)}) custom-call(s32[64]{0:T(128)} %home_hbm.1, s32[64]{0:T(128)} %adapter_hbm.1, s32[4,16]{1,0:T(4,128)} %bitcast.1, bf16[4,64,8192]{2,1,0:T(8,128)(2,1)} %a_hbm.1, bf16[4,64,8192]{2,1,0:T(8,128)(2,1)} %b_hbm.1, ...), custom_call_target="tpu_custom_call" | custom-call | bytes 4194304 | tf_op jit(solution)/shard_map/prepare/pallas_call | solution.py:98
  11.6 1.6 %collective-permute-start.2 = (bf16[8,8192]{1,0:T(8,128)(2,1)S(1)}, bf16[8,8192]{1,0:T(8,128)(2,1)S(1)}, u32[]{:S(2)}, u32[]{:S(2)}) collective-permute-start(bf16[8,8192]{1,0:T(8,128)(2,1)S(1)} %collective-permute-done.refs_4_), channel_id=1, source_target_pairs={{0,2},{2,0},{1,3},{3,1},{4,6},{6,4},{5,7},{7,5},{8,10},{10,8},{9,1... | collective-permute-start | bytes 393224 | tf_op jit(solution)/shard_map/ppermute | solution.py:22
  13.2 1.6 %collective-permute-start.1 = (bf16[8,8192]{1,0:T(8,128)(2,1)S(1)}, bf16[8,8192]{1,0:T(8,128)(2,1)S(1)}, u32[]{:S(2)}, u32[]{:S(2)}) collective-permute-start(bf16[8,8192]{1,0:T(8,128)(2,1)S(1)} %collective-permute-done.refs_4_), channel_id=1, source_target_pairs={{0,4},{4,0},{8,12},{12,8},{1,5},{5,1},{9,13},{13,9},{2,6},{6,2},{1... | collective-permute-start | bytes 393224 | tf_op jit(solution)/shard_map/ppermute | solution.py:26
  15.0 0.3 collective-permute-start.10
  15.3 0.2 collective-permute-start.6
  15.5 1.1 %collective-permute-done.2.refs_5_ = bf16[8,8192]{1,0:T(8,128)(2,1)S(1)} collective-permute-done((bf16[8,8192]{1,0:T(8,128)(2,1)S(1)}, bf16[8,8192]{1,0:T(8,128)(2,1)S(1)}, u32[]{:S(2)}, u32[]{:S(2)}) %collective-permute-start.2) | collective-permute-done | bytes 131104 | tf_op jit(solution)/shard_map/ppermute | solution.py:22
  16.6 1.7 %collective-permute-start.3 = (bf16[8,8192]{1,0:T(8,128)(2,1)S(1)}, bf16[8,8192]{1,0:T(8,128)(2,1)S(1)}, u32[]{:S(2)}, u32[]{:S(2)}) collective-permute-start(bf16[8,8192]{1,0:T(8,128)(2,1)S(1)} %collective-permute-done.2.refs_5_), channel_id=1, source_target_pairs={{0,4},{4,0},{8,12},{12,8},{1,5},{5,1},{9,13},{13,9},{2,6},{6,2},{1... | collective-permute-start | bytes 393224 | tf_op jit(solution)/shard_map/ppermute | solution.py:26
  18.3 0.5 %collective-permute-start.11 = (bf16[8,8192]{1,0:T(8,128)(2,1)S(1)}, bf16[8,8192]{1,0:T(8,128)(2,1)S(1)}, u32[]{:S(2)}, u32[]{:S(2)}) collective-permute-start(bf16[8,8192]{1,0:T(8,128)(2,1)S(1)} %collective-permute-done.9.refs_9_), channel_id=1, source_target_pairs={{0,1},{1,0},{2,3},{3,2},{4,5},{5,4},{6,7},{7,6},{8,9},{9,8},{10,11... | collective-permute-start | bytes 393224 | tf_op jit(solution)/shard_map/ppermute | solution.py:22
  18.9 0.4 collective-permute-start.7
  19.3 2.3 %collective-permute-done.3.refs_1_ = bf16[8,8192]{1,0:T(8,128)(2,1)S(1)} collective-permute-done((bf16[8,8192]{1,0:T(8,128)(2,1)S(1)}, bf16[8,8192]{1,0:T(8,128)(2,1)S(1)}, u32[]{:S(2)}, u32[]{:S(2)}) %collective-permute-start.3) | collective-permute-done | bytes 131104 | tf_op jit(solution)/shard_map/ppermute | solution.py:26
  21.6 1.3 %collective-permute-done.5.refs_3_ = bf16[8,8192]{1,0:T(8,128)(2,1)S(1)} collective-permute-done((bf16[8,8192]{1,0:T(8,128)(2,1)S(1)}, bf16[8,8192]{1,0:T(8,128)(2,1)S(1)}, u32[]{:S(2)}, u32[]{:S(2)}) %collective-permute-start.5) | collective-permute-done | bytes 131104 | tf_op jit(solution)/shard_map/ppermute | solution.py:22
  22.9 2.7 %partial_rows.1 = (f32[16,8192]{1,0:T(8,128)S(1)}, bf16[16,8192]{1,0:T(8,128)(2,1)S(1)}, f32[16,8192]{1,0:T(8,128)S(1)}, bf16[16,8192]{1,0:T(8,128)(2,1)S(1)}, f...) custom-call(s32[128,1]{1,0:T(8,128)S(1)} %get-tuple-element.20.which, ...), custom_call_target="tpu_custom_call" | custom-call | flops 1610612736 | bytes 16777216 | tf_op jit(solution)/shard_map/partial_rows/pallas_call | solution.py:153
  25.6 0.2 collective-permute-start.16
  25.8 0.4 collective-permute-start.15
  26.3 0.4 collective-permute-start.23
  26.7 0.5 %collective-permute-done.16 = bf16[16,8192]{1,0:T(8,128)(2,1)S(1)} collective-permute-done((bf16[16,8192]{1,0:T(8,128)(2,1)S(1)}, bf16[16,8192]{1,0:T(8,128)(2,1)S(1)}, u32[]{:S(2)}, u32[]{:S(2)}) %collective-permute-start.16) | collective-permute-done | bytes 262176 | tf_op jit(solution)/shard_map/ppermute | solution.py:22
  27.2 1.6 %collective-permute-start.17 = (bf16[8,8192]{1,0:T(8,128)(2,1)S(1)}, bf16[8,8192]{1,0:T(8,128)(2,1)S(1)}, u32[]{:S(2)}, u32[]{:S(2)}) collective-permute-start(bf16[8,8192]{1,0:T(8,128)(2,1)S(1)} %add_convert_fusion.6), channel_id=1, source_target_pairs={{0,2},{2,0},{1,3},{3,1},{4,6},{6,4},{5,7},{7,5},{8,10},{10,8},{9,1... | collective-permute-start | bytes 393224 | tf_op jit(solution)/shard_map/ppermute | solution.py:22
  28.9 0.7 %collective-permute-start.20 = (bf16[8,8192]{1,0:T(8,128)(2,1)S(1)}, bf16[8,8192]{1,0:T(8,128)(2,1)S(1)}, u32[]{:S(2)}, u32[]{:S(2)}) collective-permute-start(bf16[8,8192]{1,0:T(8,128)(2,1)S(1)} %add_convert_fusion.5), channel_id=1, source_target_pairs={{0,2},{2,0},{1,3},{3,1},{4,6},{6,4},{5,7},{7,5},{8,10},{10,8},{9,1... | collective-permute-start | bytes 393224 | tf_op jit(solution)/shard_map/ppermute | solution.py:22
  29.6 1.4 %collective-permute-start.24 = (bf16[8,8192]{1,0:T(8,128)(2,1)S(1)}, bf16[8,8192]{1,0:T(8,128)(2,1)S(1)}, u32[]{:S(2)}, u32[]{:S(2)}) collective-permute-start(bf16[8,8192]{1,0:T(8,128)(2,1)S(1)} %add_convert_fusion.2), channel_id=1, source_target_pairs={{0,2},{2,0},{1,3},{3,1},{4,6},{6,4},{5,7},{7,5},{8,10},{10,8},{9,1... | collective-permute-start | bytes 393224 | tf_op jit(solution)/shard_map/ppermute | solution.py:22
  31.1 2.5 %collective-permute-done.17 = bf16[8,8192]{1,0:T(8,128)(2,1)S(1)} collective-permute-done((bf16[8,8192]{1,0:T(8,128)(2,1)S(1)}, bf16[8,8192]{1,0:T(8,128)(2,1)S(1)}, u32[]{:S(2)}, u32[]{:S(2)}) %collective-permute-start.17) | collective-permute-done | bytes 131104 | tf_op jit(solution)/shard_map/ppermute | solution.py:22
  33.7 1.5 %collective-permute-start.18 = (bf16[8,8192]{1,0:T(8,128)(2,1)S(1)}, bf16[8,8192]{1,0:T(8,128)(2,1)S(1)}, u32[]{:S(2)}, u32[]{:S(2)}) collective-permute-start(bf16[8,8192]{1,0:T(8,128)(2,1)S(1)} %add_convert_fusion.7), channel_id=1, source_target_pairs={{0,2},{2,0},{1,3},{3,1},{4,6},{6,4},{5,7},{7,5},{8,10},{10,8},{9,1... | collective-permute-start | bytes 393224 | tf_op jit(solution)/shard_map/ppermute | solution.py:22
  35.2 1.5 %collective-permute-start.22 = (bf16[8,8192]{1,0:T(8,128)(2,1)S(1)}, bf16[8,8192]{1,0:T(8,128)(2,1)S(1)}, u32[]{:S(2)}, u32[]{:S(2)}) collective-permute-start(bf16[8,8192]{1,0:T(8,128)(2,1)S(1)} %add_convert_fusion.3), channel_id=1, source_target_pairs={{0,8},{4,12},{8,0},{12,4},{1,9},{5,13},{9,1},{13,5},{2,10},{6,14},... | collective-permute-start | bytes 393224 | tf_op jit(solution)/shard_map/ppermute | solution.py:26
  36.8 2.7 %collective-permute-start.21 = (bf16[8,8192]{1,0:T(8,128)(2,1)S(1)}, bf16[8,8192]{1,0:T(8,128)(2,1)S(1)}, u32[]{:S(2)}, u32[]{:S(2)}) collective-permute-start(bf16[8,8192]{1,0:T(8,128)(2,1)S(1)} %add_convert_fusion.4), channel_id=1, source_target_pairs={{0,12},{4,8},{8,4},{12,0},{1,13},{5,9},{9,5},{13,1},{2,14},{6,10},... | collective-permute-start | bytes 393224 | tf_op jit(solution)/shard_map/ppermute | solution.py:26
  39.6 1.5 %collective-permute-start.25 = (bf16[8,8192]{1,0:T(8,128)(2,1)S(1)}, bf16[8,8192]{1,0:T(8,128)(2,1)S(1)}, u32[]{:S(2)}, u32[]{:S(2)}) collective-permute-start(bf16[8,8192]{1,0:T(8,128)(2,1)S(1)} %add_convert_fusion.1), channel_id=1, source_target_pairs={{0,4},{4,0},{8,12},{12,8},{1,5},{5,1},{9,13},{13,9},{2,6},{6,2},{1... | collective-permute-start | bytes 393224 | tf_op jit(solution)/shard_map/ppermute | solution.py:26
  41.0 0.2 collective-permute-done.18
  41.3 5.3 %collective-permute-done.22 = bf16[8,8192]{1,0:T(8,128)(2,1)S(1)} collective-permute-done((bf16[8,8192]{1,0:T(8,128)(2,1)S(1)}, bf16[8,8192]{1,0:T(8,128)(2,1)S(1)}, u32[]{:S(2)}, u32[]{:S(2)}) %collective-permute-start.22) | collective-permute-done | bytes 131104 | tf_op jit(solution)/shard_map/ppermute | solution.py:26
  46.6 0.3 collective-permute-done.25
  47.0 0.7 %add_convert_fusion = bf16[8,8192]{1,0:T(8,128)(2,1)} fusion(bf16[8,8192]{1,0:T(8,128)(2,1)S(1)} %collective-permute-done.25, bf16[8,8192]{1,0:T(8,128)(2,1)S(1)} %collective-permute-done.22, bf16[8,8192]{1,0:T(8,128)(2,1)S(1)} %collective-permute-done.21, bf16[8,8192]{1,0:T(8,128)(2,1)S(1)} %collective-permute-done.18, f32[16,8192]{1,0:T(8,128)S(1)} %get-tuple-element.26, ...), kind=kLoop, calls=%fused_computation | loop fusion | flops 720896 | bytes 1048576 | tf_op jit(solution)/shard_map/convert_element_type | solution.py:205
  (34 shorter events, 0.8 us)
Async XLA Ops:
  0.0 11.6 %collective-permute-start = (bf16[8,8192]{1,0:T(8,128)(2,1)}, bf16[8,8192]{1,0:T(8,128)(2,1)S(1)}, u32[]{:S(2)}, u32[]{:S(2)}) collective-permute-start(bf16[8,8192]{1,0:T(8,128)(2,1)} %x_hbm.1), channel_id=1, source_target_pairs={{0,8},{4,12},{8,0},{12,4},{1,9},{5,13},{9,1},{13,5},{2,10},{6,14},... | collective-permute-start | bytes 393224 | tf_op jit(solution)/shard_map/ppermute | solution.py:26
  4.0 10.7 %collective-permute-start.9 = (bf16[8,8192]{1,0:T(8,128)(2,1)}, bf16[8,8192]{1,0:T(8,128)(2,1)S(1)}, u32[]{:S(2)}, u32[]{:S(2)}) collective-permute-start(bf16[8,8192]{1,0:T(8,128)(2,1)} %x_hbm.1), channel_id=1, source_target_pairs={{0,6},{2,4},{4,2},{6,0},{8,14},{10,12},{12,10},{14,8},{1,7},{3,5},... | collective-permute-start | bytes 393224 | tf_op jit(solution)/shard_map/ppermute | solution.py:31
  6.6 8.4 %collective-permute-start.8 = (bf16[8,8192]{1,0:T(8,128)(2,1)}, bf16[8,8192]{1,0:T(8,128)(2,1)S(1)}, u32[]{:S(2)}, u32[]{:S(2)}) collective-permute-start(bf16[8,8192]{1,0:T(8,128)(2,1)} %x_hbm.1), channel_id=1, source_target_pairs={{0,4},{4,0},{8,12},{12,8},{1,5},{5,1},{9,13},{13,9},{2,6},{6,2},{1... | collective-permute-start | bytes 393224 | tf_op jit(solution)/shard_map/ppermute | solution.py:26
  7.0 8.2 %collective-permute-start.12 = (bf16[8,8192]{1,0:T(8,128)(2,1)}, bf16[8,8192]{1,0:T(8,128)(2,1)S(1)}, u32[]{:S(2)}, u32[]{:S(2)}) collective-permute-start(bf16[8,8192]{1,0:T(8,128)(2,1)} %x_hbm.1), channel_id=1, source_target_pairs={{0,2},{2,0},{1,3},{3,1},{4,6},{6,4},{5,7},{7,5},{8,10},{10,8},{9,1... | collective-permute-start | bytes 393224 | tf_op jit(solution)/shard_map/ppermute | solution.py:22
  7.5 7.2 %copy-start.1 = (bf16[8,8192]{1,0:T(8,128)(2,1)S(1)}, bf16[8,8192]{1,0:T(8,128)(2,1)}, u32[]{:S(2)}) copy-start(bf16[8,8192]{1,0:T(8,128)(2,1)} %x_hbm.1) | copy-start | bytes 393220
  7.5 15.4 %copy-start = (bf16[512,8192]{1,0:T(8,128)(2,1)S(1)}, bf16[512,8192]{1,0:T(8,128)(2,1)}, u32[]{:S(2)}) copy-start(bf16[512,8192]{1,0:T(8,128)(2,1)} %w_ref.1) | copy-start | bytes 25165828
  11.6 5.0 %collective-permute-start.2 = (bf16[8,8192]{1,0:T(8,128)(2,1)S(1)}, bf16[8,8192]{1,0:T(8,128)(2,1)S(1)}, u32[]{:S(2)}, u32[]{:S(2)}) collective-permute-start(bf16[8,8192]{1,0:T(8,128)(2,1)S(1)} %collective-permute-done.refs_4_), channel_id=1, source_target_pairs={{0,2},{2,0},{1,3},{3,1},{4,6},{6,4},{5,7},{7,5},{8,10},{10,8},{9,1... | collective-permute-start | bytes 393224 | tf_op jit(solution)/shard_map/ppermute | solution.py:22
  13.2 5.1 %collective-permute-start.1 = (bf16[8,8192]{1,0:T(8,128)(2,1)S(1)}, bf16[8,8192]{1,0:T(8,128)(2,1)S(1)}, u32[]{:S(2)}, u32[]{:S(2)}) collective-permute-start(bf16[8,8192]{1,0:T(8,128)(2,1)S(1)} %collective-permute-done.refs_4_), channel_id=1, source_target_pairs={{0,4},{4,0},{8,12},{12,8},{1,5},{5,1},{9,13},{13,9},{2,6},{6,2},{1... | collective-permute-start | bytes 393224 | tf_op jit(solution)/shard_map/ppermute | solution.py:26
  14.7 3.5 %collective-permute-start.13 = (bf16[8,8192]{1,0:T(8,128)(2,1)S(1)}, bf16[8,8192]{1,0:T(8,128)(2,1)S(1)}, u32[]{:S(2)}, u32[]{:S(2)}) collective-permute-start(bf16[8,8192]{1,0:T(8,128)(2,1)S(1)} %copy-done.1), channel_id=1, source_target_pairs={{0,1},{1,0},{2,3},{3,2},{4,5},{5,4},{6,7},{7,6},{8,9},{9,8},{10,11... | collective-permute-start | bytes 393224 | tf_op jit(solution)/shard_map/ppermute | solution.py:22
  15.0 3.8 %collective-permute-start.10 = (bf16[8,8192]{1,0:T(8,128)(2,1)S(1)}, bf16[8,8192]{1,0:T(8,128)(2,1)S(1)}, u32[]{:S(2)}, u32[]{:S(2)}) collective-permute-start(bf16[8,8192]{1,0:T(8,128)(2,1)S(1)} %collective-permute-done.8.refs_8_), channel_id=1, source_target_pairs={{0,1},{1,0},{2,3},{3,2},{4,5},{5,4},{6,7},{7,6},{8,9},{9,8},{10,11... | collective-permute-start | bytes 393224 | tf_op jit(solution)/shard_map/ppermute | solution.py:22
  15.3 3.6 %collective-permute-start.6 = (bf16[8,8192]{1,0:T(8,128)(2,1)S(1)}, bf16[8,8192]{1,0:T(8,128)(2,1)S(1)}, u32[]{:S(2)}, u32[]{:S(2)}) collective-permute-start(bf16[8,8192]{1,0:T(8,128)(2,1)S(1)} %collective-permute-done.refs_4_), channel_id=1, source_target_pairs={{0,1},{1,0},{2,3},{3,2},{4,5},{5,4},{6,7},{7,6},{8,9},{9,8},{10,11... | collective-permute-start | bytes 393224 | tf_op jit(solution)/shard_map/ppermute | solution.py:22
  16.6 5.0 %collective-permute-start.3 = (bf16[8,8192]{1,0:T(8,128)(2,1)S(1)}, bf16[8,8192]{1,0:T(8,128)(2,1)S(1)}, u32[]{:S(2)}, u32[]{:S(2)}) collective-permute-start(bf16[8,8192]{1,0:T(8,128)(2,1)S(1)} %collective-permute-done.2.refs_5_), channel_id=1, source_target_pairs={{0,4},{4,0},{8,12},{12,8},{1,5},{5,1},{9,13},{13,9},{2,6},{6,2},{1... | collective-permute-start | bytes 393224 | tf_op jit(solution)/shard_map/ppermute | solution.py:26
  18.3 3.3 %collective-permute-start.14 = (bf16[8,8192]{1,0:T(8,128)(2,1)S(1)}, bf16[8,8192]{1,0:T(8,128)(2,1)S(1)}, u32[]{:S(2)}, u32[]{:S(2)}) collective-permute-start(bf16[8,8192]{1,0:T(8,128)(2,1)S(1)} %collective-permute-done.12.refs_13_), channel_id=1, source_target_pairs={{0,1},{1,0},{2,3},{3,2},{4,5},{5,4},{6,7},{7,6},{8,9},{9,8},{10,11... | collective-permute-start | bytes 393224 | tf_op jit(solution)/shard_map/ppermute | solution.py:22
  18.3 3.3 %collective-permute-start.11 = (bf16[8,8192]{1,0:T(8,128)(2,1)S(1)}, bf16[8,8192]{1,0:T(8,128)(2,1)S(1)}, u32[]{:S(2)}, u32[]{:S(2)}) collective-permute-start(bf16[8,8192]{1,0:T(8,128)(2,1)S(1)} %collective-permute-done.9.refs_9_), channel_id=1, source_target_pairs={{0,1},{1,0},{2,3},{3,2},{4,5},{5,4},{6,7},{7,6},{8,9},{9,8},{10,11... | collective-permute-start | bytes 393224 | tf_op jit(solution)/shard_map/ppermute | solution.py:22
  18.8 2.8 %collective-permute-start.4 = (bf16[8,8192]{1,0:T(8,128)(2,1)S(1)}, bf16[8,8192]{1,0:T(8,128)(2,1)S(1)}, u32[]{:S(2)}, u32[]{:S(2)}) collective-permute-start(bf16[8,8192]{1,0:T(8,128)(2,1)S(1)} %collective-permute-done.1.refs_0_), channel_id=1, source_target_pairs={{0,1},{1,0},{2,3},{3,2},{4,5},{5,4},{6,7},{7,6},{8,9},{9,8},{10,11... | collective-permute-start | bytes 393224 | tf_op jit(solution)/shard_map/ppermute | solution.py:22
  18.9 2.7 %collective-permute-start.7 = (bf16[8,8192]{1,0:T(8,128)(2,1)S(1)}, bf16[8,8192]{1,0:T(8,128)(2,1)S(1)}, u32[]{:S(2)}, u32[]{:S(2)}) collective-permute-start(bf16[8,8192]{1,0:T(8,128)(2,1)S(1)} %collective-permute-done.2.refs_5_), channel_id=1, source_target_pairs={{0,1},{1,0},{2,3},{3,2},{4,5},{5,4},{6,7},{7,6},{8,9},{9,8},{10,11... | collective-permute-start | bytes 393224 | tf_op jit(solution)/shard_map/ppermute | solution.py:22
  21.6 1.3 %collective-permute-start.5 = (bf16[8,8192]{1,0:T(8,128)(2,1)S(1)}, bf16[8,8192]{1,0:T(8,128)(2,1)S(1)}, u32[]{:S(2)}, u32[]{:S(2)}) collective-permute-start(bf16[8,8192]{1,0:T(8,128)(2,1)S(1)} %collective-permute-done.3.refs_1_), channel_id=1, source_target_pairs={{0,1},{1,0},{2,3},{3,2},{4,5},{5,4},{6,7},{7,6},{8,9},{9,8},{10,11... | collective-permute-start | bytes 393224 | tf_op jit(solution)/shard_map/ppermute | solution.py:22
  25.6 1.6 %collective-permute-start.16 = (bf16[16,8192]{1,0:T(8,128)(2,1)S(1)}, bf16[16,8192]{1,0:T(8,128)(2,1)S(1)}, u32[]{:S(2)}, u32[]{:S(2)}) collective-permute-start(bf16[16,8192]{1,0:T(8,128)(2,1)S(1)} %get-tuple-element.29), channel_id=1, source_target_pairs={{0,1},{1,0},{2,3},{3,2},{4,5},{5,4},{6,7},{7,6},{8,9},{9,8},{10,11... | collective-permute-start | bytes 786440 | tf_op jit(solution)/shard_map/ppermute | solution.py:22
  25.8 5.2 %collective-permute-start.15 = (bf16[16,8192]{1,0:T(8,128)(2,1)S(1)}, bf16[16,8192]{1,0:T(8,128)(2,1)S(1)}, u32[]{:S(2)}, u32[]{:S(2)}) collective-permute-start(bf16[16,8192]{1,0:T(8,128)(2,1)S(1)} %get-tuple-element.27), channel_id=1, source_target_pairs={{0,1},{1,0},{2,3},{3,2},{4,5},{5,4},{6,7},{7,6},{8,9},{9,8},{10,11... | collective-permute-start | bytes 786440 | tf_op jit(solution)/shard_map/ppermute | solution.py:22
  26.2 2.7 %collective-permute-start.19 = (bf16[16,8192]{1,0:T(8,128)(2,1)S(1)}, bf16[16,8192]{1,0:T(8,128)(2,1)S(1)}, u32[]{:S(2)}, u32[]{:S(2)}) collective-permute-start(bf16[16,8192]{1,0:T(8,128)(2,1)S(1)} %get-tuple-element.32), channel_id=1, source_target_pairs={{0,1},{1,0},{2,3},{3,2},{4,5},{5,4},{6,7},{7,6},{8,9},{9,8},{10,11... | collective-permute-start | bytes 786440 | tf_op jit(solution)/shard_map/ppermute | solution.py:22
  26.3 3.3 %collective-permute-start.23 = (bf16[16,8192]{1,0:T(8,128)(2,1)S(1)}, bf16[16,8192]{1,0:T(8,128)(2,1)S(1)}, u32[]{:S(2)}, u32[]{:S(2)}) collective-permute-start(bf16[16,8192]{1,0:T(8,128)(2,1)S(1)} %get-tuple-element.34), channel_id=1, source_target_pairs={{0,1},{1,0},{2,3},{3,2},{4,5},{5,4},{6,7},{7,6},{8,9},{9,8},{10,11... | collective-permute-start | bytes 786440 | tf_op jit(solution)/shard_map/ppermute | solution.py:22
  27.2 6.4 %collective-permute-start.17 = (bf16[8,8192]{1,0:T(8,128)(2,1)S(1)}, bf16[8,8192]{1,0:T(8,128)(2,1)S(1)}, u32[]{:S(2)}, u32[]{:S(2)}) collective-permute-start(bf16[8,8192]{1,0:T(8,128)(2,1)S(1)} %add_convert_fusion.6), channel_id=1, source_target_pairs={{0,2},{2,0},{1,3},{3,1},{4,6},{6,4},{5,7},{7,5},{8,10},{10,8},{9,1... | collective-permute-start | bytes 393224 | tf_op jit(solution)/shard_map/ppermute | solution.py:22
  28.9 7.9 %collective-permute-start.20 = (bf16[8,8192]{1,0:T(8,128)(2,1)S(1)}, bf16[8,8192]{1,0:T(8,128)(2,1)S(1)}, u32[]{:S(2)}, u32[]{:S(2)}) collective-permute-start(bf16[8,8192]{1,0:T(8,128)(2,1)S(1)} %add_convert_fusion.5), channel_id=1, source_target_pairs={{0,2},{2,0},{1,3},{3,1},{4,6},{6,4},{5,7},{7,5},{8,10},{10,8},{9,1... | collective-permute-start | bytes 393224 | tf_op jit(solution)/shard_map/ppermute | solution.py:22
  29.6 9.9 %collective-permute-start.24 = (bf16[8,8192]{1,0:T(8,128)(2,1)S(1)}, bf16[8,8192]{1,0:T(8,128)(2,1)S(1)}, u32[]{:S(2)}, u32[]{:S(2)}) collective-permute-start(bf16[8,8192]{1,0:T(8,128)(2,1)S(1)} %add_convert_fusion.2), channel_id=1, source_target_pairs={{0,2},{2,0},{1,3},{3,1},{4,6},{6,4},{5,7},{7,5},{8,10},{10,8},{9,1... | collective-permute-start | bytes 393224 | tf_op jit(solution)/shard_map/ppermute | solution.py:22
  33.7 7.6 %collective-permute-start.18 = (bf16[8,8192]{1,0:T(8,128)(2,1)S(1)}, bf16[8,8192]{1,0:T(8,128)(2,1)S(1)}, u32[]{:S(2)}, u32[]{:S(2)}) collective-permute-start(bf16[8,8192]{1,0:T(8,128)(2,1)S(1)} %add_convert_fusion.7), channel_id=1, source_target_pairs={{0,2},{2,0},{1,3},{3,1},{4,6},{6,4},{5,7},{7,5},{8,10},{10,8},{9,1... | collective-permute-start | bytes 393224 | tf_op jit(solution)/shard_map/ppermute | solution.py:22
  35.2 11.4 %collective-permute-start.22 = (bf16[8,8192]{1,0:T(8,128)(2,1)S(1)}, bf16[8,8192]{1,0:T(8,128)(2,1)S(1)}, u32[]{:S(2)}, u32[]{:S(2)}) collective-permute-start(bf16[8,8192]{1,0:T(8,128)(2,1)S(1)} %add_convert_fusion.3), channel_id=1, source_target_pairs={{0,8},{4,12},{8,0},{12,4},{1,9},{5,13},{9,1},{13,5},{2,10},{6,14},... | collective-permute-start | bytes 393224 | tf_op jit(solution)/shard_map/ppermute | solution.py:26
  36.8 9.8 %collective-permute-start.21 = (bf16[8,8192]{1,0:T(8,128)(2,1)S(1)}, bf16[8,8192]{1,0:T(8,128)(2,1)S(1)}, u32[]{:S(2)}, u32[]{:S(2)}) collective-permute-start(bf16[8,8192]{1,0:T(8,128)(2,1)S(1)} %add_convert_fusion.4), channel_id=1, source_target_pairs={{0,12},{4,8},{8,4},{12,0},{1,13},{5,9},{9,5},{13,1},{2,14},{6,10},... | collective-permute-start | bytes 393224 | tf_op jit(solution)/shard_map/ppermute | solution.py:26
  39.6 7.4 %collective-permute-start.25 = (bf16[8,8192]{1,0:T(8,128)(2,1)S(1)}, bf16[8,8192]{1,0:T(8,128)(2,1)S(1)}, u32[]{:S(2)}, u32[]{:S(2)}) collective-permute-start(bf16[8,8192]{1,0:T(8,128)(2,1)S(1)} %add_convert_fusion.1), channel_id=1, source_target_pairs={{0,4},{4,0},{8,12},{12,8},{1,5},{5,1},{9,13},{13,9},{2,6},{6,2},{1... | collective-permute-start | bytes 393224 | tf_op jit(solution)/shard_map/ppermute | solution.py:26

commit v7 on v6

--- a/solution.py
+++ b/solution.py
@@ -47,7 +47,7 @@
     for i, (src, dst) in enumerate(((home_hbm, home_ref), (adapter_hbm, adapter_ref), (tokens_hbm, tokens_ref))):
         tables.append(pltpu.make_async_copy(src, dst, table_sems.at[i]))
     own = pltpu.make_async_copy(x_hbm, x_ref, sems.at[2 * NAMED])
-    for copy in (*tables, own):
+    for copy in tables:
         copy.start()
     for copy in tables:
         copy.wait()
@@ -64,13 +64,13 @@
             last = jnp.where(here, jnp.maximum(last, slot), last)
         return first, last
 
-    first, last = lax.fori_loop(0, devices, extremes, (jnp.int32(store - 1), jnp.int32(0)))
+    first, last = lax.fori_loop(0, devices, extremes, (jnp.int32(store - 1), jnp.int32(0)), unroll=4)
     copies = []
     for i, slot in enumerate((first, last)):
         rows = pl.ds(i * rank, rank)
         copies.append(pltpu.make_async_copy(a_hbm.at[slot], a_ref.at[rows], sems.at[2 * i]))
         copies.append(pltpu.make_async_copy(b_hbm.at[slot], b_ref.at[rows], sems.at[2 * i + 1]))
-    for copy in copies:
+    for copy in (*copies, own):
         copy.start()
 
     def rows_of(owner, carry):

time: 47.8 us -> 47.7 us (level)
    ppermute x18, waiting for transfers between devices: 5.79 us -> 5.24 us  [other(): return lax.ppermute(x, axis, SWAP)]
where the time goes in v7:
time: 47.7 us; the launch traced here: 47.5 us
  starting transfers between devices  26.3 us (55%)
  waiting for transfers between devices  13.6 us (29%)
  Pallas kernels  6.51 us (14%)
  other arithmetic  1.01 us (2%)
    ppermute x7, starting transfers between devices, across(): lax.ppermute(x, 'z', [(i, i ^ away) for i in range(lax.axis_size('z'))])  13.8 us
    ppermute x18, starting transfers between devices, other(): return lax.ppermute(x, axis, SWAP)  9.97 us
    ppermute x7, waiting for transfers between devices, across(): lax.ppermute(x, 'z', [(i, i ^ away) for i in range(lax.axis_size('z'))])  8.33 us
    ppermute x18, waiting for transfers between devices, other(): return lax.ppermute(x, axis, SWAP)  5.24 us
    pallas_call x1, Pallas kernels, prepare(): pl.pallas_call(functools.partial(prepare_kernel, tok_rows=tok_rows), out_...  3.84 us
    pallas_call x1, Pallas kernels, partial_rows(): pl.pallas_call(functools.partial(partial_kernel, parts=parts, rank=rank),...  2.67 us
    ppermute x1, starting transfers between devices, diagonal(): lax.ppermute(x, ('z', 'y'), [(2 * i + j, 2 * (i ^ away) + 1 - j) for i, j...  2.53 us
  transfers between devices with their start and end apart: 26, of which 9 were waited for; matrix products, arithmetic and copies ran while one was open for 1% of the time, Pallas kernels for 8%

profile of v7, /device:TPU:0, one launch (start us, length us, event | category | flops | bytes accessed | tf_op | source)
XLA Modules:
  0.0 47.5 jit_solution(10800368859268269338)
XLA Ops:
  0.0 4.0 %collective-permute-start = (bf16[8,8192]{1,0:T(8,128)(2,1)}, bf16[8,8192]{1,0:T(8,128)(2,1)S(1)}, u32[]{:S(2)}, u32[]{:S(2)}) collective-permute-start(bf16[8,8192]{1,0:T(8,128)(2,1)} %x_hbm.1), channel_id=1, source_target_pairs={{0,8},{4,12},{8,0},{12,4},{1,9},{5,13},{9,1},{13,5},{2,10},{6,14},... | collective-permute-start | bytes 393224 | tf_op jit(solution)/shard_map/ppermute | solution.py:26
  4.0 2.5 %collective-permute-start.9 = (bf16[8,8192]{1,0:T(8,128)(2,1)}, bf16[8,8192]{1,0:T(8,128)(2,1)S(1)}, u32[]{:S(2)}, u32[]{:S(2)}) collective-permute-start(bf16[8,8192]{1,0:T(8,128)(2,1)} %x_hbm.1), channel_id=1, source_target_pairs={{0,6},{2,4},{4,2},{6,0},{8,14},{10,12},{12,10},{14,8},{1,7},{3,5},... | collective-permute-start | bytes 393224 | tf_op jit(solution)/shard_map/ppermute | solution.py:31
  6.6 0.4 collective-permute-start.8
  7.0 0.5 %collective-permute-start.12 = (bf16[8,8192]{1,0:T(8,128)(2,1)}, bf16[8,8192]{1,0:T(8,128)(2,1)S(1)}, u32[]{:S(2)}, u32[]{:S(2)}) collective-permute-start(bf16[8,8192]{1,0:T(8,128)(2,1)} %x_hbm.1), channel_id=1, source_target_pairs={{0,2},{2,0},{1,3},{3,1},{4,6},{6,4},{5,7},{7,5},{8,10},{10,8},{9,1... | collective-permute-start | bytes 393224 | tf_op jit(solution)/shard_map/ppermute | solution.py:22
  7.5 3.8 %prepare.1 = (s32[128,1]{1,0:T(8,128)S(1)}, bf16[128,8192]{1,0:T(8,128)(2,1)S(1)}, bf16[128,8192]{1,0:T(8,128)(2,1)S(1)}, bf16[8,8192]{1,0:T(8,128)(2,1)S(1)}) custom-call(s32[64]{0:T(128)} %home_hbm.1, s32[64]{0:T(128)} %adapter_hbm.1, s32[4,16]{1,0:T(4,128)} %bitcast.1, bf16[4,64,8192]{2,1,0:T(8,128)(2,1)} %a_hbm.1, bf16[4,64,8192]{2,1,0:T(8,128)(2,1)} %b_hbm.1, ...), custom_call_target="tpu_custom_call" | custom-call | bytes 4194304 | tf_op jit(solution)/shard_map/prepare/pallas_call | solution.py:98
  11.4 1.6 %collective-permute-start.2 = (bf16[8,8192]{1,0:T(8,128)(2,1)S(1)}, bf16[8,8192]{1,0:T(8,128)(2,1)S(1)}, u32[]{:S(2)}, u32[]{:S(2)}) collective-permute-start(bf16[8,8192]{1,0:T(8,128)(2,1)S(1)} %collective-permute-done.refs_4_), channel_id=1, source_target_pairs={{0,2},{2,0},{1,3},{3,1},{4,6},{6,4},{5,7},{7,5},{8,10},{10,8},{9,1... | collective-permute-start | bytes 393224 | tf_op jit(solution)/shard_map/ppermute | solution.py:22
  13.0 1.6 %collective-permute-start.1 = (bf16[8,8192]{1,0:T(8,128)(2,1)S(1)}, bf16[8,8192]{1,0:T(8,128)(2,1)S(1)}, u32[]{:S(2)}, u32[]{:S(2)}) collective-permute-start(bf16[8,8192]{1,0:T(8,128)(2,1)S(1)} %collective-permute-done.refs_4_), channel_id=1, source_target_pairs={{0,4},{4,0},{8,12},{12,8},{1,5},{5,1},{9,13},{13,9},{2,6},{6,2},{1... | collective-permute-start | bytes 393224 | tf_op jit(solution)/shard_map/ppermute | solution.py:26
  14.6 0.6 %collective-permute-done.8.refs_8_ = bf16[8,8192]{1,0:T(8,128)(2,1)S(1)} collective-permute-done((bf16[8,8192]{1,0:T(8,128)(2,1)}, bf16[8,8192]{1,0:T(8,128)(2,1)S(1)}, u32[]{:S(2)}, u32[]{:S(2)}) %collective-permute-start.8) | collective-permute-done | bytes 131104 | tf_op jit(solution)/shard_map/ppermute | solution.py:26
  15.2 0.5 %collective-permute-start.6 = (bf16[8,8192]{1,0:T(8,128)(2,1)S(1)}, bf16[8,8192]{1,0:T(8,128)(2,1)S(1)}, u32[]{:S(2)}, u32[]{:S(2)}) collective-permute-start(bf16[8,8192]{1,0:T(8,128)(2,1)S(1)} %collective-permute-done.refs_4_), channel_id=1, source_target_pairs={{0,1},{1,0},{2,3},{3,2},{4,5},{5,4},{6,7},{7,6},{8,9},{9,8},{10,11... | collective-permute-start | bytes 393224 | tf_op jit(solution)/shard_map/ppermute | solution.py:22
  15.7 0.8 %collective-permute-done.2.refs_5_ = bf16[8,8192]{1,0:T(8,128)(2,1)S(1)} collective-permute-done((bf16[8,8192]{1,0:T(8,128)(2,1)S(1)}, bf16[8,8192]{1,0:T(8,128)(2,1)S(1)}, u32[]{:S(2)}, u32[]{:S(2)}) %collective-permute-start.2) | collective-permute-done | bytes 131104 | tf_op jit(solution)/shard_map/ppermute | solution.py:22
  16.4 1.9 %collective-permute-start.3 = (bf16[8,8192]{1,0:T(8,128)(2,1)S(1)}, bf16[8,8192]{1,0:T(8,128)(2,1)S(1)}, u32[]{:S(2)}, u32[]{:S(2)}) collective-permute-start(bf16[8,8192]{1,0:T(8,128)(2,1)S(1)} %collective-permute-done.2.refs_5_), channel_id=1, source_target_pairs={{0,4},{4,0},{8,12},{12,8},{1,5},{5,1},{9,13},{13,9},{2,6},{6,2},{1... | collective-permute-start | bytes 393224 | tf_op jit(solution)/shard_map/ppermute | solution.py:26
  18.3 0.5 %collective-permute-start.11 = (bf16[8,8192]{1,0:T(8,128)(2,1)S(1)}, bf16[8,8192]{1,0:T(8,128)(2,1)S(1)}, u32[]{:S(2)}, u32[]{:S(2)}) collective-permute-start(bf16[8,8192]{1,0:T(8,128)(2,1)S(1)} %collective-permute-done.9.refs_9_), channel_id=1, source_target_pairs={{0,1},{1,0},{2,3},{3,2},{4,5},{5,4},{6,7},{7,6},{8,9},{9,8},{10,11... | collective-permute-start | bytes 393224 | tf_op jit(solution)/shard_map/ppermute | solution.py:22
  18.9 0.4 collective-permute-start.7
  19.3 2.1 %collective-permute-done.3.refs_1_ = bf16[8,8192]{1,0:T(8,128)(2,1)S(1)} collective-permute-done((bf16[8,8192]{1,0:T(8,128)(2,1)S(1)}, bf16[8,8192]{1,0:T(8,128)(2,1)S(1)}, u32[]{:S(2)}, u32[]{:S(2)}) %collective-permute-start.3) | collective-permute-done | bytes 131104 | tf_op jit(solution)/shard_map/ppermute | solution.py:26
  21.4 1.3 %collective-permute-done.5.refs_3_ = bf16[8,8192]{1,0:T(8,128)(2,1)S(1)} collective-permute-done((bf16[8,8192]{1,0:T(8,128)(2,1)S(1)}, bf16[8,8192]{1,0:T(8,128)(2,1)S(1)}, u32[]{:S(2)}, u32[]{:S(2)}) %collective-permute-start.5) | collective-permute-done | bytes 131104 | tf_op jit(solution)/shard_map/ppermute | solution.py:22
  22.7 2.7 %partial_rows.1 = (f32[16,8192]{1,0:T(8,128)S(1)}, bf16[16,8192]{1,0:T(8,128)(2,1)S(1)}, f32[16,8192]{1,0:T(8,128)S(1)}, bf16[16,8192]{1,0:T(8,128)(2,1)S(1)}, f...) custom-call(s32[128,1]{1,0:T(8,128)S(1)} %get-tuple-element.20.which, ...), custom_call_target="tpu_custom_call" | custom-call | flops 1610612736 | bytes 16777216 | tf_op jit(solution)/shard_map/partial_rows/pallas_call | solution.py:153
  25.4 0.2 collective-permute-start.16
  25.6 0.4 collective-permute-start.15
  26.0 0.2 collective-permute-start.19
  26.2 0.4 collective-permute-start.23
  26.5 0.5 %collective-permute-done.16 = bf16[16,8192]{1,0:T(8,128)(2,1)S(1)} collective-permute-done((bf16[16,8192]{1,0:T(8,128)(2,1)S(1)}, bf16[16,8192]{1,0:T(8,128)(2,1)S(1)}, u32[]{:S(2)}, u32[]{:S(2)}) %collective-permute-start.16) | collective-permute-done | bytes 262176 | tf_op jit(solution)/shard_map/ppermute | solution.py:22
  27.1 1.6 %collective-permute-start.17 = (bf16[8,8192]{1,0:T(8,128)(2,1)S(1)}, bf16[8,8192]{1,0:T(8,128)(2,1)S(1)}, u32[]{:S(2)}, u32[]{:S(2)}) collective-permute-start(bf16[8,8192]{1,0:T(8,128)(2,1)S(1)} %add_convert_fusion.6), channel_id=1, source_target_pairs={{0,2},{2,0},{1,3},{3,1},{4,6},{6,4},{5,7},{7,5},{8,10},{10,8},{9,1... | collective-permute-start | bytes 393224 | tf_op jit(solution)/shard_map/ppermute | solution.py:22
  28.7 0.7 %collective-permute-start.20 = (bf16[8,8192]{1,0:T(8,128)(2,1)S(1)}, bf16[8,8192]{1,0:T(8,128)(2,1)S(1)}, u32[]{:S(2)}, u32[]{:S(2)}) collective-permute-start(bf16[8,8192]{1,0:T(8,128)(2,1)S(1)} %add_convert_fusion.5), channel_id=1, source_target_pairs={{0,2},{2,0},{1,3},{3,1},{4,6},{6,4},{5,7},{7,5},{8,10},{10,8},{9,1... | collective-permute-start | bytes 393224 | tf_op jit(solution)/shard_map/ppermute | solution.py:22
  29.4 1.4 %collective-permute-start.24 = (bf16[8,8192]{1,0:T(8,128)(2,1)S(1)}, bf16[8,8192]{1,0:T(8,128)(2,1)S(1)}, u32[]{:S(2)}, u32[]{:S(2)}) collective-permute-start(bf16[8,8192]{1,0:T(8,128)(2,1)S(1)} %add_convert_fusion.2), channel_id=1, source_target_pairs={{0,2},{2,0},{1,3},{3,1},{4,6},{6,4},{5,7},{7,5},{8,10},{10,8},{9,1... | collective-permute-start | bytes 393224 | tf_op jit(solution)/shard_map/ppermute | solution.py:22
  30.9 2.6 %collective-permute-done.17 = bf16[8,8192]{1,0:T(8,128)(2,1)S(1)} collective-permute-done((bf16[8,8192]{1,0:T(8,128)(2,1)S(1)}, bf16[8,8192]{1,0:T(8,128)(2,1)S(1)}, u32[]{:S(2)}, u32[]{:S(2)}) %collective-permute-start.17) | collective-permute-done | bytes 131104 | tf_op jit(solution)/shard_map/ppermute | solution.py:22
  33.5 1.5 %collective-permute-start.18 = (bf16[8,8192]{1,0:T(8,128)(2,1)S(1)}, bf16[8,8192]{1,0:T(8,128)(2,1)S(1)}, u32[]{:S(2)}, u32[]{:S(2)}) collective-permute-start(bf16[8,8192]{1,0:T(8,128)(2,1)S(1)} %add_convert_fusion.7), channel_id=1, source_target_pairs={{0,2},{2,0},{1,3},{3,1},{4,6},{6,4},{5,7},{7,5},{8,10},{10,8},{9,1... | collective-permute-start | bytes 393224 | tf_op jit(solution)/shard_map/ppermute | solution.py:22
  35.0 1.7 %collective-permute-start.22 = (bf16[8,8192]{1,0:T(8,128)(2,1)S(1)}, bf16[8,8192]{1,0:T(8,128)(2,1)S(1)}, u32[]{:S(2)}, u32[]{:S(2)}) collective-permute-start(bf16[8,8192]{1,0:T(8,128)(2,1)S(1)} %add_convert_fusion.3), channel_id=1, source_target_pairs={{0,8},{4,12},{8,0},{12,4},{1,9},{5,13},{9,1},{13,5},{2,10},{6,14},... | collective-permute-start | bytes 393224 | tf_op jit(solution)/shard_map/ppermute | solution.py:26
  36.8 2.7 %collective-permute-start.21 = (bf16[8,8192]{1,0:T(8,128)(2,1)S(1)}, bf16[8,8192]{1,0:T(8,128)(2,1)S(1)}, u32[]{:S(2)}, u32[]{:S(2)}) collective-permute-start(bf16[8,8192]{1,0:T(8,128)(2,1)S(1)} %add_convert_fusion.4), channel_id=1, source_target_pairs={{0,12},{4,8},{8,4},{12,0},{1,13},{5,9},{9,5},{13,1},{2,14},{6,10},... | collective-permute-start | bytes 393224 | tf_op jit(solution)/shard_map/ppermute | solution.py:26
  39.6 1.5 %collective-permute-start.25 = (bf16[8,8192]{1,0:T(8,128)(2,1)S(1)}, bf16[8,8192]{1,0:T(8,128)(2,1)S(1)}, u32[]{:S(2)}, u32[]{:S(2)}) collective-permute-start(bf16[8,8192]{1,0:T(8,128)(2,1)S(1)} %add_convert_fusion.1), channel_id=1, source_target_pairs={{0,4},{4,0},{8,12},{12,8},{1,5},{5,1},{9,13},{13,9},{2,6},{6,2},{1... | collective-permute-start | bytes 393224 | tf_op jit(solution)/shard_map/ppermute | solution.py:26
  41.1 5.3 %collective-permute-done.22 = bf16[8,8192]{1,0:T(8,128)(2,1)S(1)} collective-permute-done((bf16[8,8192]{1,0:T(8,128)(2,1)S(1)}, bf16[8,8192]{1,0:T(8,128)(2,1)S(1)}, u32[]{:S(2)}, u32[]{:S(2)}) %collective-permute-start.22) | collective-permute-done | bytes 131104 | tf_op jit(solution)/shard_map/ppermute | solution.py:26
  46.5 0.3 collective-permute-done.25
  46.8 0.7 %add_convert_fusion = bf16[8,8192]{1,0:T(8,128)(2,1)} fusion(bf16[8,8192]{1,0:T(8,128)(2,1)S(1)} %collective-permute-done.25, bf16[8,8192]{1,0:T(8,128)(2,1)S(1)} %collective-permute-done.22, bf16[8,8192]{1,0:T(8,128)(2,1)S(1)} %collective-permute-done.21, bf16[8,8192]{1,0:T(8,128)(2,1)S(1)} %collective-permute-done.18, f32[16,8192]{1,0:T(8,128)S(1)} %get-tuple-element.26, ...), kind=kLoop, calls=%fused_computation | loop fusion | flops 720896 | bytes 1048576 | tf_op jit(solution)/shard_map/convert_element_type | solution.py:205
  (34 shorter events, 0.5 us)
Async XLA Ops:
  0.0 11.4 %collective-permute-start = (bf16[8,8192]{1,0:T(8,128)(2,1)}, bf16[8,8192]{1,0:T(8,128)(2,1)S(1)}, u32[]{:S(2)}, u32[]{:S(2)}) collective-permute-start(bf16[8,8192]{1,0:T(8,128)(2,1)} %x_hbm.1), channel_id=1, source_target_pairs={{0,8},{4,12},{8,0},{12,4},{1,9},{5,13},{9,1},{13,5},{2,10},{6,14},... | collective-permute-start | bytes 393224 | tf_op jit(solution)/shard_map/ppermute | solution.py:26
  4.0 10.5 %collective-permute-start.9 = (bf16[8,8192]{1,0:T(8,128)(2,1)}, bf16[8,8192]{1,0:T(8,128)(2,1)S(1)}, u32[]{:S(2)}, u32[]{:S(2)}) collective-permute-start(bf16[8,8192]{1,0:T(8,128)(2,1)} %x_hbm.1), channel_id=1, source_target_pairs={{0,6},{2,4},{4,2},{6,0},{8,14},{10,12},{12,10},{14,8},{1,7},{3,5},... | collective-permute-start | bytes 393224 | tf_op jit(solution)/shard_map/ppermute | solution.py:31
  6.6 8.6 %collective-permute-start.8 = (bf16[8,8192]{1,0:T(8,128)(2,1)}, bf16[8,8192]{1,0:T(8,128)(2,1)S(1)}, u32[]{:S(2)}, u32[]{:S(2)}) collective-permute-start(bf16[8,8192]{1,0:T(8,128)(2,1)} %x_hbm.1), channel_id=1, source_target_pairs={{0,4},{4,0},{8,12},{12,8},{1,5},{5,1},{9,13},{13,9},{2,6},{6,2},{1... | collective-permute-start | bytes 393224 | tf_op jit(solution)/shard_map/ppermute | solution.py:26
  7.0 8.1 %collective-permute-start.12 = (bf16[8,8192]{1,0:T(8,128)(2,1)}, bf16[8,8192]{1,0:T(8,128)(2,1)S(1)}, u32[]{:S(2)}, u32[]{:S(2)}) collective-permute-start(bf16[8,8192]{1,0:T(8,128)(2,1)} %x_hbm.1), channel_id=1, source_target_pairs={{0,2},{2,0},{1,3},{3,1},{4,6},{6,4},{5,7},{7,5},{8,10},{10,8},{9,1... | collective-permute-start | bytes 393224 | tf_op jit(solution)/shard_map/ppermute | solution.py:22
  7.5 7.0 %copy-start.1 = (bf16[8,8192]{1,0:T(8,128)(2,1)S(1)}, bf16[8,8192]{1,0:T(8,128)(2,1)}, u32[]{:S(2)}) copy-start(bf16[8,8192]{1,0:T(8,128)(2,1)} %x_hbm.1) | copy-start | bytes 393220
  7.5 15.2 %copy-start = (bf16[512,8192]{1,0:T(8,128)(2,1)S(1)}, bf16[512,8192]{1,0:T(8,128)(2,1)}, u32[]{:S(2)}) copy-start(bf16[512,8192]{1,0:T(8,128)(2,1)} %w_ref.1) | copy-start | bytes 25165828
  11.4 5.0 %collective-permute-start.2 = (bf16[8,8192]{1,0:T(8,128)(2,1)S(1)}, bf16[8,8192]{1,0:T(8,128)(2,1)S(1)}, u32[]{:S(2)}, u32[]{:S(2)}) collective-permute-start(bf16[8,8192]{1,0:T(8,128)(2,1)S(1)} %collective-permute-done.refs_4_), channel_id=1, source_target_pairs={{0,2},{2,0},{1,3},{3,1},{4,6},{6,4},{5,7},{7,5},{8,10},{10,8},{9,1... | collective-permute-start | bytes 393224 | tf_op jit(solution)/shard_map/ppermute | solution.py:22
  13.0 5.3 %collective-permute-start.1 = (bf16[8,8192]{1,0:T(8,128)(2,1)S(1)}, bf16[8,8192]{1,0:T(8,128)(2,1)S(1)}, u32[]{:S(2)}, u32[]{:S(2)}) collective-permute-start(bf16[8,8192]{1,0:T(8,128)(2,1)S(1)} %collective-permute-done.refs_4_), channel_id=1, source_target_pairs={{0,4},{4,0},{8,12},{12,8},{1,5},{5,1},{9,13},{13,9},{2,6},{6,2},{1... | collective-permute-start | bytes 393224 | tf_op jit(solution)/shard_map/ppermute | solution.py:26
  14.6 3.7 %collective-permute-start.13 = (bf16[8,8192]{1,0:T(8,128)(2,1)S(1)}, bf16[8,8192]{1,0:T(8,128)(2,1)S(1)}, u32[]{:S(2)}, u32[]{:S(2)}) collective-permute-start(bf16[8,8192]{1,0:T(8,128)(2,1)S(1)} %copy-done.1), channel_id=1, source_target_pairs={{0,1},{1,0},{2,3},{3,2},{4,5},{5,4},{6,7},{7,6},{8,9},{9,8},{10,11... | collective-permute-start | bytes 393224 | tf_op jit(solution)/shard_map/ppermute | solution.py:22
  15.1 3.6 %collective-permute-start.10 = (bf16[8,8192]{1,0:T(8,128)(2,1)S(1)}, bf16[8,8192]{1,0:T(8,128)(2,1)S(1)}, u32[]{:S(2)}, u32[]{:S(2)}) collective-permute-start(bf16[8,8192]{1,0:T(8,128)(2,1)S(1)} %collective-permute-done.8.refs_8_), channel_id=1, source_target_pairs={{0,1},{1,0},{2,3},{3,2},{4,5},{5,4},{6,7},{7,6},{8,9},{9,8},{10,11... | collective-permute-start | bytes 393224 | tf_op jit(solution)/shard_map/ppermute | solution.py:22
  15.2 3.7 %collective-permute-start.6 = (bf16[8,8192]{1,0:T(8,128)(2,1)S(1)}, bf16[8,8192]{1,0:T(8,128)(2,1)S(1)}, u32[]{:S(2)}, u32[]{:S(2)}) collective-permute-start(bf16[8,8192]{1,0:T(8,128)(2,1)S(1)} %collective-permute-done.refs_4_), channel_id=1, source_target_pairs={{0,1},{1,0},{2,3},{3,2},{4,5},{5,4},{6,7},{7,6},{8,9},{9,8},{10,11... | collective-permute-start | bytes 393224 | tf_op jit(solution)/shard_map/ppermute | solution.py:22
  16.4 5.0 %collective-permute-start.3 = (bf16[8,8192]{1,0:T(8,128)(2,1)S(1)}, bf16[8,8192]{1,0:T(8,128)(2,1)S(1)}, u32[]{:S(2)}, u32[]{:S(2)}) collective-permute-start(bf16[8,8192]{1,0:T(8,128)(2,1)S(1)} %collective-permute-done.2.refs_5_), channel_id=1, source_target_pairs={{0,4},{4,0},{8,12},{12,8},{1,5},{5,1},{9,13},{13,9},{2,6},{6,2},{1... | collective-permute-start | bytes 393224 | tf_op jit(solution)/shard_map/ppermute | solution.py:26
  18.3 3.1 %collective-permute-start.14 = (bf16[8,8192]{1,0:T(8,128)(2,1)S(1)}, bf16[8,8192]{1,0:T(8,128)(2,1)S(1)}, u32[]{:S(2)}, u32[]{:S(2)}) collective-permute-start(bf16[8,8192]{1,0:T(8,128)(2,1)S(1)} %collective-permute-done.12.refs_13_), channel_id=1, source_target_pairs={{0,1},{1,0},{2,3},{3,2},{4,5},{5,4},{6,7},{7,6},{8,9},{9,8},{10,11... | collective-permute-start | bytes 393224 | tf_op jit(solution)/shard_map/ppermute | solution.py:22
  18.3 3.1 %collective-permute-start.11 = (bf16[8,8192]{1,0:T(8,128)(2,1)S(1)}, bf16[8,8192]{1,0:T(8,128)(2,1)S(1)}, u32[]{:S(2)}, u32[]{:S(2)}) collective-permute-start(bf16[8,8192]{1,0:T(8,128)(2,1)S(1)} %collective-permute-done.9.refs_9_), channel_id=1, source_target_pairs={{0,1},{1,0},{2,3},{3,2},{4,5},{5,4},{6,7},{7,6},{8,9},{9,8},{10,11... | collective-permute-start | bytes 393224 | tf_op jit(solution)/shard_map/ppermute | solution.py:22
  18.8 2.6 %collective-permute-start.4 = (bf16[8,8192]{1,0:T(8,128)(2,1)S(1)}, bf16[8,8192]{1,0:T(8,128)(2,1)S(1)}, u32[]{:S(2)}, u32[]{:S(2)}) collective-permute-start(bf16[8,8192]{1,0:T(8,128)(2,1)S(1)} %collective-permute-done.1.refs_0_), channel_id=1, source_target_pairs={{0,1},{1,0},{2,3},{3,2},{4,5},{5,4},{6,7},{7,6},{8,9},{9,8},{10,11... | collective-permute-start | bytes 393224 | tf_op jit(solution)/shard_map/ppermute | solution.py:22
  18.9 2.5 %collective-permute-start.7 = (bf16[8,8192]{1,0:T(8,128)(2,1)S(1)}, bf16[8,8192]{1,0:T(8,128)(2,1)S(1)}, u32[]{:S(2)}, u32[]{:S(2)}) collective-permute-start(bf16[8,8192]{1,0:T(8,128)(2,1)S(1)} %collective-permute-done.2.refs_5_), channel_id=1, source_target_pairs={{0,1},{1,0},{2,3},{3,2},{4,5},{5,4},{6,7},{7,6},{8,9},{9,8},{10,11... | collective-permute-start | bytes 393224 | tf_op jit(solution)/shard_map/ppermute | solution.py:22
  21.4 1.3 %collective-permute-start.5 = (bf16[8,8192]{1,0:T(8,128)(2,1)S(1)}, bf16[8,8192]{1,0:T(8,128)(2,1)S(1)}, u32[]{:S(2)}, u32[]{:S(2)}) collective-permute-start(bf16[8,8192]{1,0:T(8,128)(2,1)S(1)} %collective-permute-done.3.refs_1_), channel_id=1, source_target_pairs={{0,1},{1,0},{2,3},{3,2},{4,5},{5,4},{6,7},{7,6},{8,9},{9,8},{10,11... | collective-permute-start | bytes 393224 | tf_op jit(solution)/shard_map/ppermute | solution.py:22
  25.4 1.6 %collective-permute-start.16 = (bf16[16,8192]{1,0:T(8,128)(2,1)S(1)}, bf16[16,8192]{1,0:T(8,128)(2,1)S(1)}, u32[]{:S(2)}, u32[]{:S(2)}) collective-permute-start(bf16[16,8192]{1,0:T(8,128)(2,1)S(1)} %get-tuple-element.29), channel_id=1, source_target_pairs={{0,1},{1,0},{2,3},{3,2},{4,5},{5,4},{6,7},{7,6},{8,9},{9,8},{10,11... | collective-permute-start | bytes 786440 | tf_op jit(solution)/shard_map/ppermute | solution.py:22
  25.6 5.2 %collective-permute-start.15 = (bf16[16,8192]{1,0:T(8,128)(2,1)S(1)}, bf16[16,8192]{1,0:T(8,128)(2,1)S(1)}, u32[]{:S(2)}, u32[]{:S(2)}) collective-permute-start(bf16[16,8192]{1,0:T(8,128)(2,1)S(1)} %get-tuple-element.27), channel_id=1, source_target_pairs={{0,1},{1,0},{2,3},{3,2},{4,5},{5,4},{6,7},{7,6},{8,9},{9,8},{10,11... | collective-permute-start | bytes 786440 | tf_op jit(solution)/shard_map/ppermute | solution.py:22
  26.0 2.6 %collective-permute-start.19 = (bf16[16,8192]{1,0:T(8,128)(2,1)S(1)}, bf16[16,8192]{1,0:T(8,128)(2,1)S(1)}, u32[]{:S(2)}, u32[]{:S(2)}) collective-permute-start(bf16[16,8192]{1,0:T(8,128)(2,1)S(1)} %get-tuple-element.32), channel_id=1, source_target_pairs={{0,1},{1,0},{2,3},{3,2},{4,5},{5,4},{6,7},{7,6},{8,9},{9,8},{10,11... | collective-permute-start | bytes 786440 | tf_op jit(solution)/shard_map/ppermute | solution.py:22
  26.2 3.2 %collective-permute-start.23 = (bf16[16,8192]{1,0:T(8,128)(2,1)S(1)}, bf16[16,8192]{1,0:T(8,128)(2,1)S(1)}, u32[]{:S(2)}, u32[]{:S(2)}) collective-permute-start(bf16[16,8192]{1,0:T(8,128)(2,1)S(1)} %get-tuple-element.34), channel_id=1, source_target_pairs={{0,1},{1,0},{2,3},{3,2},{4,5},{5,4},{6,7},{7,6},{8,9},{9,8},{10,11... | collective-permute-start | bytes 786440 | tf_op jit(solution)/shard_map/ppermute | solution.py:22
  27.1 6.4 %collective-permute-start.17 = (bf16[8,8192]{1,0:T(8,128)(2,1)S(1)}, bf16[8,8192]{1,0:T(8,128)(2,1)S(1)}, u32[]{:S(2)}, u32[]{:S(2)}) collective-permute-start(bf16[8,8192]{1,0:T(8,128)(2,1)S(1)} %add_convert_fusion.6), channel_id=1, source_target_pairs={{0,2},{2,0},{1,3},{3,1},{4,6},{6,4},{5,7},{7,5},{8,10},{10,8},{9,1... | collective-permute-start | bytes 393224 | tf_op jit(solution)/shard_map/ppermute | solution.py:22
  28.7 8.1 %collective-permute-start.20 = (bf16[8,8192]{1,0:T(8,128)(2,1)S(1)}, bf16[8,8192]{1,0:T(8,128)(2,1)S(1)}, u32[]{:S(2)}, u32[]{:S(2)}) collective-permute-start(bf16[8,8192]{1,0:T(8,128)(2,1)S(1)} %add_convert_fusion.5), channel_id=1, source_target_pairs={{0,2},{2,0},{1,3},{3,1},{4,6},{6,4},{5,7},{7,5},{8,10},{10,8},{9,1... | collective-permute-start | bytes 393224 | tf_op jit(solution)/shard_map/ppermute | solution.py:22
  29.4 10.1 %collective-permute-start.24 = (bf16[8,8192]{1,0:T(8,128)(2,1)S(1)}, bf16[8,8192]{1,0:T(8,128)(2,1)S(1)}, u32[]{:S(2)}, u32[]{:S(2)}) collective-permute-start(bf16[8,8192]{1,0:T(8,128)(2,1)S(1)} %add_convert_fusion.2), channel_id=1, source_target_pairs={{0,2},{2,0},{1,3},{3,1},{4,6},{6,4},{5,7},{7,5},{8,10},{10,8},{9,1... | collective-permute-start | bytes 393224 | tf_op jit(solution)/shard_map/ppermute | solution.py:22
  33.5 7.6 %collective-permute-start.18 = (bf16[8,8192]{1,0:T(8,128)(2,1)S(1)}, bf16[8,8192]{1,0:T(8,128)(2,1)S(1)}, u32[]{:S(2)}, u32[]{:S(2)}) collective-permute-start(bf16[8,8192]{1,0:T(8,128)(2,1)S(1)} %add_convert_fusion.7), channel_id=1, source_target_pairs={{0,2},{2,0},{1,3},{3,1},{4,6},{6,4},{5,7},{7,5},{8,10},{10,8},{9,1... | collective-permute-start | bytes 393224 | tf_op jit(solution)/shard_map/ppermute | solution.py:22
  35.0 11.4 %collective-permute-start.22 = (bf16[8,8192]{1,0:T(8,128)(2,1)S(1)}, bf16[8,8192]{1,0:T(8,128)(2,1)S(1)}, u32[]{:S(2)}, u32[]{:S(2)}) collective-permute-start(bf16[8,8192]{1,0:T(8,128)(2,1)S(1)} %add_convert_fusion.3), channel_id=1, source_target_pairs={{0,8},{4,12},{8,0},{12,4},{1,9},{5,13},{9,1},{13,5},{2,10},{6,14},... | collective-permute-start | bytes 393224 | tf_op jit(solution)/shard_map/ppermute | solution.py:26
  36.8 9.6 %collective-permute-start.21 = (bf16[8,8192]{1,0:T(8,128)(2,1)S(1)}, bf16[8,8192]{1,0:T(8,128)(2,1)S(1)}, u32[]{:S(2)}, u32[]{:S(2)}) collective-permute-start(bf16[8,8192]{1,0:T(8,128)(2,1)S(1)} %add_convert_fusion.4), channel_id=1, source_target_pairs={{0,12},{4,8},{8,4},{12,0},{1,13},{5,9},{9,5},{13,1},{2,14},{6,10},... | collective-permute-start | bytes 393224 | tf_op jit(solution)/shard_map/ppermute | solution.py:26
  39.6 7.2 %collective-permute-start.25 = (bf16[8,8192]{1,0:T(8,128)(2,1)S(1)}, bf16[8,8192]{1,0:T(8,128)(2,1)S(1)}, u32[]{:S(2)}, u32[]{:S(2)}) collective-permute-start(bf16[8,8192]{1,0:T(8,128)(2,1)S(1)} %add_convert_fusion.1), channel_id=1, source_target_pairs={{0,4},{4,0},{8,12},{12,8},{1,5},{5,1},{9,13},{13,9},{2,6},{6,2},{1... | collective-permute-start | bytes 393224 | tf_op jit(solution)/shard_map/ppermute | solution.py:26
